TPU v7x, 32 devices: a whole 2x2x4 slice. The times are simulated.
32 devices in a mesh: fsdp: 4 (over x, core), grp: 2 (over y), rep: 4 (over z).
Axes of the slice: x: 2, y: 2, z: 4, core: 2. Of those that a mesh axis runs over, the one named last changes fastest.
Arguments:
- iterate: bfloat16 [4096, 7168], P(('fsdp', 'grp', 'rep')), may hold values from -0.040283203 to 0.040283203
Outputs:
- update: bfloat16 [4096, 7168], P('fsdp', ('grp', 'rep'))
All inputs are finite; a program needn't handle non-finite values.
Results may differ from a plain program's by a relative error of at most 0.0059.
Values may be sent and summed in bfloat16 or wider, within the bound.
No kernel may reach another device: no remote copies, remote signals or barrier semaphores. Data moves between devices by JAX's collectives and lax.ppermute only.
A program may use at most 64 MiB of HBM per device.

v0:
```python
import math

import jax
import jax.numpy as jnp
from jax import lax
from jax.sharding import PartitionSpec as P

COLS = 7168


coef_linear = 3.4445
coef_cubic = -4.775
coef_quintic = 2.0315


def body(iterate):
    holding = lax.all_to_all(iterate, ("grp", "rep"), split_axis=1, concat_axis=0, tiled=True)
    column_panel = lax.all_gather(holding, "fsdp", axis=0, tiled=True)
    partial_value = lax.dot_general(
        holding, column_panel, (((1,), (1,)), ((), ())), preferred_element_type=jnp.float32
    )
    gram_rows = lax.psum(partial_value, ("grp", "rep")).astype(jnp.bfloat16)
    first_image = jnp.dot(gram_rows, column_panel, preferred_element_type=jnp.float32).astype(
        jnp.bfloat16
    )
    second_image = jnp.dot(
        gram_rows,
        lax.all_gather(first_image, "fsdp", axis=0, tiled=True),
        preferred_element_type=jnp.float32,
    )
    factor = 0.2 * math.sqrt(COLS)
    combined = (
        coef_linear * holding.astype(jnp.float32)
        + coef_cubic * first_image.astype(jnp.float32)
        + coef_quintic * second_image
    )
    return (factor * combined).astype(jnp.bfloat16)


def solution(mesh):
    in_specs = (P(("fsdp", "grp", "rep"), None),)
    out_specs = P("fsdp", ("grp", "rep"))
    return jax.shard_map(body, mesh=mesh, in_specs=in_specs, out_specs=out_specs, check_vma=False)
```

profile of v0, /device:TPU:0, one launch (start us, length us, event | category | flops | bytes accessed | tf_op | source)
XLA Modules:
  0.0 861.8 jit_solution(5978549925738923643)
XLA Ops:
  6.5 0.0 all-gather.3.cloned.1.call-start
  6.5 1.7 copy.5
  8.3 50.7 %all_to_all.19 = bf16[128,8,896]{2,0,1:T(8,128)(2,1)} all-to-all(bf16[128,8,896]{2,0,1:T(8,128)(2,1)S(1)} %bitcast.16), channel_id=1, replica_groups=mesh['fsdp'=4,'grp'=2,'rep'=4] {'grp','rep'}, dimensions={1} | all-to-all | bytes 3670016 | tf_op jit(solution)/shard_map/all_to_all | solution.py:17
  59.0 0.0 all-gather.3.cloned.1.call-update
  59.1 0.0 all-gather.5.cloned.1.call-start
  59.1 49.7 %all-gather.3.cloned.1.call-done = bf16[4096,896]{1,0:T(8,128)(2,1)} async-done(((bf16[1024,896]{1,0:T(8,128)(2,1)}), bf16[4096,896]{1,0:T(8,128)(2,1)}) %all-gather.3.cloned.1.call-update) | async-done | bytes 7340048 | tf_op jit(solution)/shard_map/all_gather | solution.py:18
  108.8 14.9 %fusion.9 = f32[1024,4096]{1,0:T(8,128)} fusion(bf16[1024,896]{1,0:T(8,128)(2,1)} %bitcast.14, bf16[4096,896]{1,0:T(8,128)(2,1)} %all-gather.3.cloned.1.call-done), kind=kOutput, calls=%fused_computation.7 | convolution fusion | flops 7516192768 | bytes 25952256 | tf_op jit(solution)/shard_map/dot_general | solution.py:19
  123.7 652.6 %all-reduce.1 = bf16[1024,4096]{1,0:T(8,128)(2,1)} all-reduce(f32[1024,4096]{1,0:T(8,128)} %fusion.9), channel_id=1, replica_groups=mesh['fsdp'=4,'grp'=2,'rep'=4] {'grp','rep'}, use_global_device_ids=true, to_apply=%region_0.0 | all-reduce | flops 4194304 | bytes 25165824 | tf_op jit(solution)/shard_map/psum | solution.py:22
  776.3 0.0 copy-start
  776.3 14.4 %fusion.6 = bf16[1024,896]{1,0:T(8,128)(2,1)} fusion(bf16[4096,896]{1,0:T(8,128)(2,1)} %all-gather.3.cloned.1.call-done, bf16[1024,4096]{1,0:T(8,128)(2,1)} %all-reduce.1), kind=kOutput, calls=%fused_computation.6 | convolution fusion | flops 7517110272 | bytes 17563648 | tf_op jit(solution)/shard_map/dot_general | solution.py:23
  790.7 0.0 all-gather.5.cloned.1.call-update
  790.7 49.5 %all-gather.5.cloned.1.call-done = bf16[4096,896]{1,0:T(8,128)(2,1)} async-done(((bf16[1024,896]{1,0:T(8,128)(2,1)}), bf16[4096,896]{1,0:T(8,128)(2,1)}) %all-gather.5.cloned.1.call-update) | async-done | bytes 7340048 | tf_op jit(solution)/shard_map/all_gather | solution.py:28
  840.3 0.0 copy-done
  840.3 14.7 %multiply_convert_fusion = bf16[1024,896]{1,0:T(8,128)(2,1)} fusion(bf16[1024,896]{1,0:T(8,128)(2,1)} %fusion.6, bf16[1024,896]{1,0:T(8,128)(2,1)S(1)} %bitcast.15, bf16[4096,896]{1,0:T(8,128)(2,1)} %all-gather.5.cloned.1.call-done, bf16[1024,4096]{1,0:T(8,128)(2,1)} %all-reduce.1), kind=kOutput, calls=%fused_computation.4 | convolution fusion | flops 7524450304 | bytes 21233664 | tf_op jit(solution)/shard_map/dot_general | solution.py:26
Async XLA Ops:
  6.5 102.3 %all-gather.3.cloned.1.call-start = ((), (), s32[]{:S(2)}) async-start(), calls=%async_computation.1 | async-start | bytes 9175040 | tf_op jit(solution)/shard_map/all_gather | solution.py:18
  59.1 781.2 %all-gather.5.cloned.1.call-start = ((), (), s32[]{:S(2)}) async-start(), calls=%async_computation.2 | async-start | bytes 9175040 | tf_op jit(solution)/shard_map/all_gather | solution.py:28
  776.3 63.9 %copy-start = (bf16[128,8,896]{2,0,1:T(8,128)(2,1)S(1)}, bf16[128,8,896]{2,0,1:T(8,128)(2,1)}, u32[]{:S(2)}) copy-start(bf16[128,8,896]{2,0,1:T(8,128)(2,1)} %all_to_all.19) | copy-start | bytes 5505028
Sparse Core Ops, SparseCore 0:
  59.2 49.5 all-gather.2
  790.9 49.3 all-gather.4
where the time goes:
time: 862 us
  blocking collectives  703 us (82%)
  waiting for transfers between devices  99.2 us (12%)
  matrix products  44 us (5%)
  between operations  13.4 us (2%)
    psum x1, blocking collectives, body(): gram_rows = lax.psum(partial_value, ('grp', 'rep')).astype(jnp.bfloat16)  653 us
    all_to_all x1, blocking collectives, body(): lax.all_to_all(iterate, ('grp', 'rep'), split_axis=1, concat_axis=0, tile...  50.7 us
    all_gather x1, waiting for transfers between devices, body(): column_panel = lax.all_gather(holding, 'fsdp', axis=0, tiled=True)  49.7 us
    all_gather x1, waiting for transfers between devices, body(): lax.all_gather(first_image, 'fsdp', axis=0, tiled=True)  49.5 us
  transfers between devices with their start and end apart: 2, of which 2 were waited for; matrix products, arithmetic and copies ran while one was open for 0% of the time, Pallas kernels for 0%

commit v1 on v0

v1 whole, which is shorter than its diff:
```python
import math

import jax
import jax.numpy as jnp
from jax import lax
from jax.experimental import pallas as pl
from jax.experimental.layout import Layout, with_layout_constraint
from jax.experimental.pallas import tpu as pltpu
from jax.sharding import PartitionSpec as P

COLS = 7168


coef_linear = 3.4445
coef_cubic = -4.775
coef_quintic = 2.0315


def after(value, *earlier):
    return lax.optimization_barrier((value,) + earlier)[0]


def dot_rows(left, right):
    return lax.dot_general(
        left, right, (((1,), (1,)), ((), ())), preferred_element_type=jnp.float32
    ).astype(jnp.bfloat16)


DEPTH = 1024


def accumulate(left, right, total):
    part = jnp.dot(left[...], right[...], preferred_element_type=jnp.float32)

    @pl.when(pl.program_id(0) == 0)
    def _():
        total[...] = part

    @pl.when(pl.program_id(0) > 0)
    def _():
        total[...] += part


def first_kernel(left, right, out, total):
    accumulate(left, right, total)

    @pl.when(pl.program_id(0) == pl.num_programs(0) - 1)
    def _():
        out[...] = total[...].astype(out.dtype)


def product(left, right, rows, row_at):
    depth, width = right.shape
    step = math.gcd(DEPTH, depth)
    return pl.pallas_call(
        first_kernel,
        out_shape=jax.ShapeDtypeStruct((rows, width), jnp.bfloat16),
        grid=(depth // step,),
        in_specs=[
            pl.BlockSpec((rows, step), lambda at: (row_at, at)),
            pl.BlockSpec((step, width), lambda at: (at, 0)),
        ],
        out_specs=pl.BlockSpec((rows, width), lambda at: (0, 0)),
        scratch_shapes=[pltpu.VMEM((rows, width), jnp.float32)],
        compiler_params=pltpu.CompilerParams(vmem_limit_bytes=48 << 20),
        cost_estimate=pl.CostEstimate(
            flops=2 * rows * depth * width,
            bytes_accessed=2 * (rows * depth + depth * width + rows * width),
            transcendentals=0,
        ),
    )(left, right)


def second_begin_kernel(count):
    def kernel(columns, left, *refs):
        rights, (held, top, bottom, out) = refs[:count], refs[count:]
        factor = 0.2 * math.sqrt(COLS)

        @pl.when(pl.program_id(0) == 0)
        def _():
            half = top.shape[0]
            for at, image in ((0, top), (half, bottom)):
                rows = pl.ds(at, half)
                out[rows, :] = factor * (
                    coef_linear * held[rows, :].astype(jnp.float32)
                    + coef_cubic * image[...].astype(jnp.float32)
                )

        for at, right in enumerate(rights):

            @pl.when(pl.program_id(0) == at)
            def _(right=right):
                part = jnp.dot(left[...], right[...], preferred_element_type=jnp.float32)
                out[...] += (factor * coef_quintic) * part

    return kernel


def second_end_kernel(count):
    def kernel(columns, left, *refs):
        rights, (begun, out, total) = refs[:count], refs[count:]
        factor = 0.2 * math.sqrt(COLS)
        for at, right in enumerate(rights):

            @pl.when(pl.program_id(0) == at)
            def _(at=at, right=right):
                part = jnp.dot(left[...], right[...], preferred_element_type=jnp.float32)
                before = begun if at == 0 else total
                total[...] = before[...] + (factor * coef_quintic) * part

        @pl.when(pl.program_id(0) == count - 1)
        def _():
            out[...] = total[...].astype(out.dtype)

    return kernel


def add_terms(kernel, gram, columns, rights, others, kind, scratch=False):
    rows = gram.shape[0]
    depth, width = rights[0].shape

    def fixed(value):
        return pl.BlockSpec(
            value.shape, lambda at, columns: (0, 0), pipeline_mode=pl.Buffered(1)
        )

    return pl.pallas_call(
        kernel(len(rights)),
        out_shape=jax.ShapeDtypeStruct((rows, width), kind),
        grid_spec=pltpu.PrefetchScalarGridSpec(
            num_scalar_prefetch=1,
            grid=(len(rights),),
            in_specs=[pl.BlockSpec((rows, depth), lambda at, columns: (0, columns[at]))]
            + [fixed(value) for value in (*rights, *others)],
            out_specs=pl.BlockSpec((rows, width), lambda at, columns: (0, 0)),
            scratch_shapes=[pltpu.VMEM((rows, width), jnp.float32)] if scratch else [],
        ),
        compiler_params=pltpu.CompilerParams(vmem_limit_bytes=48 << 20),
        cost_estimate=pl.CostEstimate(
            flops=2 * rows * depth * width * len(rights),
            bytes_accessed=2 * len(rights) * depth * (rows + width) + 8 * rows * width,
            transcendentals=0,
        ),
    )(columns, gram, *rights, *others)


def begin_kernel(side, block, out):
    out[...] = block[...]


def begin_gram(block, side, columns, column_at):
    rows, width = block.shape
    return pl.pallas_call(
        begin_kernel,
        out_shape=jax.ShapeDtypeStruct((2 * rows, columns * width), block.dtype),
        grid_spec=pltpu.PrefetchScalarGridSpec(
            num_scalar_prefetch=1,
            grid=(1,),
            in_specs=[pl.BlockSpec((rows, width), lambda at, side: (0, 0))],
            out_specs=pl.BlockSpec((rows, width), lambda at, side: (side[0], column_at)),
        ),
        cost_estimate=pl.CostEstimate(
            flops=0, bytes_accessed=4 * rows * width, transcendentals=0
        ),
    )(side.reshape(1), block)


def by_rows(value):
    return with_layout_constraint(value, Layout(tuple(range(value.ndim))))


def make_body(n_row, n_grp, n_rep):
    n_chip = n_row // 2
    n_col = n_grp * n_rep
    over = ("grp", "rep")
    swap_cores = [(at, at ^ 1) for at in range(n_row)]

    def from_chip(value, step):
        pairs = [(at, (at - 2 * step) % n_row) for at in range(n_row)]
        return lax.ppermute(value, "fsdp", pairs)

    def on_chip(value):
        return lax.ppermute(value, "fsdp", swap_cores)

    def place(at):
        return (at % n_chip) * 2 + (at % n_row) // n_chip

    def ring(value, step):
        pairs = [(place(at), place(at + step)) for at in range(n_row)]
        return lax.ppermute(value, "fsdp", pairs)

    def begin_sum(value):
        assert n_grp & (n_grp - 1) == 0
        bit = 1
        while True:
            rows = value.shape[0] // 2
            side = (lax.axis_index("grp") // bit) % 2
            kept = lax.dynamic_slice_in_dim(value, side * rows, rows, 0)
            sent = lax.dynamic_slice_in_dim(value, (1 - side) * rows, rows, 0)
            got = lax.ppermute(sent, "grp", [(at, at ^ bit) for at in range(n_grp)])
            if 2 * bit == n_grp:
                return kept, sent, got
            value = (kept.astype(jnp.float32) + got.astype(jnp.float32)).astype(value.dtype)
            bit = 2 * bit

    rep_bits = [1 << at for at in range(n_rep.bit_length() - 1)][::-1]
    grp_bits = [1 << at for at in range(n_grp.bit_length() - 1)][::-1]
    over_rep = [("rep", n_rep, bit) for bit in rep_bits]
    over_grp = [("grp", n_grp, bit) for bit in grp_bits]

    def swap(value, axis, size, bit):
        return lax.ppermute(value, axis, [(at, at ^ bit) for at in range(size)])

    def join(value, got, axis, bit, known_grp, known_rep):
        side = (lax.axis_index(axis) // bit) % 2
        lower = jnp.where(side == 0, value, got)
        upper = jnp.where(side == 0, got, value)
        return jnp.stack([lower, upper], axis=0 if axis == "grp" else known_grp + known_rep)

    class Gather:
        def __init__(self, value, steps):
            self.value, self.steps = value, list(steps)
            self.known = {"grp": 0, "rep": 0}

        def send(self):
            return swap(self.value, *self.steps[0])

        def take(self, got):
            axis, _, bit = self.steps.pop(0)
            self.value = join(
                self.value, got, axis, bit, self.known["grp"], self.known["rep"]
            )
            self.known[axis] += 1

    def cut_sum(parts):
        added = [
            (kept.astype(jnp.float32) + got.astype(jnp.float32))
            .astype(kept.dtype)
            .reshape(n_rep, -1, kept.shape[1])
            for kept, got in parts
        ]
        return jnp.concatenate(added, axis=1)

    def to_rep(cut):
        return lax.all_to_all(cut, "rep", split_axis=0, concat_axis=0, tiled=True)

    def end_sum(pieces):
        return jnp.sum(pieces.astype(jnp.float32), axis=0).astype(pieces.dtype)

    def body(iterate):
        at_row = lax.axis_index("fsdp")
        chip, core = at_row // 2, at_row % 2
        held = lax.all_to_all(iterate, over, split_axis=1, concat_axis=0, tiled=True)
        rows, width = held.shape
        half = rows // 2
        cut_at = rows // n_col
        other = on_chip(held)
        far = [from_chip(held, step) for step in range(1, n_chip)]

        slots = [jnp.int32(0), jnp.int32(1)]
        for step in range(1, n_chip):
            near = chip + step < n_chip
            ahead_slot, behind_slot = 2 * step, 2 * (n_chip - step) + 1
            slots.append(jnp.where(near, ahead_slot, behind_slot))
            slots.append(jnp.where(near, behind_slot, ahead_slot))

        def in_order(found, start=0, whole=None):
            size, width = found[0].shape
            if whole is None:
                whole = jnp.zeros((n_row * rows, width), found[0].dtype)
            for at, block in enumerate(found):
                whole = lax.dynamic_update_slice(whole, block, (slots[at] * rows + start, 0))
            return whole

        kept_own, sent_own, got_own = begin_sum(dot_rows(held, held))
        quadrant_at = core * half
        upper = dot_rows(
            after(held[:half], sent_own), lax.dynamic_slice_in_dim(other, quadrant_at, half, 0)
        )
        right = dot_rows(lax.dynamic_slice_in_dim(held, quadrant_at, half, 0), other[half:])
        kept_pair, _, got_pair = begin_sum(jnp.concatenate([upper, right], axis=1))

        panel, started = [held, other], []
        for step in range(1, n_chip):
            far_own, got_own, got_pair = lax.optimization_barrier(
                (far[step - 1], got_own, got_pair)
            )
            far_other = on_chip(far_own)
            panel += [far_own, far_other]
            right = jnp.where(chip + step < n_chip, far_own, far_other)
            started.append(begin_sum(by_rows(dot_rows(held, right))))
        kept_own = after(kept_own, *[sent for _, sent, _ in started])
        near_pieces = to_rep(cut_sum([(kept_own, got_own), (kept_pair, got_pair)]))
        cut = cut_sum([(kept, got) for kept, _, got in started])
        near_pieces, cut = lax.optimization_barrier((near_pieces, cut))
        near = Gather(end_sum(near_pieces), over_grp)
        while len(near.steps) > 1:
            near.take(near.send())
        near_got = near.send()
        whole = in_order(panel)
        pieces, near_got, whole = lax.optimization_barrier((to_rep(cut), near_got, whole))
        ahead = Gather(end_sum(pieces), over_rep + over_grp[:-1])
        near.take(near_got)
        own = Gather(near.value[..., :cut_at, :], over_rep)
        pair = Gather(near.value[..., cut_at:, :], over_rep)
        own.known["grp"] = pair.known["grp"] = len(over_grp)

        ahead_got = ahead.send()
        ahead.take(ahead_got)
        pair.value = after(pair.value, ahead_got)
        pair_got = pair.send()
        while ahead.steps:
            ahead.take(ahead.send())

        side_here = lax.axis_index("grp") % 2
        here = side_here * half
        there = half - here
        steps = range(1, n_chip)
        own_half = [
            by_rows(ahead.value[..., (at - 1) * cut_at : at * cut_at, :].reshape(half, rows))
            for at in steps
        ]
        def put(block, row, column):
            return lax.dynamic_update_slice(gram_rows, block, (row, column))

        rung_here = [ring(block, at) for at, block in zip(steps, own_half)]
        pair.take(after(pair_got, *own_half))
        while len(pair.steps) > 1:
            pair.take(pair.send())
        own_got, pair_got = own.send(), pair.send()
        came, rung_there = [], []
        for side in range(2):
            columns = [block[:, side * half : (side + 1) * half] for block in own_half]
            if came:
                columns[0] = after(columns[0], *came[0])
            came.append([swap(block, *over_grp[-1]) for block in columns])
            rung_there.append([ring(block, at) for at, block in zip(steps, came[side])])

        gram_rows = begin_gram(own_half[0], side_here, n_row, 2)
        for at, block in zip(steps[1:], own_half[1:]):
            gram_rows = put(block, here, 2 * at * rows)

        def put_came(side):
            (*blocks, held_rows) = lax.optimization_barrier((*came[side], gram_rows))
            for at, block in zip(steps, blocks):
                held_rows = lax.dynamic_update_slice(
                    held_rows, block, (there, 2 * at * rows + side * half)
                )
            return held_rows

        def put_rung(blocks, row, offset):
            (*blocks, held_rows) = lax.optimization_barrier((*blocks, gram_rows))
            for at, block in zip(steps, blocks):
                held_rows = lax.dynamic_update_slice(
                    held_rows, block.T, (row, (2 * at + 1) * rows + offset)
                )
            return held_rows

        gram_rows = put_came(0)
        pair_got, gram_rows = lax.optimization_barrier((pair_got, gram_rows))
        pair.take(pair_got)
        pair_half = pair.value.reshape(half, rows)
        pair_other = on_chip(pair_half)
        gram_rows = put(pair_half[:, :half], 0, rows + quadrant_at)
        gram_rows = put(pair_half[:, half:], quadrant_at, rows + half)
        own_got, gram_rows = lax.optimization_barrier((own_got, gram_rows))
        own.take(own_got)
        while len(own.steps) > 1:
            own.take(own.send())
        own_got = own.send()
        gram_rows, _ = lax.optimization_barrier((gram_rows, own.value))
        gram_rows = put_rung(rung_here, 0, here)
        gram_rows = put_came(1)
        gram_rows = put_rung(rung_there[0], 0, there)
        pair_other, gram_rows = lax.optimization_barrier((pair_other, gram_rows))
        gram_rows = put(pair_other[:, :half].T, half - quadrant_at, rows)
        gram_rows = put(pair_other[:, half:].T, half, rows + half - quadrant_at)
        own_got, gram_rows = lax.optimization_barrier((own_got, gram_rows))
        own.take(own_got)
        gram_rows = put(own.value.reshape(rows, rows), 0, 0)
        images = [product(gram_rows, whole, half, 0)]
        gram_rows = after(gram_rows, images[0])
        gram_rows = put_rung(rung_there[1], half, there)
        images.append(product(gram_rows, whole, half, 1))

        def spread(image, *earlier):
            found = [image, on_chip(image)]
            for step in range(1, n_chip):
                got = from_chip(image, step)
                if earlier:
                    got = after(got, *earlier)
                found += [got, on_chip(got)]
            return found

        top = spread(images[0], images[1])
        if half % 128 == 0:
            other = on_chip(images[1])
            early = [*top, images[1], other]
            columns = [2 * slot for slot in slots] + [jnp.int32(1), jnp.int32(3)]
            begun = add_terms(
                second_begin_kernel,
                gram_rows,
                jnp.stack(columns),
                early,
                (held, *images),
                jnp.float32,
            )
            late = []
            for step in range(1, n_chip):
                got = after(from_chip(images[1], step), begun)
                late += [got, on_chip(got)]
            columns = jnp.stack([2 * slot + 1 for slot in slots[2:]])
            return add_terms(
                second_end_kernel, gram_rows, columns, late, (begun,), jnp.bfloat16, True
            )

        bottom = spread(images[1])
        spread_image = in_order(bottom, half, in_order(top))
        second_image = jnp.dot(gram_rows, spread_image, preferred_element_type=jnp.float32)
        image = jnp.concatenate(images, axis=0)
        factor = 0.2 * math.sqrt(COLS)
        combined = (
            coef_linear * held.astype(jnp.float32)
            + coef_cubic * image.astype(jnp.float32)
            + coef_quintic * second_image
        )
        return (factor * combined).astype(jnp.bfloat16)

    return body


def solution(mesh):
    sizes = mesh.shape
    in_specs = (P(("fsdp", "grp", "rep"), None),)
    out_specs = P("fsdp", ("grp", "rep"))
    body = make_body(sizes["fsdp"], sizes["grp"], sizes["rep"])
    return jax.shard_map(body, mesh=mesh, in_specs=in_specs, out_specs=out_specs, check_vma=False)
```

time: 862 us -> 340 us (0.39)
  blocking collectives: 703 us -> 50.6 us
  waiting for transfers between devices: 99.2 us -> 159 us
  local copies, waits for them, and re-layouts: 1.75 us -> 39.2 us
  Pallas kernels: 0 us -> 37.4 us
  matrix products: 44 us -> 10.1 us
  starting transfers between devices: 0.04 us -> 27.7 us
  other arithmetic: 0 us -> 14.3 us
  between operations: 13.4 us -> 0.38 us
    psum x1 -> x0, blocking collectives: 653 us -> none  [body(): gram_rows = lax.psum(partial_value, ('grp', 'rep')).astype(jnp.bfloat16)]
    ppermute x0 -> x25, waiting for transfers between devices: none -> 138 us  [the longest x9 52.7 us: swap(): return lax.ppermute(value, axis, [(at, at ^ bit) for at in range(size)])]
    all_gather x2 -> x0, waiting for transfers between devices: 99.2 us -> none  [the longest x1 49.7 us: body(): column_panel = lax.all_gather(holding, 'fsdp', axis=0, tiled=True)]
    pallas_call x0 -> x5, Pallas kernels: none -> 37.4 us  [the longest x2 18.9 us: add_terms(): pl.pallas_call(kernel(len(rights)), out_shape=jax.ShapeDtypeStruct((rows,...]
    dot_general x3 -> x4, matrix products: 44 us -> 10.1 us  [dot_rows(): lax.dot_general(left, right, (((1,), (1,)), ((), ())), preferred_element_...]
    dynamic_update_slice x0 -> x14, local copies, waits for them, and re-layouts: none -> 26.4 us  [the longest x4 12.2 us: in_order(): lax.dynamic_update_slice(whole, block, (slots[at] * rows + start, 0))]
    all_to_all x0 -> x2, waiting for transfers between devices: none -> 20.8 us  [to_rep(): return lax.all_to_all(cut, 'rep', split_axis=0, concat_axis=0, tiled=True)]
    ppermute x0 -> x25, starting transfers between devices: none -> 19.9 us  [the longest x9 8.77 us: swap(): return lax.ppermute(value, axis, [(at, at ^ bit) for at in range(size)])]
  transfers between devices with their start and end apart: 2 -> 27, of which waited for: 2 -> 19; matrix products, arithmetic and copies ran while one was open for 0% -> 15% of each run, Pallas kernels for 0% -> 9%
where the time goes in v1:
time: 340 us; the launch traced here: 338 us
  waiting for transfers between devices  159 us (47%)
  blocking collectives  50.6 us (15%)
  local copies, waits for them, and re-layouts  39.2 us (12%)
  Pallas kernels  37.4 us (11%)
  starting transfers between devices  27.7 us (8%)
  other arithmetic  14.3 us (4%)
  matrix products  10.1 us (3%)
    ppermute x9, waiting for transfers between devices, swap(): return lax.ppermute(value, axis, [(at, at ^ bit) for at in range(size)])  52.7 us
    all_to_all x1, blocking collectives, body(): lax.all_to_all(iterate, over, split_axis=1, concat_axis=0, tiled=True)  50.6 us
    ppermute x3, waiting for transfers between devices, begin_sum(): got = lax.ppermute(sent, 'grp', [(at, at ^ bit) for at in range(n_grp)])  44.8 us
    ppermute x3, waiting for transfers between devices, from_chip(): return lax.ppermute(value, 'fsdp', pairs)  31.3 us
    all_to_all x2, waiting for transfers between devices, to_rep(): return lax.all_to_all(cut, 'rep', split_axis=0, concat_axis=0, tiled=True)  20.8 us
    pallas_call x2, Pallas kernels, add_terms(): pl.pallas_call(kernel(len(rights)), out_shape=jax.ShapeDtypeStruct((rows,...  18.9 us
    pallas_call x2, Pallas kernels, product(): pl.pallas_call(first_kernel, out_shape=jax.ShapeDtypeStruct((rows, width)...  16.2 us
    dynamic_update_slice x4, local copies, waits for them, and re-layouts, in_order(): lax.dynamic_update_slice(whole, block, (slots[at] * rows + start, 0))  12.2 us
  transfers between devices with their start and end apart: 27, of which 19 were waited for; matrix products, arithmetic and copies ran while one was open for 15% of the time, Pallas kernels for 9%

profile of v1, /device:TPU:0, one launch (start us, length us, event | category | flops | bytes accessed | tf_op | source)
XLA Modules:
  0.0 338.4 jit_solution(5915082864178940150)
XLA Ops:
  1.8 50.6 %all_to_all.29 = bf16[128,8,896]{2,0,1:T(8,128)(2,1)S(1)} all-to-all(bf16[128,8,896]{2,0,1:T(8,128)(2,1)S(1)} %bitcast.83), channel_id=1, replica_groups=mesh['fsdp'=4,'grp'=2,'rep'=4] {'grp','rep'}, dimensions={1} | all-to-all | bytes 3670016 | tf_op jit(solution)/shard_map/all_to_all | solution.py:253
  54.0 2.4 convolution_convert_fusion
  62.6 20.0 %collective-permute-done.1 = bf16[512,1024]{1,0:T(8,128)(2,1)S(1)} collective-permute-done((bf16[512,1024]{1,0:T(8,128)(2,1)S(1)}, bf16[512,1024]{1,0:T(8,128)(2,1)S(1)}, u32[]{:S(2)}, u32[]{:S(2)}) %collective-permute-start.1) | collective-permute-done | bytes 1048608 | tf_op jit(solution)/shard_map/ppermute | solution.py:200
  82.6 12.3 %collective-permute-done = bf16[1024,896]{1,0:T(8,128)(2,1)} collective-permute-done((bf16[1024,896]{1,0:T(8,128)(2,1)S(1)}, bf16[1024,896]{1,0:T(8,128)(2,1)}, u32[]{:S(2)}, u32[]{:S(2)}) %collective-permute-start) | collective-permute-done | bytes 1835040 | tf_op jit(solution)/shard_map/ppermute | solution.py:180
  99.9 3.9 %convert_bitcast_fusion = bf16[1024,1024]{1,0:T(8,128)(2,1)S(1)} fusion(bf16[1024,896]{1,0:T(8,128)(2,1)S(1)} %bitcast.74, bf16[1024,896]{1,0:T(8,128)(2,1)} %collective-permute-done, bf16[1024,896]{1,0:T(8,128)(2,1)} %collective-permute-done.4, pred[]{:T(512)S(6)} %lt.83), kind=kOutput, calls=%fused_computation.3 | convolution fusion | flops 1881014272 | bytes 7602177 | tf_op jit(solution)/shard_map/dot_general | solution.py:24
  107.6 3.6 %all-to-all-start.1 = ((bf16[4,192,1024]{2,1,0:T(8,128)(2,1)}), bf16[4,192,1024]{2,1,0:T(8,128)(2,1)S(1)}, u32[]{:S(2)}, u32[]{:S(2)}) async-start(bf16[4,192,1024]{2,1,0:T(8,128)(2,1)} %pad_maximum_fusion.1), calls=%async_computation.1 | async-start | bytes 3145728 | tf_op jit(solution)/shard_map/all_to_all | solution.py:245
  111.8 24.8 %collective-permute-done.5 = bf16[512,1024]{1,0:T(8,128)(2,1)S(1)} collective-permute-done((bf16[512,1024]{1,0:T(8,128)(2,1)}, bf16[512,1024]{1,0:T(8,128)(2,1)S(1)}, u32[]{:S(2)}, u32[]{:S(2)}) %collective-permute-start.5) | collective-permute-done | bytes 1048608 | tf_op jit(solution)/shard_map/ppermute | solution.py:200
  136.6 2.6 add_convert_fusion
  139.2 9.4 %all-to-all-done.1 = bf16[4,192,1024]{2,1,0:T(8,128)(2,1)S(1)} async-done(((bf16[4,192,1024]{2,1,0:T(8,128)(2,1)}), bf16[4,192,1024]{2,1,0:T(8,128)(2,1)S(1)}, u32[]{:S(2)}, u32[]{:S(2)}) %all-to-all-start.1) | async-done | bytes 1572896 | tf_op jit(solution)/shard_map/all_to_all | solution.py:245
  148.7 4.2 %all-to-all-start.2 = ((bf16[4,128,1024]{2,1,0:T(8,128)(2,1)}), bf16[4,128,1024]{2,1,0:T(8,128)(2,1)}, u32[]{:S(2)}, u32[]{:S(2)}) async-start(bf16[4,128,1024]{2,1,0:T(8,128)(2,1)} %bitcast.85), calls=%async_computation.2 | async-start | bytes 2097152 | tf_op jit(solution)/shard_map/all_to_all | solution.py:245
  152.9 3.5 %dynamic_update_slice.42 = bf16[4096,896]{1,0:T(8,128)(2,1)} pad(bf16[1024,896]{1,0:T(8,128)(2,1)S(1)} %bitcast.75, bf16[]{:T(256)} %constant.132.clone.1), padding=0_3072x0_0 | pad | bytes 9175042 | tf_op jit(solution)/shard_map/dynamic_update_slice | solution.py:272
  157.4 2.9 constant_dynamic-update-slice_fusion.3
  160.2 2.9 constant_dynamic-update-slice_fusion.2
  163.2 2.9 constant_dynamic-update-slice_fusion.1.right
  167.1 11.3 %all-to-all-done.2 = bf16[4,128,1024]{2,1,0:T(8,128)(2,1)} async-done(((bf16[4,128,1024]{2,1,0:T(8,128)(2,1)}), bf16[4,128,1024]{2,1,0:T(8,128)(2,1)}, u32[]{:S(2)}, u32[]{:S(2)}) %all-to-all-start.2) | async-done | bytes 1048608 | tf_op jit(solution)/shard_map/all_to_all | solution.py:245
  180.0 11.9 %collective-permute-done.7 = bf16[128,1024]{1,0:T(8,128)(2,1)S(1)} collective-permute-done((bf16[128,1024]{1,0:T(8,128)(2,1)S(1)}, bf16[128,1024]{1,0:T(8,128)(2,1)S(1)}, u32[]{:S(2)}, u32[]{:S(2)}) %collective-permute-start.7) | collective-permute-done | bytes 262176 | tf_op jit(solution)/shard_map/ppermute | solution.py:212
  192.2 3.2 collective-permute-start.13
  195.4 16.1 %collective-permute-done.8 = bf16[2,128,1024]{2,1,0:T(8,128)(2,1)S(1)} collective-permute-done((bf16[2,128,1024]{2,1,0:T(8,128)(2,1)S(1)}, bf16[2,128,1024]{2,1,0:T(8,128)(2,1)S(1)}, u32[]{:S(2)}, u32[]{:S(2)}) %collective-permute-start.8) | collective-permute-done | bytes 524320 | tf_op jit(solution)/shard_map/ppermute | solution.py:212
  215.6 2.7 collective-permute-start.12
  222.1 4.5 %collective-permute-done.9 = bf16[512,512]{0,1:T(8,128)(2,1)} collective-permute-done((bf16[512,512]{0,1:T(8,128)(2,1)}, bf16[512,512]{0,1:T(8,128)(2,1)}, u32[]{:S(2)}, u32[]{:S(2)}) %collective-permute-start.9) | collective-permute-done | bytes 524320 | tf_op jit(solution)/shard_map/ppermute | solution.py:212
  228.8 8.5 %collective-permute-done.14 = bf16[2,2,64,1024]{3,2,1,0:T(8,128)(2,1)S(1)} collective-permute-done((bf16[2,2,64,1024]{3,2,1,0:T(8,128)(2,1)}, bf16[2,2,64,1024]{3,2,1,0:T(8,128)(2,1)S(1)}, u32[]{:S(2)}, u32[]{:S(2)}) %collective-permute-start.14) | collective-permute-done | bytes 524320 | tf_op jit(solution)/shard_map/ppermute | solution.py:212
  246.2 2.3 bitcast_dynamic-update-slice_fusion
  248.5 4.3 %collective-permute-done.10 = bf16[512,512]{0,1:T(8,128)(2,1)S(1)} collective-permute-done((bf16[512,512]{0,1:T(8,128)(2,1)S(1)}, bf16[512,512]{0,1:T(8,128)(2,1)S(1)}, u32[]{:S(2)}, u32[]{:S(2)}) %collective-permute-start.10) | collective-permute-done | bytes 524320 | tf_op jit(solution)/shard_map/ppermute | solution.py:212
  254.0 3.5 %collective-permute-done.17 = bf16[512,512]{0,1:T(8,128)(2,1)} collective-permute-done((bf16[512,512]{0,1:T(8,128)(2,1)}, bf16[512,512]{0,1:T(8,128)(2,1)}, u32[]{:S(2)}, u32[]{:S(2)}) %collective-permute-start.17) | collective-permute-done | bytes 524320 | tf_op jit(solution)/shard_map/ppermute | solution.py:190
  265.7 6.1 %collective-permute-done.15 = bf16[2,2,128,1024]{3,2,0,1:T(8,128)(2,1)} collective-permute-done((bf16[2,2,128,1024]{3,2,0,1:T(8,128)(2,1)}, bf16[2,2,128,1024]{3,2,0,1:T(8,128)(2,1)}, u32[]{:S(2)}, u32[]{:S(2)}) %collective-permute-start.15) | collective-permute-done | bytes 1048608 | tf_op jit(solution)/shard_map/ppermute | solution.py:212
  275.1 8.1 %shard_map.18.refs_0_.refs_7_ = bf16[512,896]{1,0:T(8,128)(2,1)S(1)} custom-call(bf16[1024,4096]{1,0:T(8,128)(2,1)} %constant_dynamic-update-slice_fusion.left, bf16[4096,896]{1,0:T(8,128)(2,1)} %constant_dynamic-update-slice_fusion.1.right), custom_call_target="tpu_custom_call" | custom-call | flops 3758096384 | bytes 12451840 | tf_op jit(solution)/shard_map/pallas_call | solution.py:55
  284.6 8.1 %shard_map.19.refs_4_.refs_8_ = bf16[512,896]{1,0:T(8,128)(2,1)S(1)} custom-call(bf16[1024,4096]{1,0:T(8,128)(2,1)} %bitcast_dynamic-update-slice_fusion.1.left, bf16[4096,896]{1,0:T(8,128)(2,1)} %constant_dynamic-update-slice_fusion.1.right), custom_call_target="tpu_custom_call" | custom-call | flops 3758096384 | bytes 12451840 | tf_op jit(solution)/shard_map/pallas_call | solution.py:55
  293.3 11.7 %collective-permute-done.21.refs_2_ = bf16[512,896]{1,0:T(8,128)(2,1)S(1)} collective-permute-done((bf16[512,896]{1,0:T(8,128)(2,1)S(1)}, bf16[512,896]{1,0:T(8,128)(2,1)S(1)}, u32[]{:S(2)}, u32[]{:S(2)}) %collective-permute-start.21) | collective-permute-done | bytes 917536 | tf_op jit(solution)/shard_map/ppermute | solution.py:180
  307.6 13.0 %shard_map.20.refs_2_ = f32[1024,896]{1,0:T(8,128)} custom-call(s32[6]{0:T(128)S(1)} %stack.107.columns, bf16[1024,4096]{1,0:T(8,128)(2,1)} %bitcast_dynamic-update-slice_fusion.1.left, bf16[512,896]{1,0:T(8,128)(2,1)S(1)} %shard_map.18.refs_0_.refs_7_, bf16[512,896]{1,0:T(8,128)(2,1)} %collective-permute-done.20.refs_1_, ...), custom_call_target="tpu_custom_call" | custom-call | flops 5637144576 | bytes 19136512 | tf_op jit(solution)/shard_map/pallas_call | solution.py:127
  320.6 7.2 %collective-permute-done.19.refs_0_ = bf16[512,896]{1,0:T(8,128)(2,1)} collective-permute-done((bf16[512,896]{1,0:T(8,128)(2,1)S(1)}, bf16[512,896]{1,0:T(8,128)(2,1)}, u32[]{:S(2)}, u32[]{:S(2)}) %collective-permute-start.19) | collective-permute-done | bytes 917536 | tf_op jit(solution)/shard_map/ppermute | solution.py:180
  327.9 2.6 collective-permute-done.24.refs_1_
  332.5 5.9 %shard_map.21 = bf16[1024,896]{1,0:T(8,128)(2,1)} custom-call(s32[2]{0:T(128)S(1)} %pad_add_fusion.columns, bf16[1024,4096]{1,0:T(8,128)(2,1)} %bitcast_dynamic-update-slice_fusion.1.left, bf16[512,896]{1,0:T(8,128)(2,1)} %collective-permute-done.19.refs_0_, bf16[512,896]{1,0:T(8,128)(2,1)S(1)} %collective-permute-done.24.refs_1_, f32[1024,896]{1,0:T(8,128)S(1)} %copy-done), custom_call_target="tpu_custom_call" | custom-call | flops 1879048192 | bytes 11272192 | tf_op jit(solution)/shard_map/pallas_call | solution.py:127
  (99 shorter events, 60.8 us)
Async XLA Ops:
  52.4 100.5 %copy-start.1 = (bf16[128,8,896]{2,0,1:T(8,128)(2,1)}, bf16[128,8,896]{2,0,1:T(8,128)(2,1)S(1)}, u32[]{:S(2)}) copy-start(bf16[128,8,896]{2,0,1:T(8,128)(2,1)S(1)} %all_to_all.29) | copy-start | bytes 5505028
  52.4 4.8 %collective-permute-start.2 = (bf16[1024,896]{1,0:T(8,128)(2,1)S(1)}, bf16[1024,896]{1,0:T(8,128)(2,1)}, u32[]{:S(2)}, u32[]{:S(2)}) collective-permute-start(bf16[1024,896]{1,0:T(8,128)(2,1)S(1)} %bitcast.69), channel_id=1, source_target_pairs={{0,8},{8,0},{16,24},{24,16},{1,9},{9,1},{17,25},{25,17},{2,10},{10... | collective-permute-start | bytes 5505032 | tf_op jit(solution)/shard_map/ppermute | solution.py:183
  52.4 42.5 %collective-permute-start = (bf16[1024,896]{1,0:T(8,128)(2,1)S(1)}, bf16[1024,896]{1,0:T(8,128)(2,1)}, u32[]{:S(2)}, u32[]{:S(2)}) collective-permute-start(bf16[1024,896]{1,0:T(8,128)(2,1)S(1)} %bitcast.70), channel_id=1, source_target_pairs={{0,16},{8,24},{16,0},{24,8},{1,17},{9,25},{17,1},{25,9},{2,18},{10... | collective-permute-start | bytes 5505032 | tf_op jit(solution)/shard_map/ppermute | solution.py:180
  56.5 26.1 %collective-permute-start.1 = (bf16[512,1024]{1,0:T(8,128)(2,1)S(1)}, bf16[512,1024]{1,0:T(8,128)(2,1)S(1)}, u32[]{:S(2)}, u32[]{:S(2)}) collective-permute-start(bf16[512,1024]{1,0:T(8,128)(2,1)S(1)} %get-tuple-element.78), channel_id=1, source_target_pairs={{0,4},{4,0},{1,5},{5,1},{2,6},{6,2},{3,7},{7,3},{8,12},{12,8},{9,1... | collective-permute-start | bytes 3145736 | tf_op jit(solution)/shard_map/ppermute | solution.py:200
  61.0 33.9 %copy-start.3 = (bf16[512,512]{0,1:T(8,128)(2,1)}, bf16[512,512]{0,1:T(8,128)(2,1)S(1)}, u32[]{:S(2)}) copy-start(bf16[512,512]{0,1:T(8,128)(2,1)S(1)} %convolution_convert_fusion.2) | copy-start | bytes 1572868
  61.1 33.9 %collective-permute-start.3 = (bf16[256,1024]{0,1:T(8,128)(2,1)S(1)}, bf16[256,1024]{0,1:T(8,128)(2,1)S(1)}, u32[]{:S(2)}, u32[]{:S(2)}) collective-permute-start(bf16[256,1024]{0,1:T(8,128)(2,1)S(1)} %fusion.7), channel_id=1, source_target_pairs={{0,4},{4,0},{1,5},{5,1},{2,6},{6,2},{3,7},{7,3},{8,12},{12,8},{9,1... | collective-permute-start | bytes 1572872 | tf_op jit(solution)/shard_map/ppermute | solution.py:200
  82.6 12.4 %copy-start.5 = (bf16[512,1024]{1,0:T(8,128)(2,1)}, bf16[512,1024]{1,0:T(8,128)(2,1)S(1)}, u32[]{:S(2)}) copy-start(bf16[512,1024]{1,0:T(8,128)(2,1)S(1)} %collective-permute-done.1) | copy-start | bytes 3145732
  95.8 4.1 %collective-permute-start.4 = (bf16[1024,896]{1,0:T(8,128)(2,1)}, bf16[1024,896]{1,0:T(8,128)(2,1)}, u32[]{:S(2)}, u32[]{:S(2)}) collective-permute-start(bf16[1024,896]{1,0:T(8,128)(2,1)} %collective-permute-done), channel_id=1, source_target_pairs={{0,8},{8,0},{16,24},{24,16},{1,9},{9,1},{17,25},{25,17},{2,10},{10... | collective-permute-start | bytes 5505032 | tf_op jit(solution)/shard_map/ppermute | solution.py:183
  103.8 2.4 copy-start.4
  107.6 41.1 %all-to-all-start.1 = ((bf16[4,192,1024]{2,1,0:T(8,128)(2,1)}), bf16[4,192,1024]{2,1,0:T(8,128)(2,1)S(1)}, u32[]{:S(2)}, u32[]{:S(2)}) async-start(bf16[4,192,1024]{2,1,0:T(8,128)(2,1)} %pad_maximum_fusion.1), calls=%async_computation.1 | async-start | bytes 3145728 | tf_op jit(solution)/shard_map/all_to_all | solution.py:245
  111.2 25.5 %collective-permute-start.5 = (bf16[512,1024]{1,0:T(8,128)(2,1)}, bf16[512,1024]{1,0:T(8,128)(2,1)S(1)}, u32[]{:S(2)}, u32[]{:S(2)}) collective-permute-start(bf16[512,1024]{1,0:T(8,128)(2,1)} %constant_dynamic-slice_fusion), channel_id=1, source_target_pairs={{0,4},{4,0},{1,5},{5,1},{2,6},{6,2},{3,7},{7,3},{8,12},{12,8},{9,1... | collective-permute-start | bytes 3145736 | tf_op jit(solution)/shard_map/ppermute | solution.py:200
  148.7 29.8 %all-to-all-start.2 = ((bf16[4,128,1024]{2,1,0:T(8,128)(2,1)}), bf16[4,128,1024]{2,1,0:T(8,128)(2,1)}, u32[]{:S(2)}, u32[]{:S(2)}) async-start(bf16[4,128,1024]{2,1,0:T(8,128)(2,1)} %bitcast.85), calls=%async_computation.2 | async-start | bytes 2097152 | tf_op jit(solution)/shard_map/all_to_all | solution.py:245
  156.7 10.4 %collective-permute-start.6 = (bf16[192,1024]{1,0:T(8,128)(2,1)S(1)}, bf16[192,1024]{1,0:T(8,128)(2,1)S(1)}, u32[]{:S(2)}, u32[]{:S(2)}) collective-permute-start(bf16[192,1024]{1,0:T(8,128)(2,1)S(1)} %reduce_sum.24), channel_id=1, source_target_pairs={{0,4},{4,0},{1,5},{5,1},{2,6},{6,2},{3,7},{7,3},{8,12},{12,8},{9,1... | collective-permute-start | bytes 1179656 | tf_op jit(solution)/shard_map/ppermute | solution.py:212
  179.9 12.0 %collective-permute-start.7 = (bf16[128,1024]{1,0:T(8,128)(2,1)S(1)}, bf16[128,1024]{1,0:T(8,128)(2,1)S(1)}, u32[]{:S(2)}, u32[]{:S(2)}) collective-permute-start(bf16[128,1024]{1,0:T(8,128)(2,1)S(1)} %reduce_sum.25), channel_id=1, source_target_pairs={{0,2},{1,3},{2,0},{3,1},{4,6},{5,7},{6,4},{7,5},{8,10},{9,11},{10,... | collective-permute-start | bytes 786440 | tf_op jit(solution)/shard_map/ppermute | solution.py:212
  192.0 19.5 %collective-permute-start.8 = (bf16[2,128,1024]{2,1,0:T(8,128)(2,1)S(1)}, bf16[2,128,1024]{2,1,0:T(8,128)(2,1)S(1)}, u32[]{:S(2)}, u32[]{:S(2)}) collective-permute-start(bf16[2,128,1024]{2,1,0:T(8,128)(2,1)S(1)} %pad_maximum_fusion.5), channel_id=1, source_target_pairs={{0,1},{1,0},{2,3},{3,2},{4,5},{5,4},{6,7},{7,6},{8,9},{9,8},{10,11... | collective-permute-start | bytes 1572872 | tf_op jit(solution)/shard_map/ppermute | solution.py:212
  192.2 21.6 %collective-permute-start.13 = (bf16[2,64,1024]{2,1,0:T(8,128)(2,1)S(1)}, bf16[2,64,1024]{2,1,0:T(8,128)(2,1)S(1)}, u32[]{:S(2)}, u32[]{:S(2)}) collective-permute-start(bf16[2,64,1024]{2,1,0:T(8,128)(2,1)S(1)} %pad_maximum_fusion.7), channel_id=1, source_target_pairs={{0,2},{1,3},{2,0},{3,1},{4,6},{5,7},{6,4},{7,5},{8,10},{9,11},{10,... | collective-permute-start | bytes 786440 | tf_op jit(solution)/shard_map/ppermute | solution.py:212
  213.3 13.3 %collective-permute-start.9 = (bf16[512,512]{0,1:T(8,128)(2,1)}, bf16[512,512]{0,1:T(8,128)(2,1)}, u32[]{:S(2)}, u32[]{:S(2)}) collective-permute-start(bf16[512,512]{0,1:T(8,128)(2,1)} %get-tuple-element.83), channel_id=1, source_target_pairs={{0,4},{4,0},{1,5},{5,1},{2,6},{6,2},{3,7},{7,3},{8,12},{12,8},{9,1... | collective-permute-start | bytes 1572872 | tf_op jit(solution)/shard_map/ppermute | solution.py:212
  214.7 22.6 %collective-permute-start.14 = (bf16[2,2,64,1024]{3,2,1,0:T(8,128)(2,1)}, bf16[2,2,64,1024]{3,2,1,0:T(8,128)(2,1)S(1)}, u32[]{:S(2)}, u32[]{:S(2)}) collective-permute-start(bf16[2,2,64,1024]{3,2,1,0:T(8,128)(2,1)} %pad_maximum_fusion.6), channel_id=1, source_target_pairs={{0,1},{1,0},{2,3},{3,2},{4,5},{5,4},{6,7},{7,6},{8,9},{9,8},{10,11... | collective-permute-start | bytes 1572872 | tf_op jit(solution)/shard_map/ppermute | solution.py:212
  215.6 25.2 %collective-permute-start.12 = (bf16[2,128,1024]{2,1,0:T(8,128)(2,1)}, bf16[2,128,1024]{2,1,0:T(8,128)(2,1)}, u32[]{:S(2)}, u32[]{:S(2)}) collective-permute-start(bf16[2,128,1024]{2,1,0:T(8,128)(2,1)} %fusion.5), channel_id=1, source_target_pairs={{0,2},{1,3},{2,0},{3,1},{4,6},{5,7},{6,4},{7,5},{8,10},{9,11},{10,... | collective-permute-start | bytes 1572872 | tf_op jit(solution)/shard_map/ppermute | solution.py:212
  218.3 27.9 %collective-permute-start.18 = (bf16[512,1024]{0,1:T(8,128)(2,1)S(1)}, bf16[512,1024]{0,1:T(8,128)(2,1)}, u32[]{:S(2)}, u32[]{:S(2)}) collective-permute-start(bf16[512,1024]{0,1:T(8,128)(2,1)S(1)} %copy.18), channel_id=1, source_target_pairs={{0,16},{16,8},{8,24},{24,0},{1,17},{17,9},{9,25},{25,1},{2,18},{18... | collective-permute-start | bytes 3145736 | tf_op jit(solution)/shard_map/ppermute | solution.py:190
  240.8 12.1 %collective-permute-start.10 = (bf16[512,512]{0,1:T(8,128)(2,1)S(1)}, bf16[512,512]{0,1:T(8,128)(2,1)S(1)}, u32[]{:S(2)}, u32[]{:S(2)}) collective-permute-start(bf16[512,512]{0,1:T(8,128)(2,1)S(1)} %copy-done.8), channel_id=1, source_target_pairs={{0,4},{4,0},{1,5},{5,1},{2,6},{6,2},{3,7},{7,3},{8,12},{12,8},{9,1... | collective-permute-start | bytes 1572872 | tf_op jit(solution)/shard_map/ppermute | solution.py:212
  242.3 19.5 %collective-permute-start.16 = (bf16[512,1024]{0,1:T(8,128)(2,1)}, bf16[512,1024]{0,1:T(8,128)(2,1)}, u32[]{:S(2)}, u32[]{:S(2)}) collective-permute-start(bf16[512,1024]{0,1:T(8,128)(2,1)} %copy.23), channel_id=1, source_target_pairs={{0,8},{8,0},{16,24},{24,16},{1,9},{9,1},{17,25},{25,17},{2,10},{10... | collective-permute-start | bytes 3145736 | tf_op jit(solution)/shard_map/ppermute | solution.py:183
  243.4 14.1 %collective-permute-start.17 = (bf16[512,512]{0,1:T(8,128)(2,1)}, bf16[512,512]{0,1:T(8,128)(2,1)}, u32[]{:S(2)}, u32[]{:S(2)}) collective-permute-start(bf16[512,512]{0,1:T(8,128)(2,1)} %collective-permute-done.9), channel_id=1, source_target_pairs={{0,16},{16,8},{8,24},{24,0},{1,17},{17,9},{9,25},{25,1},{2,18},{18... | collective-permute-start | bytes 1572872 | tf_op jit(solution)/shard_map/ppermute | solution.py:190
  246.2 25.6 %collective-permute-start.15 = (bf16[2,2,128,1024]{3,2,0,1:T(8,128)(2,1)}, bf16[2,2,128,1024]{3,2,0,1:T(8,128)(2,1)}, u32[]{:S(2)}, u32[]{:S(2)}) collective-permute-start(bf16[2,2,128,1024]{3,2,0,1:T(8,128)(2,1)} %pad_maximum_fusion.4), channel_id=1, source_target_pairs={{0,1},{1,0},{2,3},{3,2},{4,5},{5,4},{6,7},{7,6},{8,9},{9,8},{10,11... | collective-permute-start | bytes 3145736 | tf_op jit(solution)/shard_map/ppermute | solution.py:212
  257.5 26.2 %collective-permute-start.11 = (bf16[512,512]{0,1:T(8,128)(2,1)S(1)}, bf16[512,512]{0,1:T(8,128)(2,1)S(1)}, u32[]{:S(2)}, u32[]{:S(2)}) collective-permute-start(bf16[512,512]{0,1:T(8,128)(2,1)S(1)} %collective-permute-done.10), channel_id=1, source_target_pairs={{0,16},{16,8},{8,24},{24,0},{1,17},{17,9},{9,25},{25,1},{2,18},{18... | collective-permute-start | bytes 1572872 | tf_op jit(solution)/shard_map/ppermute | solution.py:190
  283.2 21.7 %collective-permute-start.21 = (bf16[512,896]{1,0:T(8,128)(2,1)S(1)}, bf16[512,896]{1,0:T(8,128)(2,1)S(1)}, u32[]{:S(2)}, u32[]{:S(2)}) collective-permute-start(bf16[512,896]{1,0:T(8,128)(2,1)S(1)} %shard_map.18.refs_0_.refs_7_), channel_id=1, source_target_pairs={{0,16},{8,24},{16,0},{24,8},{1,17},{9,25},{17,1},{25,9},{2,18},{10... | collective-permute-start | bytes 2752520 | tf_op jit(solution)/shard_map/ppermute | solution.py:180
  283.7 21.6 %collective-permute-start.20 = (bf16[512,896]{1,0:T(8,128)(2,1)S(1)}, bf16[512,896]{1,0:T(8,128)(2,1)}, u32[]{:S(2)}, u32[]{:S(2)}) collective-permute-start(bf16[512,896]{1,0:T(8,128)(2,1)S(1)} %shard_map.18.refs_0_.refs_7_), channel_id=1, source_target_pairs={{0,8},{8,0},{16,24},{24,16},{1,9},{9,1},{17,25},{25,17},{2,10},{10... | collective-permute-start | bytes 2752520 | tf_op jit(solution)/shard_map/ppermute | solution.py:183
  292.7 12.6 %collective-permute-start.23 = (bf16[512,896]{1,0:T(8,128)(2,1)S(1)}, bf16[512,896]{1,0:T(8,128)(2,1)}, u32[]{:S(2)}, u32[]{:S(2)}) collective-permute-start(bf16[512,896]{1,0:T(8,128)(2,1)S(1)} %shard_map.19.refs_4_.refs_8_), channel_id=1, source_target_pairs={{0,8},{8,0},{16,24},{24,16},{1,9},{9,1},{17,25},{25,17},{2,10},{10... | collective-permute-start | bytes 2752520 | tf_op jit(solution)/shard_map/ppermute | solution.py:183
  304.9 2.6 collective-permute-start.22
  305.0 22.9 %collective-permute-start.19 = (bf16[512,896]{1,0:T(8,128)(2,1)S(1)}, bf16[512,896]{1,0:T(8,128)(2,1)}, u32[]{:S(2)}, u32[]{:S(2)}) collective-permute-start(bf16[512,896]{1,0:T(8,128)(2,1)S(1)} %shard_map.19.refs_4_.refs_8_), channel_id=1, source_target_pairs={{0,16},{8,24},{16,0},{24,8},{1,17},{9,25},{17,1},{25,9},{2,18},{10... | collective-permute-start | bytes 2752520 | tf_op jit(solution)/shard_map/ppermute | solution.py:180
  327.8 2.7 collective-permute-start.24
  330.5 2.0 copy-start
  (4 other events, 6.3 us)

commit v2 on v1

--- a/solution.py
+++ b/solution.py
@@ -115,7 +115,7 @@
     return kernel
 
 
-def add_terms(kernel, gram, columns, rights, others, kind, scratch=False):
+def add_terms(kernel, gram, columns, rights, others, kind, scratch=False, limit=48 << 20):
     rows = gram.shape[0]
     depth, width = rights[0].shape
 
@@ -135,7 +135,7 @@
             out_specs=pl.BlockSpec((rows, width), lambda at, columns: (0, 0)),
             scratch_shapes=[pltpu.VMEM((rows, width), jnp.float32)] if scratch else [],
         ),
-        compiler_params=pltpu.CompilerParams(vmem_limit_bytes=48 << 20),
+        compiler_params=pltpu.CompilerParams(vmem_limit_bytes=limit),
         cost_estimate=pl.CostEstimate(
             flops=2 * rows * depth * width * len(rights),
             bytes_accessed=2 * len(rights) * depth * (rows + width) + 8 * rows * width,
@@ -289,21 +289,19 @@
             panel += [far_own, far_other]
             right = jnp.where(chip + step < n_chip, far_own, far_other)
             started.append(begin_sum(by_rows(dot_rows(held, right))))
-        kept_own = after(kept_own, *[sent for _, sent, _ in started])
         near_pieces = to_rep(cut_sum([(kept_own, got_own), (kept_pair, got_pair)]))
         cut = cut_sum([(kept, got) for kept, _, got in started])
         near_pieces, cut = lax.optimization_barrier((near_pieces, cut))
-        near = Gather(end_sum(near_pieces), over_grp)
-        while len(near.steps) > 1:
-            near.take(near.send())
-        near_got = near.send()
+        near_piece = end_sum(near_pieces)
+        own = Gather(near_piece[:cut_at], over_rep + over_grp[:-1])
+        pair = Gather(near_piece[cut_at:], over_grp + over_rep)
+        while len(pair.steps) > len(over_rep) + 1:
+            pair.take(pair.send())
+        pair_got = pair.send()
         whole = in_order(panel)
-        pieces, near_got, whole = lax.optimization_barrier((to_rep(cut), near_got, whole))
+        pieces, pair_got, whole = lax.optimization_barrier((to_rep(cut), pair_got, whole))
         ahead = Gather(end_sum(pieces), over_rep + over_grp[:-1])
-        near.take(near_got)
-        own = Gather(near.value[..., :cut_at, :], over_rep)
-        pair = Gather(near.value[..., cut_at:, :], over_rep)
-        own.known["grp"] = pair.known["grp"] = len(over_grp)
+        pair.take(pair_got)
 
         ahead_got = ahead.send()
         ahead.take(ahead_got)
@@ -327,6 +325,7 @@
         pair.take(after(pair_got, *own_half))
         while len(pair.steps) > 1:
             pair.take(pair.send())
+        own.value = after(own.value, *own_half)
         own_got, pair_got = own.send(), pair.send()
         came, rung_there = [], []
         for side in range(2):
@@ -369,15 +368,19 @@
             own.take(own.send())
         own_got = own.send()
         gram_rows, _ = lax.optimization_barrier((gram_rows, own.value))
+        gram_rows = put_came(1)
         gram_rows = put_rung(rung_here, 0, here)
-        gram_rows = put_came(1)
+        own_got, gram_rows = lax.optimization_barrier((own_got, gram_rows))
+        own.take(own_got)
+        own_rows = own.value.reshape(half, rows)
+        own_came = swap(own_rows, *over_grp[-1])
+        gram_rows = put(own_rows, here, 0)
         gram_rows = put_rung(rung_there[0], 0, there)
         pair_other, gram_rows = lax.optimization_barrier((pair_other, gram_rows))
         gram_rows = put(pair_other[:, :half].T, half - quadrant_at, rows)
         gram_rows = put(pair_other[:, half:].T, half, rows + half - quadrant_at)
-        own_got, gram_rows = lax.optimization_barrier((own_got, gram_rows))
-        own.take(own_got)
-        gram_rows = put(own.value.reshape(rows, rows), 0, 0)
+        own_came, gram_rows = lax.optimization_barrier((own_came, gram_rows))
+        gram_rows = put(own_came, there, 0)
         images = [product(gram_rows, whole, half, 0)]
         gram_rows = after(gram_rows, images[0])
         gram_rows = put_rung(rung_there[1], half, there)
@@ -411,7 +414,14 @@
                 late += [got, on_chip(got)]
             columns = jnp.stack([2 * slot + 1 for slot in slots[2:]])
             return add_terms(
-                second_end_kernel, gram_rows, columns, late, (begun,), jnp.bfloat16, True
+                second_end_kernel,
+                gram_rows,
+                columns,
+                late,
+                (begun,),
+                jnp.bfloat16,
+                scratch=True,
+                limit=58 << 20,
             )
 
         bottom = spread(images[1])

time: 340 us -> 331 us (0.974)
  waiting for transfers between devices: 159 us -> 151 us
  local copies, waits for them, and re-layouts: 39.2 us -> 34.6 us
  starting transfers between devices: 27.7 us -> 31.1 us
    ppermute x9 -> x10, waiting for transfers between devices: 52.7 us -> 58.1 us  [swap(): return lax.ppermute(value, axis, [(at, at ^ bit) for at in range(size)])]
    ppermute x3, waiting for transfers between devices: 31.3 us -> 26.9 us  [from_chip(): return lax.ppermute(value, 'fsdp', pairs)]
    ppermute x3, waiting for transfers between devices: 3.54 us -> 0.01 us  [ring(): return lax.ppermute(value, 'fsdp', pairs)]
    ppermute x9 -> x10, starting transfers between devices: 8.77 us -> 10.4 us  [swap(): return lax.ppermute(value, axis, [(at, at ^ bit) for at in range(size)])]
    dynamic_update_slice x5 -> x6, local copies, waits for them, and re-layouts: 7.22 us -> 5.75 us  [put(): return lax.dynamic_update_slice(gram_rows, block, (row, column))]
  transfers between devices with their start and end apart: 27 -> 28, of which waited for: 19 -> 17; matrix products, arithmetic and copies ran while one was open for 15% -> 16% of each run, Pallas kernels for 9% -> 10%
where the time goes in v2:
time: 331 us; the launch traced here: 329 us
  waiting for transfers between devices  151 us (46%)
  blocking collectives  50.6 us (15%)
  Pallas kernels  38.9 us (12%)
  local copies, waits for them, and re-layouts  34.6 us (10%)
  starting transfers between devices  31.1 us (9%)
  other arithmetic  12.7 us (4%)
  matrix products  10.1 us (3%)
    ppermute x10, waiting for transfers between devices, swap(): return lax.ppermute(value, axis, [(at, at ^ bit) for at in range(size)])  58.1 us
    all_to_all x1, blocking collectives, body(): lax.all_to_all(iterate, over, split_axis=1, concat_axis=0, tiled=True)  50.6 us
    ppermute x3, waiting for transfers between devices, begin_sum(): got = lax.ppermute(sent, 'grp', [(at, at ^ bit) for at in range(n_grp)])  45 us
    ppermute x3, waiting for transfers between devices, from_chip(): return lax.ppermute(value, 'fsdp', pairs)  26.9 us
    pallas_call x2, Pallas kernels, add_terms(): pl.pallas_call(kernel(len(rights)), out_shape=jax.ShapeDtypeStruct((rows,...  20.4 us
    all_to_all x2, waiting for transfers between devices, to_rep(): return lax.all_to_all(cut, 'rep', split_axis=0, concat_axis=0, tiled=True)  18 us
    pallas_call x2, Pallas kernels, product(): pl.pallas_call(first_kernel, out_shape=jax.ShapeDtypeStruct((rows, width)...  16.2 us
    dynamic_update_slice x4, local copies, waits for them, and re-layouts, in_order(): lax.dynamic_update_slice(whole, block, (slots[at] * rows + start, 0))  12.2 us
  transfers between devices with their start and end apart: 28, of which 17 were waited for; matrix products, arithmetic and copies ran while one was open for 16% of the time, Pallas kernels for 10%

profile of v2, /device:TPU:0, one launch (start us, length us, event | category | flops | bytes accessed | tf_op | source)
XLA Modules:
  0.0 329.5 jit_solution(15858880427141753803)
XLA Ops:
  1.8 50.6 %all_to_all.29 = bf16[128,8,896]{2,0,1:T(8,128)(2,1)S(1)} all-to-all(bf16[128,8,896]{2,0,1:T(8,128)(2,1)S(1)} %bitcast.80), channel_id=1, replica_groups=mesh['fsdp'=4,'grp'=2,'rep'=4] {'grp','rep'}, dimensions={1} | all-to-all | bytes 3670016 | tf_op jit(solution)/shard_map/all_to_all | solution.py:253
  54.0 2.4 convolution_convert_fusion
  62.5 20.0 %collective-permute-done.1 = bf16[512,1024]{1,0:T(8,128)(2,1)S(1)} collective-permute-done((bf16[512,1024]{1,0:T(8,128)(2,1)S(1)}, bf16[512,1024]{1,0:T(8,128)(2,1)S(1)}, u32[]{:S(2)}, u32[]{:S(2)}) %collective-permute-start.1) | collective-permute-done | bytes 1048608 | tf_op jit(solution)/shard_map/ppermute | solution.py:200
  82.5 12.4 %collective-permute-done = bf16[1024,896]{1,0:T(8,128)(2,1)} collective-permute-done((bf16[1024,896]{1,0:T(8,128)(2,1)S(1)}, bf16[1024,896]{1,0:T(8,128)(2,1)}, u32[]{:S(2)}, u32[]{:S(2)}) %collective-permute-start) | collective-permute-done | bytes 1835040 | tf_op jit(solution)/shard_map/ppermute | solution.py:180
  97.1 1.9 add_convert_fusion.1
  100.4 3.6 %all-to-all-start.1 = ((bf16[4,192,1024]{2,1,0:T(8,128)(2,1)}), bf16[4,192,1024]{2,1,0:T(8,128)(2,1)S(1)}, u32[]{:S(2)}, u32[]{:S(2)}) async-start(bf16[4,192,1024]{2,1,0:T(8,128)(2,1)} %pad_maximum_fusion), calls=%async_computation.1 | async-start | bytes 3145728 | tf_op jit(solution)/shard_map/all_to_all | solution.py:245
  104.0 3.9 %convert_bitcast_fusion = bf16[1024,1024]{1,0:T(8,128)(2,1)S(1)} fusion(bf16[1024,896]{1,0:T(8,128)(2,1)S(1)} %bitcast.72, bf16[1024,896]{1,0:T(8,128)(2,1)} %collective-permute-done, bf16[1024,896]{1,0:T(8,128)(2,1)} %collective-permute-done.4, pred[]{:T(512)S(6)} %lt.85), kind=kOutput, calls=%fused_computation.1 | convolution fusion | flops 1881014272 | bytes 7602177 | tf_op jit(solution)/shard_map/dot_general | solution.py:24
  108.6 25.0 %collective-permute-done.5 = bf16[512,1024]{1,0:T(8,128)(2,1)S(1)} collective-permute-done((bf16[512,1024]{1,0:T(8,128)(2,1)S(1)}, bf16[512,1024]{1,0:T(8,128)(2,1)S(1)}, u32[]{:S(2)}, u32[]{:S(2)}) %collective-permute-start.5) | collective-permute-done | bytes 1048608 | tf_op jit(solution)/shard_map/ppermute | solution.py:200
  135.0 6.9 %all-to-all-done.1 = bf16[4,192,1024]{2,1,0:T(8,128)(2,1)S(1)} async-done(((bf16[4,192,1024]{2,1,0:T(8,128)(2,1)}), bf16[4,192,1024]{2,1,0:T(8,128)(2,1)S(1)}, u32[]{:S(2)}, u32[]{:S(2)}) %all-to-all-start.1) | async-done | bytes 1572896 | tf_op jit(solution)/shard_map/all_to_all | solution.py:245
  141.8 4.3 %all-to-all-start.2 = ((bf16[4,128,1024]{2,1,0:T(8,128)(2,1)}), bf16[4,128,1024]{2,1,0:T(8,128)(2,1)}, u32[]{:S(2)}, u32[]{:S(2)}) async-start(bf16[4,128,1024]{2,1,0:T(8,128)(2,1)} %bitcast.84), calls=%async_computation.2 | async-start | bytes 2097152 | tf_op jit(solution)/shard_map/all_to_all | solution.py:245
  146.1 3.5 %dynamic_update_slice.45 = bf16[4096,896]{1,0:T(8,128)(2,1)} pad(bf16[1024,896]{1,0:T(8,128)(2,1)S(1)} %bitcast.73, bf16[]{:T(256)} %constant.132.clone.1), padding=0_3072x0_0 | pad | bytes 9175042 | tf_op jit(solution)/shard_map/dynamic_update_slice | solution.py:272
  149.6 2.9 constant_dynamic-update-slice_fusion.4
  152.5 2.9 constant_dynamic-update-slice_fusion.3
  156.4 2.9 constant_dynamic-update-slice_fusion.2.right
  160.9 11.1 %all-to-all-done.2 = bf16[4,128,1024]{2,1,0:T(8,128)(2,1)} async-done(((bf16[4,128,1024]{2,1,0:T(8,128)(2,1)}), bf16[4,128,1024]{2,1,0:T(8,128)(2,1)}, u32[]{:S(2)}, u32[]{:S(2)}) %all-to-all-start.2) | async-done | bytes 1048608 | tf_op jit(solution)/shard_map/all_to_all | solution.py:245
  173.6 12.3 %collective-permute-done.7 = bf16[128,1024]{1,0:T(8,128)(2,1)S(1)} collective-permute-done((bf16[128,1024]{1,0:T(8,128)(2,1)S(1)}, bf16[128,1024]{1,0:T(8,128)(2,1)S(1)}, u32[]{:S(2)}, u32[]{:S(2)}) %collective-permute-start.7) | collective-permute-done | bytes 262176 | tf_op jit(solution)/shard_map/ppermute | solution.py:212
  186.2 3.2 collective-permute-start.13
  189.4 16.2 %collective-permute-done.8 = bf16[2,128,1024]{2,1,0:T(8,128)(2,1)S(1)} collective-permute-done((bf16[2,128,1024]{2,1,0:T(8,128)(2,1)S(1)}, bf16[2,128,1024]{2,1,0:T(8,128)(2,1)S(1)}, u32[]{:S(2)}, u32[]{:S(2)}) %collective-permute-start.8) | collective-permute-done | bytes 524320 | tf_op jit(solution)/shard_map/ppermute | solution.py:212
  210.5 2.3 shard_map.17
  212.8 3.2 collective-permute-start.12
  216.0 4.8 %collective-permute-done.9 = bf16[512,512]{0,1:T(8,128)(2,1)} collective-permute-done((bf16[512,512]{0,1:T(8,128)(2,1)}, bf16[512,512]{0,1:T(8,128)(2,1)}, u32[]{:S(2)}, u32[]{:S(2)}) %collective-permute-start.9) | collective-permute-done | bytes 524320 | tf_op jit(solution)/shard_map/ppermute | solution.py:212
  222.9 4.6 %collective-permute-done.14 = bf16[2,2,64,1024]{3,2,1,0:T(8,128)(2,1)S(1)} collective-permute-done((bf16[2,2,64,1024]{3,2,1,0:T(8,128)(2,1)}, bf16[2,2,64,1024]{3,2,1,0:T(8,128)(2,1)S(1)}, u32[]{:S(2)}, u32[]{:S(2)}) %collective-permute-start.14) | collective-permute-done | bytes 524320 | tf_op jit(solution)/shard_map/ppermute | solution.py:212
  235.6 4.3 %collective-permute-done.10 = bf16[512,512]{0,1:T(8,128)(2,1)} collective-permute-done((bf16[512,512]{0,1:T(8,128)(2,1)}, bf16[512,512]{0,1:T(8,128)(2,1)}, u32[]{:S(2)}, u32[]{:S(2)}) %collective-permute-start.10) | collective-permute-done | bytes 524320 | tf_op jit(solution)/shard_map/ppermute | solution.py:212
  242.1 2.4 bitcast_dynamic-update-slice_fusion
  253.9 14.1 %collective-permute-done.17 = bf16[512,1024]{1,0:T(8,128)(2,1)S(1)} collective-permute-done((bf16[512,1024]{1,0:T(8,128)(2,1)S(1)}, bf16[512,1024]{1,0:T(8,128)(2,1)S(1)}, u32[]{:S(2)}, u32[]{:S(2)}) %collective-permute-start.17) | collective-permute-done | bytes 1048608 | tf_op jit(solution)/shard_map/ppermute | solution.py:212
  269.1 8.1 %shard_map.18.refs_0_.refs_7_ = bf16[512,896]{1,0:T(8,128)(2,1)S(1)} custom-call(bf16[1024,4096]{1,0:T(8,128)(2,1)} %constant_dynamic-update-slice_fusion.left, bf16[4096,896]{1,0:T(8,128)(2,1)} %constant_dynamic-update-slice_fusion.2.right), custom_call_target="tpu_custom_call" | custom-call | flops 3758096384 | bytes 12451840 | tf_op jit(solution)/shard_map/pallas_call | solution.py:55
  279.7 8.1 %shard_map.19.refs_4_.refs_8_ = bf16[512,896]{1,0:T(8,128)(2,1)S(1)} custom-call(bf16[1024,4096]{1,0:T(8,128)(2,1)} %bitcast_dynamic-update-slice_fusion.1.left, bf16[4096,896]{1,0:T(8,128)(2,1)} %constant_dynamic-update-slice_fusion.2.right), custom_call_target="tpu_custom_call" | custom-call | flops 3758096384 | bytes 12451840 | tf_op jit(solution)/shard_map/pallas_call | solution.py:55
  288.4 7.2 %collective-permute-done.22.refs_2_ = bf16[512,896]{1,0:T(8,128)(2,1)S(1)} collective-permute-done((bf16[512,896]{1,0:T(8,128)(2,1)S(1)}, bf16[512,896]{1,0:T(8,128)(2,1)S(1)}, u32[]{:S(2)}, u32[]{:S(2)}) %collective-permute-start.22) | collective-permute-done | bytes 917536 | tf_op jit(solution)/shard_map/ppermute | solution.py:180
  298.2 13.0 %shard_map.20.refs_2_ = f32[1024,896]{1,0:T(8,128)} custom-call(s32[6]{0:T(128)S(1)} %stack.107.columns, bf16[1024,4096]{1,0:T(8,128)(2,1)} %bitcast_dynamic-update-slice_fusion.1.left, bf16[512,896]{1,0:T(8,128)(2,1)S(1)} %shard_map.18.refs_0_.refs_7_, bf16[512,896]{1,0:T(8,128)(2,1)} %collective-permute-done.21.refs_1_, ...), custom_call_target="tpu_custom_call" | custom-call | flops 5637144576 | bytes 19136512 | tf_op jit(solution)/shard_map/pallas_call | solution.py:127
  311.2 7.2 %collective-permute-done.20.refs_0_ = bf16[512,896]{1,0:T(8,128)(2,1)} collective-permute-done((bf16[512,896]{1,0:T(8,128)(2,1)S(1)}, bf16[512,896]{1,0:T(8,128)(2,1)}, u32[]{:S(2)}, u32[]{:S(2)}) %collective-permute-start.20) | collective-permute-done | bytes 917536 | tf_op jit(solution)/shard_map/ppermute | solution.py:180
  319.1 2.0 collective-permute-done.25.refs_1_
  322.1 7.4 %shard_map.21 = bf16[1024,896]{1,0:T(8,128)(2,1)} custom-call(s32[2]{0:T(128)} %pad_add_fusion.columns, bf16[1024,4096]{1,0:T(8,128)(2,1)} %bitcast_dynamic-update-slice_fusion.1.left, bf16[512,896]{1,0:T(8,128)(2,1)} %collective-permute-done.20.refs_0_, bf16[512,896]{1,0:T(8,128)(2,1)} %copy-done.6, f32[1024,896]{1,0:T(8,128)} %shard_map.20.refs_2_), custom_call_target="tpu_custom_call" | custom-call | flops 1879048192 | bytes 11272192 | tf_op jit(solution)/shard_map/pallas_call | solution.py:127
  (102 shorter events, 54.5 us)
Async XLA Ops:
  52.4 93.7 %copy-start = (bf16[128,8,896]{2,0,1:T(8,128)(2,1)}, bf16[128,8,896]{2,0,1:T(8,128)(2,1)S(1)}, u32[]{:S(2)}) copy-start(bf16[128,8,896]{2,0,1:T(8,128)(2,1)S(1)} %all_to_all.29) | copy-start | bytes 5505028
  52.4 4.7 %collective-permute-start.2 = (bf16[1024,896]{1,0:T(8,128)(2,1)S(1)}, bf16[1024,896]{1,0:T(8,128)(2,1)}, u32[]{:S(2)}, u32[]{:S(2)}) collective-permute-start(bf16[1024,896]{1,0:T(8,128)(2,1)S(1)} %bitcast.67), channel_id=1, source_target_pairs={{0,8},{8,0},{16,24},{24,16},{1,9},{9,1},{17,25},{25,17},{2,10},{10... | collective-permute-start | bytes 5505032 | tf_op jit(solution)/shard_map/ppermute | solution.py:183
  52.4 42.5 %collective-permute-start = (bf16[1024,896]{1,0:T(8,128)(2,1)S(1)}, bf16[1024,896]{1,0:T(8,128)(2,1)}, u32[]{:S(2)}, u32[]{:S(2)}) collective-permute-start(bf16[1024,896]{1,0:T(8,128)(2,1)S(1)} %bitcast.68), channel_id=1, source_target_pairs={{0,16},{8,24},{16,0},{24,8},{1,17},{9,25},{17,1},{25,9},{2,18},{10... | collective-permute-start | bytes 5505032 | tf_op jit(solution)/shard_map/ppermute | solution.py:180
  56.3 4.6 %copy-start.4 = (bf16[1024,1024]{1,0:T(8,128)(2,1)}, bf16[1024,1024]{1,0:T(8,128)(2,1)S(1)}, u32[]{:S(2)}) copy-start(bf16[1024,1024]{1,0:T(8,128)(2,1)S(1)} %convolution_convert_fusion) | copy-start | bytes 6291460
  56.4 26.1 %collective-permute-start.1 = (bf16[512,1024]{1,0:T(8,128)(2,1)S(1)}, bf16[512,1024]{1,0:T(8,128)(2,1)S(1)}, u32[]{:S(2)}, u32[]{:S(2)}) collective-permute-start(bf16[512,1024]{1,0:T(8,128)(2,1)S(1)} %constant_dynamic-slice_fusion.1), channel_id=1, source_target_pairs={{0,4},{4,0},{1,5},{5,1},{2,6},{6,2},{3,7},{7,3},{8,12},{12,8},{9,1... | collective-permute-start | bytes 3145736 | tf_op jit(solution)/shard_map/ppermute | solution.py:200
  61.0 34.0 %collective-permute-start.3 = (bf16[256,1024]{0,1:T(8,128)(2,1)S(1)}, bf16[256,1024]{0,1:T(8,128)(2,1)S(1)}, u32[]{:S(2)}, u32[]{:S(2)}) collective-permute-start(bf16[256,1024]{0,1:T(8,128)(2,1)S(1)} %fusion.6), channel_id=1, source_target_pairs={{0,4},{4,0},{1,5},{5,1},{2,6},{6,2},{3,7},{7,3},{8,12},{12,8},{9,1... | collective-permute-start | bytes 1572872 | tf_op jit(solution)/shard_map/ppermute | solution.py:200
  82.5 12.4 %copy-start.5 = (bf16[512,1024]{1,0:T(8,128)(2,1)}, bf16[512,1024]{1,0:T(8,128)(2,1)S(1)}, u32[]{:S(2)}) copy-start(bf16[512,1024]{1,0:T(8,128)(2,1)S(1)} %collective-permute-done.1) | copy-start | bytes 3145732
  95.7 8.2 %collective-permute-start.4 = (bf16[1024,896]{1,0:T(8,128)(2,1)}, bf16[1024,896]{1,0:T(8,128)(2,1)}, u32[]{:S(2)}, u32[]{:S(2)}) collective-permute-start(bf16[1024,896]{1,0:T(8,128)(2,1)} %collective-permute-done), channel_id=1, source_target_pairs={{0,8},{8,0},{16,24},{24,16},{1,9},{9,1},{17,25},{25,17},{2,10},{10... | collective-permute-start | bytes 5505032 | tf_op jit(solution)/shard_map/ppermute | solution.py:183
  100.4 41.4 %all-to-all-start.1 = ((bf16[4,192,1024]{2,1,0:T(8,128)(2,1)}), bf16[4,192,1024]{2,1,0:T(8,128)(2,1)S(1)}, u32[]{:S(2)}, u32[]{:S(2)}) async-start(bf16[4,192,1024]{2,1,0:T(8,128)(2,1)} %pad_maximum_fusion), calls=%async_computation.1 | async-start | bytes 3145728 | tf_op jit(solution)/shard_map/all_to_all | solution.py:245
  107.9 25.6 %collective-permute-start.5 = (bf16[512,1024]{1,0:T(8,128)(2,1)S(1)}, bf16[512,1024]{1,0:T(8,128)(2,1)S(1)}, u32[]{:S(2)}, u32[]{:S(2)}) collective-permute-start(bf16[512,1024]{1,0:T(8,128)(2,1)S(1)} %constant_dynamic-slice_fusion), channel_id=1, source_target_pairs={{0,4},{4,0},{1,5},{5,1},{2,6},{6,2},{3,7},{7,3},{8,12},{12,8},{9,1... | collective-permute-start | bytes 3145736 | tf_op jit(solution)/shard_map/ppermute | solution.py:200
  141.8 30.2 %all-to-all-start.2 = ((bf16[4,128,1024]{2,1,0:T(8,128)(2,1)}), bf16[4,128,1024]{2,1,0:T(8,128)(2,1)}, u32[]{:S(2)}, u32[]{:S(2)}) async-start(bf16[4,128,1024]{2,1,0:T(8,128)(2,1)} %bitcast.84), calls=%async_computation.2 | async-start | bytes 2097152 | tf_op jit(solution)/shard_map/all_to_all | solution.py:245
  155.7 30.4 %copy-start.2 = (bf16[192,1024]{1,0:T(8,128)(2,1)}, bf16[192,1024]{1,0:T(8,128)(2,1)S(1)}, u32[]{:S(2)}) copy-start(bf16[192,1024]{1,0:T(8,128)(2,1)S(1)} %reduce_sum.24) | copy-start | bytes 1179652
  155.7 5.2 %collective-permute-start.6 = (bf16[64,1024]{1,0:T(8,128)(2,1)S(1)}, bf16[64,1024]{1,0:T(8,128)(2,1)S(1)}, u32[]{:S(2)}, u32[]{:S(2)}) collective-permute-start(bf16[64,1024]{1,0:T(8,128)(2,1)S(1)} %slice.46), channel_id=1, source_target_pairs={{0,4},{4,0},{1,5},{5,1},{2,6},{6,2},{3,7},{7,3},{8,12},{12,8},{9,1... | collective-permute-start | bytes 393224 | tf_op jit(solution)/shard_map/ppermute | solution.py:212
  173.5 12.4 %collective-permute-start.7 = (bf16[128,1024]{1,0:T(8,128)(2,1)S(1)}, bf16[128,1024]{1,0:T(8,128)(2,1)S(1)}, u32[]{:S(2)}, u32[]{:S(2)}) collective-permute-start(bf16[128,1024]{1,0:T(8,128)(2,1)S(1)} %reduce_sum.25), channel_id=1, source_target_pairs={{0,2},{1,3},{2,0},{3,1},{4,6},{5,7},{6,4},{7,5},{8,10},{9,11},{10,... | collective-permute-start | bytes 786440 | tf_op jit(solution)/shard_map/ppermute | solution.py:212
  186.0 19.5 %collective-permute-start.8 = (bf16[2,128,1024]{2,1,0:T(8,128)(2,1)S(1)}, bf16[2,128,1024]{2,1,0:T(8,128)(2,1)S(1)}, u32[]{:S(2)}, u32[]{:S(2)}) collective-permute-start(bf16[2,128,1024]{2,1,0:T(8,128)(2,1)S(1)} %pad_maximum_fusion.4), channel_id=1, source_target_pairs={{0,1},{1,0},{2,3},{3,2},{4,5},{5,4},{6,7},{7,6},{8,9},{9,8},{10,11... | collective-permute-start | bytes 1572872 | tf_op jit(solution)/shard_map/ppermute | solution.py:212
  186.2 21.8 %collective-permute-start.13 = (bf16[2,64,1024]{2,1,0:T(8,128)(2,1)S(1)}, bf16[2,64,1024]{2,1,0:T(8,128)(2,1)S(1)}, u32[]{:S(2)}, u32[]{:S(2)}) collective-permute-start(bf16[2,64,1024]{2,1,0:T(8,128)(2,1)S(1)} %pad_maximum_fusion.7), channel_id=1, source_target_pairs={{0,2},{1,3},{2,0},{3,1},{4,6},{5,7},{6,4},{7,5},{8,10},{9,11},{10,... | collective-permute-start | bytes 786440 | tf_op jit(solution)/shard_map/ppermute | solution.py:212
  207.4 13.3 %collective-permute-start.9 = (bf16[512,512]{0,1:T(8,128)(2,1)}, bf16[512,512]{0,1:T(8,128)(2,1)}, u32[]{:S(2)}, u32[]{:S(2)}) collective-permute-start(bf16[512,512]{0,1:T(8,128)(2,1)} %get-tuple-element.83), channel_id=1, source_target_pairs={{0,4},{4,0},{1,5},{5,1},{2,6},{6,2},{3,7},{7,3},{8,12},{12,8},{9,1... | collective-permute-start | bytes 1572872 | tf_op jit(solution)/shard_map/ppermute | solution.py:212
  208.9 18.5 %collective-permute-start.14 = (bf16[2,2,64,1024]{3,2,1,0:T(8,128)(2,1)}, bf16[2,2,64,1024]{3,2,1,0:T(8,128)(2,1)S(1)}, u32[]{:S(2)}, u32[]{:S(2)}) collective-permute-start(bf16[2,2,64,1024]{3,2,1,0:T(8,128)(2,1)} %pad_maximum_fusion.5), channel_id=1, source_target_pairs={{0,1},{1,0},{2,3},{3,2},{4,5},{5,4},{6,7},{7,6},{8,9},{9,8},{10,11... | collective-permute-start | bytes 1572872 | tf_op jit(solution)/shard_map/ppermute | solution.py:212
  209.0 33.1 %collective-permute-start.16 = (bf16[512,1024]{0,1:T(8,128)(2,1)S(1)}, bf16[512,1024]{0,1:T(8,128)(2,1)}, u32[]{:S(2)}, u32[]{:S(2)}) collective-permute-start(bf16[512,1024]{0,1:T(8,128)(2,1)S(1)} %copy.17), channel_id=1, source_target_pairs={{0,16},{16,8},{8,24},{24,0},{1,17},{17,9},{9,25},{25,1},{2,18},{18... | collective-permute-start | bytes 3145736 | tf_op jit(solution)/shard_map/ppermute | solution.py:190
  212.8 18.1 %collective-permute-start.12 = (bf16[128,1024]{1,0:T(8,128)(2,1)S(1)}, bf16[128,1024]{1,0:T(8,128)(2,1)}, u32[]{:S(2)}, u32[]{:S(2)}) collective-permute-start(bf16[128,1024]{1,0:T(8,128)(2,1)S(1)} %slice.49), channel_id=1, source_target_pairs={{0,2},{1,3},{2,0},{3,1},{4,6},{5,7},{6,4},{7,5},{8,10},{9,11},{10,... | collective-permute-start | bytes 786440 | tf_op jit(solution)/shard_map/ppermute | solution.py:212
  227.5 12.3 %collective-permute-start.10 = (bf16[512,512]{0,1:T(8,128)(2,1)}, bf16[512,512]{0,1:T(8,128)(2,1)}, u32[]{:S(2)}, u32[]{:S(2)}) collective-permute-start(bf16[512,512]{0,1:T(8,128)(2,1)} %get-tuple-element.49), channel_id=1, source_target_pairs={{0,4},{4,0},{1,5},{5,1},{2,6},{6,2},{3,7},{7,3},{8,12},{12,8},{9,1... | collective-permute-start | bytes 1572872 | tf_op jit(solution)/shard_map/ppermute | solution.py:212
  232.7 11.9 %collective-permute-start.15 = (bf16[2,128,1024]{2,1,0:T(8,128)(2,1)}, bf16[2,128,1024]{2,1,0:T(8,128)(2,1)}, u32[]{:S(2)}, u32[]{:S(2)}) collective-permute-start(bf16[2,128,1024]{2,1,0:T(8,128)(2,1)} %pad_maximum_fusion.6), channel_id=1, source_target_pairs={{0,1},{1,0},{2,3},{3,2},{4,5},{5,4},{6,7},{7,6},{8,9},{9,8},{10,11... | collective-permute-start | bytes 1572872 | tf_op jit(solution)/shard_map/ppermute | solution.py:212
  234.1 18.1 %collective-permute-start.18 = (bf16[512,1024]{0,1:T(8,128)(2,1)}, bf16[512,1024]{0,1:T(8,128)(2,1)S(1)}, u32[]{:S(2)}, u32[]{:S(2)}) collective-permute-start(bf16[512,1024]{0,1:T(8,128)(2,1)} %copy.25), channel_id=1, source_target_pairs={{0,8},{8,0},{16,24},{24,16},{1,9},{9,1},{17,25},{25,17},{2,10},{10... | collective-permute-start | bytes 3145736 | tf_op jit(solution)/shard_map/ppermute | solution.py:183
  234.1 14.2 %collective-permute-start.19 = (bf16[512,512]{0,1:T(8,128)(2,1)}, bf16[512,512]{0,1:T(8,128)(2,1)}, u32[]{:S(2)}, u32[]{:S(2)}) collective-permute-start(bf16[512,512]{0,1:T(8,128)(2,1)} %collective-permute-done.9), channel_id=1, source_target_pairs={{0,16},{16,8},{8,24},{24,0},{1,17},{17,9},{9,25},{25,1},{2,18},{18... | collective-permute-start | bytes 1572872 | tf_op jit(solution)/shard_map/ppermute | solution.py:190
  246.0 22.1 %collective-permute-start.17 = (bf16[512,1024]{1,0:T(8,128)(2,1)S(1)}, bf16[512,1024]{1,0:T(8,128)(2,1)S(1)}, u32[]{:S(2)}, u32[]{:S(2)}) collective-permute-start(bf16[512,1024]{1,0:T(8,128)(2,1)S(1)} %bitcast.82), channel_id=1, source_target_pairs={{0,4},{4,0},{1,5},{5,1},{2,6},{6,2},{3,7},{7,3},{8,12},{12,8},{9,1... | collective-permute-start | bytes 3145736 | tf_op jit(solution)/shard_map/ppermute | solution.py:212
  248.3 30.5 %collective-permute-start.11 = (bf16[512,512]{0,1:T(8,128)(2,1)}, bf16[512,512]{0,1:T(8,128)(2,1)S(1)}, u32[]{:S(2)}, u32[]{:S(2)}) collective-permute-start(bf16[512,512]{0,1:T(8,128)(2,1)} %collective-permute-done.10), channel_id=1, source_target_pairs={{0,16},{16,8},{8,24},{24,0},{1,17},{17,9},{9,25},{25,1},{2,18},{18... | collective-permute-start | bytes 1572872 | tf_op jit(solution)/shard_map/ppermute | solution.py:190
  277.2 18.3 %collective-permute-start.22 = (bf16[512,896]{1,0:T(8,128)(2,1)S(1)}, bf16[512,896]{1,0:T(8,128)(2,1)S(1)}, u32[]{:S(2)}, u32[]{:S(2)}) collective-permute-start(bf16[512,896]{1,0:T(8,128)(2,1)S(1)} %shard_map.18.refs_0_.refs_7_), channel_id=1, source_target_pairs={{0,16},{8,24},{16,0},{24,8},{1,17},{9,25},{17,1},{25,9},{2,18},{10... | collective-permute-start | bytes 2752520 | tf_op jit(solution)/shard_map/ppermute | solution.py:180
  278.8 18.4 %collective-permute-start.21 = (bf16[512,896]{1,0:T(8,128)(2,1)S(1)}, bf16[512,896]{1,0:T(8,128)(2,1)}, u32[]{:S(2)}, u32[]{:S(2)}) collective-permute-start(bf16[512,896]{1,0:T(8,128)(2,1)S(1)} %shard_map.18.refs_0_.refs_7_), channel_id=1, source_target_pairs={{0,8},{8,0},{16,24},{24,16},{1,9},{9,1},{17,25},{25,17},{2,10},{10... | collective-permute-start | bytes 2752520 | tf_op jit(solution)/shard_map/ppermute | solution.py:183
  287.8 9.3 %collective-permute-start.24 = (bf16[512,896]{1,0:T(8,128)(2,1)S(1)}, bf16[512,896]{1,0:T(8,128)(2,1)}, u32[]{:S(2)}, u32[]{:S(2)}) collective-permute-start(bf16[512,896]{1,0:T(8,128)(2,1)S(1)} %shard_map.19.refs_4_.refs_8_), channel_id=1, source_target_pairs={{0,8},{8,0},{16,24},{24,16},{1,9},{9,1},{17,25},{25,17},{2,10},{10... | collective-permute-start | bytes 2752520 | tf_op jit(solution)/shard_map/ppermute | solution.py:183
  295.6 2.6 collective-permute-start.23
  295.6 22.9 %collective-permute-start.20 = (bf16[512,896]{1,0:T(8,128)(2,1)S(1)}, bf16[512,896]{1,0:T(8,128)(2,1)}, u32[]{:S(2)}, u32[]{:S(2)}) collective-permute-start(bf16[512,896]{1,0:T(8,128)(2,1)S(1)} %shard_map.19.refs_4_.refs_8_), channel_id=1, source_target_pairs={{0,16},{8,24},{16,0},{24,8},{1,17},{9,25},{17,1},{25,9},{2,18},{10... | collective-permute-start | bytes 2752520 | tf_op jit(solution)/shard_map/ppermute | solution.py:180
  318.5 2.7 collective-permute-start.25
  (4 other events, 7.9 us)

commit v3 on v2

--- a/solution.py
+++ b/solution.py
@@ -63,26 +63,22 @@
         out_specs=pl.BlockSpec((rows, width), lambda at: (0, 0)),
         scratch_shapes=[pltpu.VMEM((rows, width), jnp.float32)],
         compiler_params=pltpu.CompilerParams(vmem_limit_bytes=48 << 20),
-        cost_estimate=pl.CostEstimate(
-            flops=2 * rows * depth * width,
-            bytes_accessed=2 * (rows * depth + depth * width + rows * width),
-            transcendentals=0,
-        ),
     )(left, right)
 
 
 def second_begin_kernel(count):
     def kernel(columns, left, *refs):
-        rights, (held, top, bottom, out) = refs[:count], refs[count:]
+        rights, (held, image_here, image_there, out) = refs[:count], refs[count:]
         factor = 0.2 * math.sqrt(COLS)
 
         @pl.when(pl.program_id(0) == 0)
         def _():
-            half = top.shape[0]
-            for at, image in ((0, top), (half, bottom)):
-                rows = pl.ds(at, half)
-                out[rows, :] = factor * (
-                    coef_linear * held[rows, :].astype(jnp.float32)
+            half = image_here.shape[0]
+            side = columns[count]
+            for at, row_half, image in ((0, side, image_here), (half, 1 - side, image_there)):
+                held_rows = held[pl.ds(pl.multiple_of(row_half * half, half), half), :]
+                out[pl.ds(at, half), :] = factor * (
+                    coef_linear * held_rows.astype(jnp.float32)
                     + coef_cubic * image[...].astype(jnp.float32)
                 )
 
@@ -110,7 +106,11 @@
 
         @pl.when(pl.program_id(0) == count - 1)
         def _():
-            out[...] = total[...].astype(out.dtype)
+            half = total.shape[0] // 2
+            side = columns[count]
+            for at, row_half in ((0, side), (half, 1 - side)):
+                rows = pl.ds(pl.multiple_of(row_half * half, half), half)
+                out[rows, :] = total[pl.ds(at, half), :].astype(out.dtype)
 
     return kernel
 
@@ -136,33 +136,22 @@
             scratch_shapes=[pltpu.VMEM((rows, width), jnp.float32)] if scratch else [],
         ),
         compiler_params=pltpu.CompilerParams(vmem_limit_bytes=limit),
-        cost_estimate=pl.CostEstimate(
-            flops=2 * rows * depth * width * len(rights),
-            bytes_accessed=2 * len(rights) * depth * (rows + width) + 8 * rows * width,
-            transcendentals=0,
-        ),
     )(columns, gram, *rights, *others)
 
 
-def begin_kernel(side, block, out):
+def begin_kernel(block, out):
     out[...] = block[...]
 
 
-def begin_gram(block, side, columns, column_at):
+def begin_gram(block, columns, column_at):
     rows, width = block.shape
     return pl.pallas_call(
         begin_kernel,
         out_shape=jax.ShapeDtypeStruct((2 * rows, columns * width), block.dtype),
-        grid_spec=pltpu.PrefetchScalarGridSpec(
-            num_scalar_prefetch=1,
-            grid=(1,),
-            in_specs=[pl.BlockSpec((rows, width), lambda at, side: (0, 0))],
-            out_specs=pl.BlockSpec((rows, width), lambda at, side: (side[0], column_at)),
-        ),
-        cost_estimate=pl.CostEstimate(
-            flops=0, bytes_accessed=4 * rows * width, transcendentals=0
-        ),
-    )(side.reshape(1), block)
+        grid=(1,),
+        in_specs=[pl.BlockSpec((rows, width), lambda at: (0, 0))],
+        out_specs=pl.BlockSpec((rows, width), lambda at: (0, column_at)),
+    )(block)
 
 
 def by_rows(value):
@@ -305,8 +294,8 @@
 
         ahead_got = ahead.send()
         ahead.take(ahead_got)
-        pair.value = after(pair.value, ahead_got)
-        pair_got = pair.send()
+        pair.value, own.value, _ = lax.optimization_barrier((pair.value, own.value, ahead_got))
+        own_got, pair_got = own.send(), pair.send()
         while ahead.steps:
             ahead.take(ahead.send())
 
@@ -322,68 +311,84 @@
             return lax.dynamic_update_slice(gram_rows, block, (row, column))
 
         rung_here = [ring(block, at) for at, block in zip(steps, own_half)]
-        pair.take(after(pair_got, *own_half))
+        own_got, pair_got, *own_half = lax.optimization_barrier((own_got, pair_got, *own_half))
+        own.take(own_got)
+        pair.take(pair_got)
+        while len(own.steps) > 1:
+            own.take(own.send())
         while len(pair.steps) > 1:
             pair.take(pair.send())
-        own.value = after(own.value, *own_half)
-        own_got, pair_got = own.send(), pair.send()
+        own_got = own.send()
+        pair.value = after(pair.value, own.value)
+        pair_got = pair.send()
         came, rung_there = [], []
-        for side in range(2):
-            columns = [block[:, side * half : (side + 1) * half] for block in own_half]
+
+        for start in (there, here):
+            columns = [lax.dynamic_slice_in_dim(block, start, half, 1) for block in own_half]
             if came:
                 columns[0] = after(columns[0], *came[0])
             came.append([swap(block, *over_grp[-1]) for block in columns])
-            rung_there.append([ring(block, at) for at, block in zip(steps, came[side])])
-
-        gram_rows = begin_gram(own_half[0], side_here, n_row, 2)
+            rung_there.append([ring(block, at) for at, block in zip(steps, came[-1])])
+
+        gram_rows = begin_gram(own_half[0], n_row, 2)
         for at, block in zip(steps[1:], own_half[1:]):
-            gram_rows = put(block, here, 2 * at * rows)
-
-        def put_came(side):
-            (*blocks, held_rows) = lax.optimization_barrier((*came[side], gram_rows))
+            gram_rows = put(block, 0, 2 * at * rows)
+
+        def put_came(which, column):
+            (*blocks, held_rows) = lax.optimization_barrier((*came[which], gram_rows))
             for at, block in zip(steps, blocks):
                 held_rows = lax.dynamic_update_slice(
-                    held_rows, block, (there, 2 * at * rows + side * half)
+                    held_rows, block, (half, 2 * at * rows + column)
                 )
             return held_rows
 
-        def put_rung(blocks, row, offset):
+        def put_rung(blocks, row, column, part=None):
             (*blocks, held_rows) = lax.optimization_barrier((*blocks, gram_rows))
             for at, block in zip(steps, blocks):
+                if part is not None:
+                    block = lax.dynamic_slice_in_dim(block, part, half, 1)
                 held_rows = lax.dynamic_update_slice(
-                    held_rows, block.T, (row, (2 * at + 1) * rows + offset)
+                    held_rows, block.T, (row, (2 * at + 1) * rows + column)
                 )
             return held_rows
 
-        gram_rows = put_came(0)
+        gram_rows = put_came(0, here)
+        own_got, gram_rows = lax.optimization_barrier((own_got, gram_rows))
+        own.take(own_got)
+        own_rows = own.value.reshape(half, rows)
+        own_came = swap(after(own_rows, *came[1]), *over_grp[-1])
+        gram_rows = put(own_rows, 0, 0)
         pair_got, gram_rows = lax.optimization_barrier((pair_got, gram_rows))
         pair.take(pair_got)
         pair_half = pair.value.reshape(half, rows)
         pair_other = on_chip(pair_half)
-        gram_rows = put(pair_half[:, :half], 0, rows + quadrant_at)
-        gram_rows = put(pair_half[:, half:], quadrant_at, rows + half)
-        own_got, gram_rows = lax.optimization_barrier((own_got, gram_rows))
-        own.take(own_got)
-        while len(own.steps) > 1:
-            own.take(own.send())
-        own_got = own.send()
-        gram_rows, _ = lax.optimization_barrier((gram_rows, own.value))
-        gram_rows = put_came(1)
-        gram_rows = put_rung(rung_here, 0, here)
-        own_got, gram_rows = lax.optimization_barrier((own_got, gram_rows))
-        own.take(own_got)
-        own_rows = own.value.reshape(half, rows)
-        own_came = swap(own_rows, *over_grp[-1])
-        gram_rows = put(own_rows, here, 0)
+        gram_rows = put_came(1, there)
+        gram_rows = put_rung(rung_here, 0, here, here)
         gram_rows = put_rung(rung_there[0], 0, there)
         pair_other, gram_rows = lax.optimization_barrier((pair_other, gram_rows))
-        gram_rows = put(pair_other[:, :half].T, half - quadrant_at, rows)
-        gram_rows = put(pair_other[:, half:].T, half, rows + half - quadrant_at)
-        own_came, gram_rows = lax.optimization_barrier((own_came, gram_rows))
-        gram_rows = put(own_came, there, 0)
+
+        left, right = pair_half[:, :half], pair_half[:, half:]
+        left_t, right_t = pair_other[:, :half].T, pair_other[:, half:].T
+        as_first, as_upper = core == 0, side_here == 0
+
+        def put_pair(row, upper):
+            first = jnp.where(
+                as_first, jnp.where(upper, left, left_t), jnp.where(upper, left_t, right_t)
+            )
+            second = jnp.where(
+                as_first, jnp.where(upper, right, right_t), jnp.where(upper, left, right)
+            )
+            held_rows = lax.dynamic_update_slice(gram_rows, first, (row, rows))
+            return lax.dynamic_update_slice(held_rows, second, (row, rows + half))
+
+        gram_rows = put_pair(0, as_upper)
         images = [product(gram_rows, whole, half, 0)]
         gram_rows = after(gram_rows, images[0])
+        gram_rows = put_pair(half, jnp.logical_not(as_upper))
+        gram_rows = put_rung(rung_here, half, here, there)
         gram_rows = put_rung(rung_there[1], half, there)
+        own_came, gram_rows = lax.optimization_barrier((own_came, gram_rows))
+        gram_rows = put(own_came, half, 0)
         images.append(product(gram_rows, whole, half, 1))
 
         def spread(image, *earlier):
@@ -395,11 +400,12 @@
                 found += [got, on_chip(got)]
             return found
 
-        top = spread(images[0], images[1])
+        found_here = spread(images[0], images[1])
+        side_there = 1 - side_here
         if half % 128 == 0:
-            other = on_chip(images[1])
-            early = [*top, images[1], other]
-            columns = [2 * slot for slot in slots] + [jnp.int32(1), jnp.int32(3)]
+            early = [*found_here, images[1], on_chip(images[1])]
+            columns = [2 * slot + side_here for slot in slots]
+            columns += [side_there, 2 + side_there, side_here]
             begun = add_terms(
                 second_begin_kernel,
                 gram_rows,
@@ -412,11 +418,11 @@
             for step in range(1, n_chip):
                 got = after(from_chip(images[1], step), begun)
                 late += [got, on_chip(got)]
-            columns = jnp.stack([2 * slot + 1 for slot in slots[2:]])
+            columns = [2 * slot + side_there for slot in slots[2:]] + [side_here]
             return add_terms(
                 second_end_kernel,
                 gram_rows,
-                columns,
+                jnp.stack(columns),
                 late,
                 (begun,),
                 jnp.bfloat16,
@@ -424,17 +430,20 @@
                 limit=58 << 20,
             )
 
-        bottom = spread(images[1])
-        spread_image = in_order(bottom, half, in_order(top))
+        spread_image = in_order(spread(images[1]), there, in_order(found_here, here))
         second_image = jnp.dot(gram_rows, spread_image, preferred_element_type=jnp.float32)
-        image = jnp.concatenate(images, axis=0)
         factor = 0.2 * math.sqrt(COLS)
-        combined = (
-            coef_linear * held.astype(jnp.float32)
-            + coef_cubic * image.astype(jnp.float32)
-            + coef_quintic * second_image
-        )
-        return (factor * combined).astype(jnp.bfloat16)
+        update = jnp.zeros(held.shape, jnp.bfloat16)
+        for at, start in enumerate((here, there)):
+            combined = (
+                coef_linear * lax.dynamic_slice_in_dim(held, start, half, 0).astype(jnp.float32)
+                + coef_cubic * images[at].astype(jnp.float32)
+                + coef_quintic * second_image[at * half : (at + 1) * half]
+            )
+            update = lax.dynamic_update_slice_in_dim(
+                update, (factor * combined).astype(jnp.bfloat16), start, 0
+            )
+        return update
 
     return body
 

time: 331 us -> 331 us (level)
  other arithmetic: 12.7 us -> 16.2 us
    ppermute x3, waiting for transfers between devices: 26.9 us -> 20.4 us  [from_chip(): return lax.ppermute(value, 'fsdp', pairs)]
    dynamic_update_slice x0 -> x4, other arithmetic: none -> 4.4 us  [the longest x2 2.23 us: put_pair(): held_rows = lax.dynamic_update_slice(gram_rows, first, (row, rows))]
    ppermute x10, waiting for transfers between devices: 58.1 us -> 62.3 us  [swap(): return lax.ppermute(value, axis, [(at, at ^ bit) for at in range(size)])]
  transfers between devices with their start and end apart: 28 -> 28, of which waited for: 17 -> 19; matrix products, arithmetic and copies ran while one was open for 16% -> 16% of each run, Pallas kernels for 10% -> 10%
where the time goes in v3:
time: 331 us; the launch traced here: 330 us
  waiting for transfers between devices  150 us (45%)
  blocking collectives  50.6 us (15%)
  Pallas kernels  39.1 us (12%)
  local copies, waits for them, and re-layouts  35.2 us (11%)
  starting transfers between devices  28.6 us (9%)
  other arithmetic  16.2 us (5%)
  matrix products  10.1 us (3%)
    ppermute x10, waiting for transfers between devices, swap(): return lax.ppermute(value, axis, [(at, at ^ bit) for at in range(size)])  62.3 us
    all_to_all x1, blocking collectives, body(): lax.all_to_all(iterate, over, split_axis=1, concat_axis=0, tiled=True)  50.6 us
    ppermute x3, waiting for transfers between devices, begin_sum(): got = lax.ppermute(sent, 'grp', [(at, at ^ bit) for at in range(n_grp)])  45 us
    pallas_call x2, Pallas kernels, add_terms(): pl.pallas_call(kernel(len(rights)), out_shape=jax.ShapeDtypeStruct((rows,...  20.5 us
    ppermute x3, waiting for transfers between devices, from_chip(): return lax.ppermute(value, 'fsdp', pairs)  20.4 us
    all_to_all x2, waiting for transfers between devices, to_rep(): return lax.all_to_all(cut, 'rep', split_axis=0, concat_axis=0, tiled=True)  18 us
    pallas_call x2, Pallas kernels, product(): pl.pallas_call(first_kernel, out_shape=jax.ShapeDtypeStruct((rows, width)...  16.2 us
    dynamic_update_slice x4, local copies, waits for them, and re-layouts, in_order(): lax.dynamic_update_slice(whole, block, (slots[at] * rows + start, 0))  12.1 us
  transfers between devices with their start and end apart: 28, of which 19 were waited for; matrix products, arithmetic and copies ran while one was open for 16% of the time, Pallas kernels for 10%

profile of v3, /device:TPU:0, one launch (start us, length us, event | category | flops | bytes accessed | tf_op | source)
XLA Modules:
  0.0 330.1 jit_solution(16147185754689069516)
XLA Ops:
  1.8 50.6 %all_to_all.29 = bf16[128,8,896]{2,0,1:T(8,128)(2,1)S(1)} all-to-all(bf16[128,8,896]{2,0,1:T(8,128)(2,1)S(1)} %bitcast.112), channel_id=1, replica_groups=mesh['fsdp'=4,'grp'=2,'rep'=4] {'grp','rep'}, dimensions={1} | all-to-all | bytes 3670016 | tf_op jit(solution)/shard_map/all_to_all | solution.py:242
  54.0 2.4 convolution_convert_fusion
  62.5 20.0 %collective-permute-done.1 = bf16[512,1024]{1,0:T(8,128)(2,1)S(1)} collective-permute-done((bf16[512,1024]{1,0:T(8,128)(2,1)S(1)}, bf16[512,1024]{1,0:T(8,128)(2,1)S(1)}, u32[]{:S(2)}, u32[]{:S(2)}) %collective-permute-start.1) | collective-permute-done | bytes 1048608 | tf_op jit(solution)/shard_map/ppermute | solution.py:189
  82.5 12.4 %collective-permute-done = bf16[1024,896]{1,0:T(8,128)(2,1)} collective-permute-done((bf16[1024,896]{1,0:T(8,128)(2,1)S(1)}, bf16[1024,896]{1,0:T(8,128)(2,1)}, u32[]{:S(2)}, u32[]{:S(2)}) %collective-permute-start) | collective-permute-done | bytes 1835040 | tf_op jit(solution)/shard_map/ppermute | solution.py:169
  97.1 1.9 add_convert_fusion.1
  100.4 3.6 %all-to-all-start.1 = ((bf16[4,192,1024]{2,1,0:T(8,128)(2,1)}), bf16[4,192,1024]{2,1,0:T(8,128)(2,1)S(1)}, u32[]{:S(2)}, u32[]{:S(2)}) async-start(bf16[4,192,1024]{2,1,0:T(8,128)(2,1)} %pad_maximum_fusion), calls=%async_computation.1 | async-start | bytes 3145728 | tf_op jit(solution)/shard_map/all_to_all | solution.py:234
  104.0 3.9 %convert_bitcast_fusion = bf16[1024,1024]{1,0:T(8,128)(2,1)S(1)} fusion(bf16[1024,896]{1,0:T(8,128)(2,1)S(1)} %bitcast.101, bf16[1024,896]{1,0:T(8,128)(2,1)} %collective-permute-done, bf16[1024,896]{1,0:T(8,128)(2,1)} %collective-permute-done.4, pred[]{:T(512)S(6)} %lt.82), kind=kOutput, calls=%fused_computation.1 | convolution fusion | flops 1881014272 | bytes 7602177 | tf_op jit(solution)/shard_map/dot_general | solution.py:24
  108.6 25.0 %collective-permute-done.5 = bf16[512,1024]{1,0:T(8,128)(2,1)S(1)} collective-permute-done((bf16[512,1024]{1,0:T(8,128)(2,1)S(1)}, bf16[512,1024]{1,0:T(8,128)(2,1)S(1)}, u32[]{:S(2)}, u32[]{:S(2)}) %collective-permute-start.5) | collective-permute-done | bytes 1048608 | tf_op jit(solution)/shard_map/ppermute | solution.py:189
  135.0 6.9 %all-to-all-done.1 = bf16[4,192,1024]{2,1,0:T(8,128)(2,1)S(1)} async-done(((bf16[4,192,1024]{2,1,0:T(8,128)(2,1)}), bf16[4,192,1024]{2,1,0:T(8,128)(2,1)S(1)}, u32[]{:S(2)}, u32[]{:S(2)}) %all-to-all-start.1) | async-done | bytes 1572896 | tf_op jit(solution)/shard_map/all_to_all | solution.py:234
  141.8 4.3 %all-to-all-start.2 = ((bf16[4,128,1024]{2,1,0:T(8,128)(2,1)}), bf16[4,128,1024]{2,1,0:T(8,128)(2,1)}, u32[]{:S(2)}, u32[]{:S(2)}) async-start(bf16[4,128,1024]{2,1,0:T(8,128)(2,1)} %bitcast.114), calls=%async_computation.2 | async-start | bytes 2097152 | tf_op jit(solution)/shard_map/all_to_all | solution.py:234
  146.1 3.4 %dynamic_update_slice.48 = bf16[4096,896]{1,0:T(8,128)(2,1)} pad(bf16[1024,896]{1,0:T(8,128)(2,1)S(1)} %bitcast.102, bf16[]{:T(256)} %constant.128.clone.1), padding=0_3072x0_0 | pad | bytes 9175042 | tf_op jit(solution)/shard_map/dynamic_update_slice | solution.py:261
  149.6 2.9 constant_dynamic-update-slice_fusion.4
  152.4 2.9 constant_dynamic-update-slice_fusion.3
  156.3 2.9 constant_dynamic-update-slice_fusion.2.right
  160.9 11.2 %all-to-all-done.2 = bf16[4,128,1024]{2,1,0:T(8,128)(2,1)} async-done(((bf16[4,128,1024]{2,1,0:T(8,128)(2,1)}), bf16[4,128,1024]{2,1,0:T(8,128)(2,1)}, u32[]{:S(2)}, u32[]{:S(2)}) %all-to-all-start.2) | async-done | bytes 1048608 | tf_op jit(solution)/shard_map/all_to_all | solution.py:234
  173.6 12.3 %collective-permute-done.7 = bf16[128,1024]{1,0:T(8,128)(2,1)S(1)} collective-permute-done((bf16[128,1024]{1,0:T(8,128)(2,1)S(1)}, bf16[128,1024]{1,0:T(8,128)(2,1)S(1)}, u32[]{:S(2)}, u32[]{:S(2)}) %collective-permute-start.7) | collective-permute-done | bytes 262176 | tf_op jit(solution)/shard_map/ppermute | solution.py:201
  186.2 3.2 collective-permute-start.8
  189.5 21.3 %collective-permute-done.10 = bf16[2,128,1024]{2,1,0:T(8,128)(2,1)S(1)} collective-permute-done((bf16[2,128,1024]{2,1,0:T(8,128)(2,1)S(1)}, bf16[2,128,1024]{2,1,0:T(8,128)(2,1)S(1)}, u32[]{:S(2)}, u32[]{:S(2)}) %collective-permute-start.10) | collective-permute-done | bytes 524320 | tf_op jit(solution)/shard_map/ppermute | solution.py:201
  217.8 2.4 shard_map.17
  223.8 3.0 collective-permute-done.12
  228.9 2.5 collective-permute-done.11
  232.5 2.3 constant_dynamic-update-slice_fusion.1
  234.8 4.5 %collective-permute-done.17 = bf16[2,2,64,1024]{3,2,0,1:T(8,128)(2,1)} collective-permute-done((bf16[2,2,64,1024]{3,2,0,1:T(8,128)(2,1)S(1)}, bf16[2,2,64,1024]{3,2,0,1:T(8,128)(2,1)}, u32[]{:S(2)}, u32[]{:S(2)}) %collective-permute-start.17) | collective-permute-done | bytes 524320 | tf_op jit(solution)/shard_map/ppermute | solution.py:201
  243.7 11.4 %collective-permute-done.13 = bf16[512,512]{0,1:T(8,128)(2,1)} collective-permute-done((bf16[512,512]{0,1:T(8,128)(2,1)S(1)}, bf16[512,512]{0,1:T(8,128)(2,1)}, u32[]{:S(2)}, u32[]{:S(2)}) %collective-permute-start.13) | collective-permute-done | bytes 524320 | tf_op jit(solution)/shard_map/ppermute | solution.py:201
  265.8 8.1 %shard_map.18.refs_0_.refs_7_ = bf16[512,896]{1,0:T(8,128)(2,1)S(1)} custom-call(bf16[1024,4096]{1,0:T(8,128)(2,1)} %fusion.10.left, bf16[4096,896]{1,0:T(8,128)(2,1)} %constant_dynamic-update-slice_fusion.2.right), custom_call_target="tpu_custom_call" | custom-call | tf_op jit(solution)/shard_map/pallas_call | solution.py:55
  280.4 4.2 %collective-permute-done.14 = bf16[512,1024]{1,0:T(8,128)(2,1)} collective-permute-done((bf16[512,1024]{1,0:T(8,128)(2,1)}, bf16[512,1024]{1,0:T(8,128)(2,1)}, u32[]{:S(2)}, u32[]{:S(2)}) %collective-permute-start.14) | collective-permute-done | bytes 1048608 | tf_op jit(solution)/shard_map/ppermute | solution.py:201
  284.6 2.4 constant_dynamic-update-slice_fusion.left
  287.0 8.1 %shard_map.19.refs_4_.refs_8_ = bf16[512,896]{1,0:T(8,128)(2,1)S(1)} custom-call(bf16[1024,4096]{1,0:T(8,128)(2,1)} %constant_dynamic-update-slice_fusion.left, bf16[4096,896]{1,0:T(8,128)(2,1)} %constant_dynamic-update-slice_fusion.2.right), custom_call_target="tpu_custom_call" | custom-call | tf_op jit(solution)/shard_map/pallas_call | solution.py:55
  299.1 13.0 %shard_map.20.refs_2_ = f32[1024,896]{1,0:T(8,128)} custom-call(s32[7]{0:T(128)S(1)} %stack.125.columns, bf16[1024,4096]{1,0:T(8,128)(2,1)} %constant_dynamic-update-slice_fusion.left, bf16[512,896]{1,0:T(8,128)(2,1)S(1)} %shard_map.18.refs_0_.refs_7_, bf16[512,896]{1,0:T(8,128)(2,1)} %collective-permute-done.21.refs_1_, ...), custom_call_target="tpu_custom_call" | custom-call | tf_op jit(solution)/shard_map/pallas_call | solution.py:127
  312.1 6.9 %collective-permute-done.20.refs_0_ = bf16[512,896]{1,0:T(8,128)(2,1)} collective-permute-done((bf16[512,896]{1,0:T(8,128)(2,1)S(1)}, bf16[512,896]{1,0:T(8,128)(2,1)}, u32[]{:S(2)}, u32[]{:S(2)}) %collective-permute-start.20) | collective-permute-done | bytes 917536 | tf_op jit(solution)/shard_map/ppermute | solution.py:169
  319.7 2.1 collective-permute-done.25.refs_1_
  322.7 7.4 %shard_map.21 = bf16[1024,896]{1,0:T(8,128)(2,1)} custom-call(s32[3]{0:T(128)} %pad_add_fusion.columns, bf16[1024,4096]{1,0:T(8,128)(2,1)} %constant_dynamic-update-slice_fusion.left, bf16[512,896]{1,0:T(8,128)(2,1)} %collective-permute-done.20.refs_0_, bf16[512,896]{1,0:T(8,128)(2,1)} %copy-done.8, f32[1024,896]{1,0:T(8,128)} %shard_map.20.refs_2_), custom_call_target="tpu_custom_call" | custom-call | tf_op jit(solution)/shard_map/pallas_call | solution.py:127
  (116 shorter events, 60.2 us)
Async XLA Ops:
  52.4 93.7 %copy-start = (bf16[128,8,896]{2,0,1:T(8,128)(2,1)}, bf16[128,8,896]{2,0,1:T(8,128)(2,1)S(1)}, u32[]{:S(2)}) copy-start(bf16[128,8,896]{2,0,1:T(8,128)(2,1)S(1)} %all_to_all.29) | copy-start | bytes 5505028
  52.4 4.7 %collective-permute-start.2 = (bf16[1024,896]{1,0:T(8,128)(2,1)S(1)}, bf16[1024,896]{1,0:T(8,128)(2,1)}, u32[]{:S(2)}, u32[]{:S(2)}) collective-permute-start(bf16[1024,896]{1,0:T(8,128)(2,1)S(1)} %bitcast.96), channel_id=1, source_target_pairs={{0,8},{8,0},{16,24},{24,16},{1,9},{9,1},{17,25},{25,17},{2,10},{10... | collective-permute-start | bytes 5505032 | tf_op jit(solution)/shard_map/ppermute | solution.py:172
  52.4 42.5 %collective-permute-start = (bf16[1024,896]{1,0:T(8,128)(2,1)S(1)}, bf16[1024,896]{1,0:T(8,128)(2,1)}, u32[]{:S(2)}, u32[]{:S(2)}) collective-permute-start(bf16[1024,896]{1,0:T(8,128)(2,1)S(1)} %bitcast.97), channel_id=1, source_target_pairs={{0,16},{8,24},{16,0},{24,8},{1,17},{9,25},{17,1},{25,9},{2,18},{10... | collective-permute-start | bytes 5505032 | tf_op jit(solution)/shard_map/ppermute | solution.py:169
  56.4 26.1 %collective-permute-start.1 = (bf16[512,1024]{1,0:T(8,128)(2,1)S(1)}, bf16[512,1024]{1,0:T(8,128)(2,1)S(1)}, u32[]{:S(2)}, u32[]{:S(2)}) collective-permute-start(bf16[512,1024]{1,0:T(8,128)(2,1)S(1)} %constant_dynamic-slice_fusion.3), channel_id=1, source_target_pairs={{0,4},{4,0},{1,5},{5,1},{2,6},{6,2},{3,7},{7,3},{8,12},{12,8},{9,1... | collective-permute-start | bytes 3145736 | tf_op jit(solution)/shard_map/ppermute | solution.py:189
  61.0 34.0 %collective-permute-start.3 = (bf16[256,1024]{0,1:T(8,128)(2,1)S(1)}, bf16[256,1024]{0,1:T(8,128)(2,1)S(1)}, u32[]{:S(2)}, u32[]{:S(2)}) collective-permute-start(bf16[256,1024]{0,1:T(8,128)(2,1)S(1)} %fusion.6), channel_id=1, source_target_pairs={{0,4},{4,0},{1,5},{5,1},{2,6},{6,2},{3,7},{7,3},{8,12},{12,8},{9,1... | collective-permute-start | bytes 1572872 | tf_op jit(solution)/shard_map/ppermute | solution.py:189
  82.5 12.4 %copy-start.7 = (bf16[512,1024]{1,0:T(8,128)(2,1)}, bf16[512,1024]{1,0:T(8,128)(2,1)S(1)}, u32[]{:S(2)}) copy-start(bf16[512,1024]{1,0:T(8,128)(2,1)S(1)} %collective-permute-done.1) | copy-start | bytes 3145732
  95.7 8.2 %collective-permute-start.4 = (bf16[1024,896]{1,0:T(8,128)(2,1)}, bf16[1024,896]{1,0:T(8,128)(2,1)}, u32[]{:S(2)}, u32[]{:S(2)}) collective-permute-start(bf16[1024,896]{1,0:T(8,128)(2,1)} %collective-permute-done), channel_id=1, source_target_pairs={{0,8},{8,0},{16,24},{24,16},{1,9},{9,1},{17,25},{25,17},{2,10},{10... | collective-permute-start | bytes 5505032 | tf_op jit(solution)/shard_map/ppermute | solution.py:172
  100.4 41.4 %all-to-all-start.1 = ((bf16[4,192,1024]{2,1,0:T(8,128)(2,1)}), bf16[4,192,1024]{2,1,0:T(8,128)(2,1)S(1)}, u32[]{:S(2)}, u32[]{:S(2)}) async-start(bf16[4,192,1024]{2,1,0:T(8,128)(2,1)} %pad_maximum_fusion), calls=%async_computation.1 | async-start | bytes 3145728 | tf_op jit(solution)/shard_map/all_to_all | solution.py:234
  107.9 25.6 %collective-permute-start.5 = (bf16[512,1024]{1,0:T(8,128)(2,1)S(1)}, bf16[512,1024]{1,0:T(8,128)(2,1)S(1)}, u32[]{:S(2)}, u32[]{:S(2)}) collective-permute-start(bf16[512,1024]{1,0:T(8,128)(2,1)S(1)} %constant_dynamic-slice_fusion.2), channel_id=1, source_target_pairs={{0,4},{4,0},{1,5},{5,1},{2,6},{6,2},{3,7},{7,3},{8,12},{12,8},{9,1... | collective-permute-start | bytes 3145736 | tf_op jit(solution)/shard_map/ppermute | solution.py:189
  141.8 30.2 %all-to-all-start.2 = ((bf16[4,128,1024]{2,1,0:T(8,128)(2,1)}), bf16[4,128,1024]{2,1,0:T(8,128)(2,1)}, u32[]{:S(2)}, u32[]{:S(2)}) async-start(bf16[4,128,1024]{2,1,0:T(8,128)(2,1)} %bitcast.114), calls=%async_computation.2 | async-start | bytes 2097152 | tf_op jit(solution)/shard_map/all_to_all | solution.py:234
  155.7 5.2 %collective-permute-start.6 = (bf16[64,1024]{1,0:T(8,128)(2,1)S(1)}, bf16[64,1024]{1,0:T(8,128)(2,1)S(1)}, u32[]{:S(2)}, u32[]{:S(2)}) collective-permute-start(bf16[64,1024]{1,0:T(8,128)(2,1)S(1)} %slice.38), channel_id=1, source_target_pairs={{0,4},{4,0},{1,5},{5,1},{2,6},{6,2},{3,7},{7,3},{8,12},{12,8},{9,1... | collective-permute-start | bytes 393224 | tf_op jit(solution)/shard_map/ppermute | solution.py:201
  173.5 12.4 %collective-permute-start.7 = (bf16[128,1024]{1,0:T(8,128)(2,1)S(1)}, bf16[128,1024]{1,0:T(8,128)(2,1)S(1)}, u32[]{:S(2)}, u32[]{:S(2)}) collective-permute-start(bf16[128,1024]{1,0:T(8,128)(2,1)S(1)} %reduce_sum.25), channel_id=1, source_target_pairs={{0,2},{1,3},{2,0},{3,1},{4,6},{5,7},{6,4},{7,5},{8,10},{9,11},{10,... | collective-permute-start | bytes 786440 | tf_op jit(solution)/shard_map/ppermute | solution.py:201
  186.0 24.8 %collective-permute-start.10 = (bf16[2,128,1024]{2,1,0:T(8,128)(2,1)S(1)}, bf16[2,128,1024]{2,1,0:T(8,128)(2,1)S(1)}, u32[]{:S(2)}, u32[]{:S(2)}) collective-permute-start(bf16[2,128,1024]{2,1,0:T(8,128)(2,1)S(1)} %pad_maximum_fusion.4), channel_id=1, source_target_pairs={{0,1},{1,0},{2,3},{3,2},{4,5},{5,4},{6,7},{7,6},{8,9},{9,8},{10,11... | collective-permute-start | bytes 1572872 | tf_op jit(solution)/shard_map/ppermute | solution.py:201
  186.2 24.8 %collective-permute-start.8 = (bf16[128,1024]{1,0:T(8,128)(2,1)S(1)}, bf16[128,1024]{1,0:T(8,128)(2,1)S(1)}, u32[]{:S(2)}, u32[]{:S(2)}) collective-permute-start(bf16[128,1024]{1,0:T(8,128)(2,1)S(1)} %slice.39), channel_id=1, source_target_pairs={{0,2},{1,3},{2,0},{3,1},{4,6},{5,7},{6,4},{7,5},{8,10},{9,11},{10,... | collective-permute-start | bytes 786440 | tf_op jit(solution)/shard_map/ppermute | solution.py:201
  189.4 23.1 %collective-permute-start.9 = (bf16[2,64,1024]{2,1,0:T(8,128)(2,1)S(1)}, bf16[2,64,1024]{2,1,0:T(8,128)(2,1)S(1)}, u32[]{:S(2)}, u32[]{:S(2)}) collective-permute-start(bf16[2,64,1024]{2,1,0:T(8,128)(2,1)S(1)} %pad_maximum_fusion.7), channel_id=1, source_target_pairs={{0,2},{1,3},{2,0},{3,1},{4,6},{5,7},{6,4},{7,5},{8,10},{9,11},{10,... | collective-permute-start | bytes 786440 | tf_op jit(solution)/shard_map/ppermute | solution.py:201
  214.8 11.9 %collective-permute-start.12 = (bf16[512,512]{0,1:T(8,128)(2,1)}, bf16[512,512]{0,1:T(8,128)(2,1)}, u32[]{:S(2)}, u32[]{:S(2)}) collective-permute-start(bf16[512,512]{0,1:T(8,128)(2,1)} %get-tuple-element.90), channel_id=1, source_target_pairs={{0,4},{4,0},{1,5},{5,1},{2,6},{6,2},{3,7},{7,3},{8,12},{12,8},{9,1... | collective-permute-start | bytes 1572872 | tf_op jit(solution)/shard_map/ppermute | solution.py:201
  216.3 15.1 %collective-permute-start.11 = (bf16[2,128,1024]{2,1,0:T(8,128)(2,1)}, bf16[2,128,1024]{2,1,0:T(8,128)(2,1)S(1)}, u32[]{:S(2)}, u32[]{:S(2)}) collective-permute-start(bf16[2,128,1024]{2,1,0:T(8,128)(2,1)} %pad_maximum_fusion.5), channel_id=1, source_target_pairs={{0,1},{1,0},{2,3},{3,2},{4,5},{5,4},{6,7},{7,6},{8,9},{9,8},{10,11... | collective-permute-start | bytes 1572872 | tf_op jit(solution)/shard_map/ppermute | solution.py:201
  220.4 18.9 %collective-permute-start.17 = (bf16[2,2,64,1024]{3,2,0,1:T(8,128)(2,1)S(1)}, bf16[2,2,64,1024]{3,2,0,1:T(8,128)(2,1)}, u32[]{:S(2)}, u32[]{:S(2)}) collective-permute-start(bf16[2,2,64,1024]{3,2,0,1:T(8,128)(2,1)S(1)} %pad_maximum_fusion.6), channel_id=1, source_target_pairs={{0,1},{1,0},{2,3},{3,2},{4,5},{5,4},{6,7},{7,6},{8,9},{9,8},{10,11... | collective-permute-start | bytes 1572872 | tf_op jit(solution)/shard_map/ppermute | solution.py:201
  222.3 35.0 %collective-permute-start.16 = (bf16[512,1024]{0,1:T(8,128)(2,1)}, bf16[512,1024]{0,1:T(8,128)(2,1)S(1)}, u32[]{:S(2)}, u32[]{:S(2)}) collective-permute-start(bf16[512,1024]{0,1:T(8,128)(2,1)} %copy.21), channel_id=1, source_target_pairs={{0,16},{16,8},{8,24},{24,0},{1,17},{17,9},{9,25},{25,1},{2,18},{18... | collective-permute-start | bytes 3145736 | tf_op jit(solution)/shard_map/ppermute | solution.py:179
  234.8 5.8 %copy-start.10 = (bf16[512,512]{0,1:T(8,128)(2,1)S(1)}, bf16[512,512]{0,1:T(8,128)(2,1)}, u32[]{:S(2)}) copy-start(bf16[512,512]{0,1:T(8,128)(2,1)} %get-tuple-element.60) | copy-start | bytes 1572868
  240.6 21.4 %collective-permute-start.18 = (bf16[512,1024]{1,0:T(8,128)(2,1)S(1)}, bf16[512,1024]{1,0:T(8,128)(2,1)}, u32[]{:S(2)}, u32[]{:S(2)}) collective-permute-start(bf16[512,1024]{1,0:T(8,128)(2,1)S(1)} %bitcast.107), channel_id=1, source_target_pairs={{0,8},{8,0},{16,24},{24,16},{1,9},{9,1},{17,25},{25,17},{2,10},{10... | collective-permute-start | bytes 3145736 | tf_op jit(solution)/shard_map/ppermute | solution.py:172
  240.7 14.4 %collective-permute-start.13 = (bf16[512,512]{0,1:T(8,128)(2,1)S(1)}, bf16[512,512]{0,1:T(8,128)(2,1)}, u32[]{:S(2)}, u32[]{:S(2)}) collective-permute-start(bf16[512,512]{0,1:T(8,128)(2,1)S(1)} %copy-done.10), channel_id=1, source_target_pairs={{0,4},{4,0},{1,5},{5,1},{2,6},{6,2},{3,7},{7,3},{8,12},{12,8},{9,1... | collective-permute-start | bytes 1572872 | tf_op jit(solution)/shard_map/ppermute | solution.py:201
  242.2 17.0 %collective-permute-start.19 = (bf16[512,512]{0,1:T(8,128)(2,1)}, bf16[512,512]{0,1:T(8,128)(2,1)S(1)}, u32[]{:S(2)}, u32[]{:S(2)}) collective-permute-start(bf16[512,512]{0,1:T(8,128)(2,1)} %collective-permute-done.12), channel_id=1, source_target_pairs={{0,16},{16,8},{8,24},{24,0},{1,17},{17,9},{9,25},{25,1},{2,18},{18... | collective-permute-start | bytes 1572872 | tf_op jit(solution)/shard_map/ppermute | solution.py:179
  259.1 25.5 %collective-permute-start.14 = (bf16[512,1024]{1,0:T(8,128)(2,1)}, bf16[512,1024]{1,0:T(8,128)(2,1)}, u32[]{:S(2)}, u32[]{:S(2)}) collective-permute-start(bf16[512,1024]{1,0:T(8,128)(2,1)} %bitcast.23), channel_id=1, source_target_pairs={{0,4},{4,0},{1,5},{5,1},{2,6},{6,2},{3,7},{7,3},{8,12},{12,8},{9,1... | collective-permute-start | bytes 3145736 | tf_op jit(solution)/shard_map/ppermute | solution.py:201
  260.6 18.0 %collective-permute-start.15 = (bf16[512,512]{0,1:T(8,128)(2,1)}, bf16[512,512]{0,1:T(8,128)(2,1)}, u32[]{:S(2)}, u32[]{:S(2)}) collective-permute-start(bf16[512,512]{0,1:T(8,128)(2,1)} %collective-permute-done.13), channel_id=1, source_target_pairs={{0,16},{16,8},{8,24},{24,0},{1,17},{17,9},{9,25},{25,1},{2,18},{18... | collective-permute-start | bytes 1572872 | tf_op jit(solution)/shard_map/ppermute | solution.py:179
  265.8 9.6 %copy-start.3 = (bf16[512,512]{0,1:T(8,128)(2,1)S(1)}, bf16[512,512]{0,1:T(8,128)(2,1)}, u32[]{:S(2)}) copy-start(bf16[512,512]{0,1:T(8,128)(2,1)} %copy-done.2) | copy-start | bytes 1572868
  274.0 22.2 %collective-permute-start.22 = (bf16[512,896]{1,0:T(8,128)(2,1)S(1)}, bf16[512,896]{1,0:T(8,128)(2,1)S(1)}, u32[]{:S(2)}, u32[]{:S(2)}) collective-permute-start(bf16[512,896]{1,0:T(8,128)(2,1)S(1)} %shard_map.18.refs_0_.refs_7_), channel_id=1, source_target_pairs={{0,16},{8,24},{16,0},{24,8},{1,17},{9,25},{17,1},{25,9},{2,18},{10... | collective-permute-start | bytes 2752520 | tf_op jit(solution)/shard_map/ppermute | solution.py:169
  275.0 23.0 %collective-permute-start.21 = (bf16[512,896]{1,0:T(8,128)(2,1)S(1)}, bf16[512,896]{1,0:T(8,128)(2,1)}, u32[]{:S(2)}, u32[]{:S(2)}) collective-permute-start(bf16[512,896]{1,0:T(8,128)(2,1)S(1)} %shard_map.18.refs_0_.refs_7_), channel_id=1, source_target_pairs={{0,8},{8,0},{16,24},{24,16},{1,9},{9,1},{17,25},{25,17},{2,10},{10... | collective-permute-start | bytes 2752520 | tf_op jit(solution)/shard_map/ppermute | solution.py:172
  295.1 2.9 collective-permute-start.24
  296.2 2.9 collective-permute-start.23
  296.2 22.9 %collective-permute-start.20 = (bf16[512,896]{1,0:T(8,128)(2,1)S(1)}, bf16[512,896]{1,0:T(8,128)(2,1)}, u32[]{:S(2)}, u32[]{:S(2)}) collective-permute-start(bf16[512,896]{1,0:T(8,128)(2,1)S(1)} %shard_map.19.refs_4_.refs_8_), channel_id=1, source_target_pairs={{0,16},{8,24},{16,0},{24,8},{1,17},{9,25},{17,1},{25,9},{2,18},{10... | collective-permute-start | bytes 2752520 | tf_op jit(solution)/shard_map/ppermute | solution.py:169
  319.1 2.7 collective-permute-start.25
  (9 other events, 24.6 us)

commit v4 on v3

--- a/solution.py
+++ b/solution.py
@@ -294,8 +294,8 @@
 
         ahead_got = ahead.send()
         ahead.take(ahead_got)
-        pair.value, own.value, _ = lax.optimization_barrier((pair.value, own.value, ahead_got))
-        own_got, pair_got = own.send(), pair.send()
+        pair.value = after(pair.value, ahead_got)
+        pair_got = pair.send()
         while ahead.steps:
             ahead.take(ahead.send())
 
@@ -310,61 +310,66 @@
         def put(block, row, column):
             return lax.dynamic_update_slice(gram_rows, block, (row, column))
 
-        rung_here = [ring(block, at) for at, block in zip(steps, own_half)]
-        own_got, pair_got, *own_half = lax.optimization_barrier((own_got, pair_got, *own_half))
-        own.take(own_got)
+        def columns_from(start):
+            return [lax.dynamic_slice_in_dim(block, start, half, 1) for block in own_half]
+
+        def ring_all(blocks):
+            return [ring(block, at) for at, block in zip(steps, blocks)]
+
+        def swap_all(blocks):
+            return [swap(block, *over_grp[-1]) for block in blocks]
+
+        came_first = swap_all(columns_from(there))
+        rung_own = ring_all(columns_from(here))
+        pair_got, *own_half = lax.optimization_barrier((pair_got, *own_half))
         pair.take(pair_got)
-        while len(own.steps) > 1:
-            own.take(own.send())
         while len(pair.steps) > 1:
             pair.take(pair.send())
+        pair_got = pair.send()
+        own.value = after(own.value, *own_half)
         own_got = own.send()
-        pair.value = after(pair.value, own.value)
-        pair_got = pair.send()
-        came, rung_there = [], []
-
-        for start in (there, here):
-            columns = [lax.dynamic_slice_in_dim(block, start, half, 1) for block in own_half]
-            if came:
-                columns[0] = after(columns[0], *came[0])
-            came.append([swap(block, *over_grp[-1]) for block in columns])
-            rung_there.append([ring(block, at) for at, block in zip(steps, came[-1])])
+        rung_first = ring_all(came_first)
+        later = columns_from(here)
+        later[0] = after(later[0], *came_first)
+        came_second = swap_all(later)
+        later = columns_from(there)
+        later[0] = after(later[0], *rung_own)
+        rung_other = ring_all(later)
+        rung_second = ring_all(came_second)
 
         gram_rows = begin_gram(own_half[0], n_row, 2)
         for at, block in zip(steps[1:], own_half[1:]):
             gram_rows = put(block, 0, 2 * at * rows)
 
-        def put_came(which, column):
-            (*blocks, held_rows) = lax.optimization_barrier((*came[which], gram_rows))
+        def put_came(blocks, column):
+            (*blocks, held_rows) = lax.optimization_barrier((*blocks, gram_rows))
             for at, block in zip(steps, blocks):
                 held_rows = lax.dynamic_update_slice(
                     held_rows, block, (half, 2 * at * rows + column)
                 )
             return held_rows
 
-        def put_rung(blocks, row, column, part=None):
+        def put_rung(blocks, row, column):
             (*blocks, held_rows) = lax.optimization_barrier((*blocks, gram_rows))
             for at, block in zip(steps, blocks):
-                if part is not None:
-                    block = lax.dynamic_slice_in_dim(block, part, half, 1)
                 held_rows = lax.dynamic_update_slice(
                     held_rows, block.T, (row, (2 * at + 1) * rows + column)
                 )
             return held_rows
 
-        gram_rows = put_came(0, here)
-        own_got, gram_rows = lax.optimization_barrier((own_got, gram_rows))
-        own.take(own_got)
-        own_rows = own.value.reshape(half, rows)
-        own_came = swap(after(own_rows, *came[1]), *over_grp[-1])
-        gram_rows = put(own_rows, 0, 0)
+        gram_rows = after(gram_rows, *came_first)
         pair_got, gram_rows = lax.optimization_barrier((pair_got, gram_rows))
         pair.take(pair_got)
         pair_half = pair.value.reshape(half, rows)
         pair_other = on_chip(pair_half)
-        gram_rows = put_came(1, there)
-        gram_rows = put_rung(rung_here, 0, here, here)
-        gram_rows = put_rung(rung_there[0], 0, there)
+        gram_rows = put_rung(rung_own, 0, here)
+        own_got, gram_rows = lax.optimization_barrier((own_got, gram_rows))
+        own.take(own_got)
+        while len(own.steps) > 1:
+            own.take(own.send())
+        own_got = own.send()
+        gram_rows = after(gram_rows, own.value, *came_second)
+        gram_rows = put_rung(rung_first, 0, there)
         pair_other, gram_rows = lax.optimization_barrier((pair_other, gram_rows))
 
         left, right = pair_half[:, :half], pair_half[:, half:]
@@ -382,11 +387,18 @@
             return lax.dynamic_update_slice(held_rows, second, (row, rows + half))
 
         gram_rows = put_pair(0, as_upper)
+        own_got, gram_rows = lax.optimization_barrier((own_got, gram_rows))
+        own.take(own_got)
+        own_rows = own.value.reshape(half, rows)
+        own_came = swap(own_rows, *over_grp[-1])
+        gram_rows = put(own_rows, 0, 0)
         images = [product(gram_rows, whole, half, 0)]
         gram_rows = after(gram_rows, images[0])
+        gram_rows = put_rung(rung_other, half, here)
         gram_rows = put_pair(half, jnp.logical_not(as_upper))
-        gram_rows = put_rung(rung_here, half, here, there)
-        gram_rows = put_rung(rung_there[1], half, there)
+        gram_rows = put_came(came_first, here)
+        gram_rows = put_came(came_second, there)
+        gram_rows = put_rung(rung_second, half, there)
         own_came, gram_rows = lax.optimization_barrier((own_came, gram_rows))
         gram_rows = put(own_came, half, 0)
         images.append(product(gram_rows, whole, half, 1))

time: 331 us -> 324 us (0.979)
  waiting for transfers between devices: 150 us -> 139 us
    ppermute x10, waiting for transfers between devices: 62.3 us -> 51.2 us  [swap(): return lax.ppermute(value, axis, [(at, at ^ bit) for at in range(size)])]
  transfers between devices with their start and end apart: 28 -> 29, of which waited for: 19 -> 19; matrix products, arithmetic and copies ran while one was open for 16% -> 18% of each run, Pallas kernels for 10% -> 10%
where the time goes in v4:
time: 324 us; the launch traced here: 323 us
  waiting for transfers between devices  139 us (43%)
  blocking collectives  50.6 us (16%)
  Pallas kernels  39.1 us (12%)
  local copies, waits for them, and re-layouts  37 us (11%)
  starting transfers between devices  29.6 us (9%)
  other arithmetic  17 us (5%)
  matrix products  10.1 us (3%)
    ppermute x10, waiting for transfers between devices, swap(): return lax.ppermute(value, axis, [(at, at ^ bit) for at in range(size)])  51.2 us
    all_to_all x1, blocking collectives, body(): lax.all_to_all(iterate, over, split_axis=1, concat_axis=0, tiled=True)  50.6 us
    ppermute x3, waiting for transfers between devices, begin_sum(): got = lax.ppermute(sent, 'grp', [(at, at ^ bit) for at in range(n_grp)])  45 us
    pallas_call x2, Pallas kernels, add_terms(): pl.pallas_call(kernel(len(rights)), out_shape=jax.ShapeDtypeStruct((rows,...  20.5 us
    ppermute x3, waiting for transfers between devices, from_chip(): return lax.ppermute(value, 'fsdp', pairs)  18.4 us
    all_to_all x2, waiting for transfers between devices, to_rep(): return lax.all_to_all(cut, 'rep', split_axis=0, concat_axis=0, tiled=True)  18 us
    pallas_call x2, Pallas kernels, product(): pl.pallas_call(first_kernel, out_shape=jax.ShapeDtypeStruct((rows, width)...  16.3 us
    dynamic_update_slice x4, local copies, waits for them, and re-layouts, in_order(): lax.dynamic_update_slice(whole, block, (slots[at] * rows + start, 0))  12.1 us
  transfers between devices with their start and end apart: 29, of which 19 were waited for; matrix products, arithmetic and copies ran while one was open for 18% of the time, Pallas kernels for 10%

profile of v4, /device:TPU:0, one launch (start us, length us, event | category | flops | bytes accessed | tf_op | source)
XLA Modules:
  0.0 323.2 jit_solution(8300392476527065530)
XLA Ops:
  1.8 50.6 %all_to_all.29 = bf16[128,8,896]{2,0,1:T(8,128)(2,1)S(1)} all-to-all(bf16[128,8,896]{2,0,1:T(8,128)(2,1)S(1)} %bitcast.111), channel_id=1, replica_groups=mesh['fsdp'=4,'grp'=2,'rep'=4] {'grp','rep'}, dimensions={1} | all-to-all | bytes 3670016 | tf_op jit(solution)/shard_map/all_to_all | solution.py:242
  54.0 2.4 convolution_convert_fusion
  59.0 1.9 convolution_convert_fusion.2
  62.5 20.0 %collective-permute-done.1 = bf16[512,1024]{1,0:T(8,128)(2,1)S(1)} collective-permute-done((bf16[512,1024]{1,0:T(8,128)(2,1)S(1)}, bf16[512,1024]{1,0:T(8,128)(2,1)S(1)}, u32[]{:S(2)}, u32[]{:S(2)}) %collective-permute-start.1) | collective-permute-done | bytes 1048608 | tf_op jit(solution)/shard_map/ppermute | solution.py:189
  82.5 12.4 %collective-permute-done = bf16[1024,896]{1,0:T(8,128)(2,1)} collective-permute-done((bf16[1024,896]{1,0:T(8,128)(2,1)S(1)}, bf16[1024,896]{1,0:T(8,128)(2,1)}, u32[]{:S(2)}, u32[]{:S(2)}) %collective-permute-start) | collective-permute-done | bytes 1835040 | tf_op jit(solution)/shard_map/ppermute | solution.py:169
  97.1 1.9 add_convert_fusion.1
  100.4 3.6 %all-to-all-start.1 = ((bf16[4,192,1024]{2,1,0:T(8,128)(2,1)}), bf16[4,192,1024]{2,1,0:T(8,128)(2,1)S(1)}, u32[]{:S(2)}, u32[]{:S(2)}) async-start(bf16[4,192,1024]{2,1,0:T(8,128)(2,1)} %pad_maximum_fusion), calls=%async_computation.1 | async-start | bytes 3145728 | tf_op jit(solution)/shard_map/all_to_all | solution.py:234
  104.0 3.9 %convert_bitcast_fusion = bf16[1024,1024]{1,0:T(8,128)(2,1)S(1)} fusion(bf16[1024,896]{1,0:T(8,128)(2,1)S(1)} %bitcast.100, bf16[1024,896]{1,0:T(8,128)(2,1)} %collective-permute-done, bf16[1024,896]{1,0:T(8,128)(2,1)} %collective-permute-done.4, pred[]{:T(512)S(6)} %lt.82), kind=kOutput, calls=%fused_computation.1 | convolution fusion | flops 1881014272 | bytes 7602177 | tf_op jit(solution)/shard_map/dot_general | solution.py:24
  108.6 25.0 %collective-permute-done.5 = bf16[512,1024]{1,0:T(8,128)(2,1)S(1)} collective-permute-done((bf16[512,1024]{1,0:T(8,128)(2,1)S(1)}, bf16[512,1024]{1,0:T(8,128)(2,1)S(1)}, u32[]{:S(2)}, u32[]{:S(2)}) %collective-permute-start.5) | collective-permute-done | bytes 1048608 | tf_op jit(solution)/shard_map/ppermute | solution.py:189
  135.0 6.9 %all-to-all-done.1 = bf16[4,192,1024]{2,1,0:T(8,128)(2,1)S(1)} async-done(((bf16[4,192,1024]{2,1,0:T(8,128)(2,1)}), bf16[4,192,1024]{2,1,0:T(8,128)(2,1)S(1)}, u32[]{:S(2)}, u32[]{:S(2)}) %all-to-all-start.1) | async-done | bytes 1572896 | tf_op jit(solution)/shard_map/all_to_all | solution.py:234
  141.8 4.3 %all-to-all-start.2 = ((bf16[4,128,1024]{2,1,0:T(8,128)(2,1)}), bf16[4,128,1024]{2,1,0:T(8,128)(2,1)}, u32[]{:S(2)}, u32[]{:S(2)}) async-start(bf16[4,128,1024]{2,1,0:T(8,128)(2,1)} %bitcast.113), calls=%async_computation.2 | async-start | bytes 2097152 | tf_op jit(solution)/shard_map/all_to_all | solution.py:234
  146.1 3.4 %dynamic_update_slice.48 = bf16[4096,896]{1,0:T(8,128)(2,1)} pad(bf16[1024,896]{1,0:T(8,128)(2,1)S(1)} %bitcast.101, bf16[]{:T(256)} %constant.128.clone.1), padding=0_3072x0_0 | pad | bytes 9175042 | tf_op jit(solution)/shard_map/dynamic_update_slice | solution.py:261
  149.6 2.9 constant_dynamic-update-slice_fusion.5
  152.4 2.9 constant_dynamic-update-slice_fusion.4
  156.3 2.9 constant_dynamic-update-slice_fusion.3.right
  160.9 11.2 %all-to-all-done.2 = bf16[4,128,1024]{2,1,0:T(8,128)(2,1)} async-done(((bf16[4,128,1024]{2,1,0:T(8,128)(2,1)}), bf16[4,128,1024]{2,1,0:T(8,128)(2,1)}, u32[]{:S(2)}, u32[]{:S(2)}) %all-to-all-start.2) | async-done | bytes 1048608 | tf_op jit(solution)/shard_map/all_to_all | solution.py:234
  173.6 12.3 %collective-permute-done.7 = bf16[128,1024]{1,0:T(8,128)(2,1)S(1)} collective-permute-done((bf16[128,1024]{1,0:T(8,128)(2,1)S(1)}, bf16[128,1024]{1,0:T(8,128)(2,1)S(1)}, u32[]{:S(2)}, u32[]{:S(2)}) %collective-permute-start.7) | collective-permute-done | bytes 262176 | tf_op jit(solution)/shard_map/ppermute | solution.py:201
  186.2 3.2 collective-permute-start.8
  189.4 16.2 %collective-permute-done.9 = bf16[2,128,1024]{2,1,0:T(8,128)(2,1)S(1)} collective-permute-done((bf16[2,128,1024]{2,1,0:T(8,128)(2,1)S(1)}, bf16[2,128,1024]{2,1,0:T(8,128)(2,1)S(1)}, u32[]{:S(2)}, u32[]{:S(2)}) %collective-permute-start.9) | collective-permute-done | bytes 524320 | tf_op jit(solution)/shard_map/ppermute | solution.py:201
  209.4 2.4 shard_map.17
  214.2 6.0 %collective-permute-done.13 = bf16[512,512]{1,0:T(8,128)(2,1)} collective-permute-done((bf16[512,512]{1,0:T(8,128)(2,1)}, bf16[512,512]{1,0:T(8,128)(2,1)}, u32[]{:S(2)}, u32[]{:S(2)}) %collective-permute-start.13) | collective-permute-done | bytes 524320 | tf_op jit(solution)/shard_map/ppermute | solution.py:201
  229.5 8.1 %collective-permute-done.10 = bf16[128,1024]{1,0:T(8,128)(2,1)S(1)} collective-permute-done((bf16[128,1024]{1,0:T(8,128)(2,1)S(1)}, bf16[128,1024]{1,0:T(8,128)(2,1)S(1)}, u32[]{:S(2)}, u32[]{:S(2)}) %collective-permute-start.10) | collective-permute-done | bytes 262176 | tf_op jit(solution)/shard_map/ppermute | solution.py:201
  246.8 5.4 %collective-permute-done.14 = bf16[2,128,1024]{2,1,0:T(8,128)(2,1)} collective-permute-done((bf16[2,128,1024]{2,1,0:T(8,128)(2,1)}, bf16[2,128,1024]{2,1,0:T(8,128)(2,1)}, u32[]{:S(2)}, u32[]{:S(2)}) %collective-permute-start.14) | collective-permute-done | bytes 524320 | tf_op jit(solution)/shard_map/ppermute | solution.py:201
  255.9 2.3 constant_dynamic-update-slice_fusion.1.left
  258.2 8.2 %shard_map.18.refs_0_.refs_7_ = bf16[512,896]{1,0:T(8,128)(2,1)S(1)} custom-call(bf16[1024,4096]{1,0:T(8,128)(2,1)} %constant_dynamic-update-slice_fusion.1.left, bf16[4096,896]{1,0:T(8,128)(2,1)} %constant_dynamic-update-slice_fusion.3.right), custom_call_target="tpu_custom_call" | custom-call | tf_op jit(solution)/shard_map/pallas_call | solution.py:55
  268.0 1.9 bitcast_dynamic-update-slice_fusion.1
  278.6 2.4 constant_dynamic-update-slice_fusion.left
  281.0 8.1 %shard_map.19.refs_4_.refs_8_ = bf16[512,896]{1,0:T(8,128)(2,1)S(1)} custom-call(bf16[1024,4096]{1,0:T(8,128)(2,1)} %constant_dynamic-update-slice_fusion.left, bf16[4096,896]{1,0:T(8,128)(2,1)} %constant_dynamic-update-slice_fusion.3.right), custom_call_target="tpu_custom_call" | custom-call | tf_op jit(solution)/shard_map/pallas_call | solution.py:55
  293.1 13.0 %shard_map.20.refs_2_ = f32[1024,896]{1,0:T(8,128)} custom-call(s32[7]{0:T(128)S(1)} %stack.125.columns, bf16[1024,4096]{1,0:T(8,128)(2,1)} %constant_dynamic-update-slice_fusion.left, bf16[512,896]{1,0:T(8,128)(2,1)S(1)} %shard_map.18.refs_0_.refs_7_, bf16[512,896]{1,0:T(8,128)(2,1)} %collective-permute-done.22.refs_1_, ...), custom_call_target="tpu_custom_call" | custom-call | tf_op jit(solution)/shard_map/pallas_call | solution.py:127
  306.1 6.0 %collective-permute-done.21.refs_0_ = bf16[512,896]{1,0:T(8,128)(2,1)} collective-permute-done((bf16[512,896]{1,0:T(8,128)(2,1)S(1)}, bf16[512,896]{1,0:T(8,128)(2,1)}, u32[]{:S(2)}, u32[]{:S(2)}) %collective-permute-start.21) | collective-permute-done | bytes 917536 | tf_op jit(solution)/shard_map/ppermute | solution.py:169
  312.7 2.1 collective-permute-done.26.refs_1_
  315.7 7.4 %shard_map.21 = bf16[1024,896]{1,0:T(8,128)(2,1)} custom-call(s32[3]{0:T(128)} %pad_add_fusion.columns, bf16[1024,4096]{1,0:T(8,128)(2,1)} %constant_dynamic-update-slice_fusion.left, bf16[512,896]{1,0:T(8,128)(2,1)} %collective-permute-done.21.refs_0_, bf16[512,896]{1,0:T(8,128)(2,1)} %copy-done.9, f32[1024,896]{1,0:T(8,128)} %shard_map.20.refs_2_), custom_call_target="tpu_custom_call" | custom-call | tf_op jit(solution)/shard_map/pallas_call | solution.py:127
  (115 shorter events, 61.6 us)
Async XLA Ops:
  52.4 93.7 %copy-start = (bf16[128,8,896]{2,0,1:T(8,128)(2,1)}, bf16[128,8,896]{2,0,1:T(8,128)(2,1)S(1)}, u32[]{:S(2)}) copy-start(bf16[128,8,896]{2,0,1:T(8,128)(2,1)S(1)} %all_to_all.29) | copy-start | bytes 5505028
  52.4 4.7 %collective-permute-start.2 = (bf16[1024,896]{1,0:T(8,128)(2,1)S(1)}, bf16[1024,896]{1,0:T(8,128)(2,1)}, u32[]{:S(2)}, u32[]{:S(2)}) collective-permute-start(bf16[1024,896]{1,0:T(8,128)(2,1)S(1)} %bitcast.95), channel_id=1, source_target_pairs={{0,8},{8,0},{16,24},{24,16},{1,9},{9,1},{17,25},{25,17},{2,10},{10... | collective-permute-start | bytes 5505032 | tf_op jit(solution)/shard_map/ppermute | solution.py:172
  52.4 42.5 %collective-permute-start = (bf16[1024,896]{1,0:T(8,128)(2,1)S(1)}, bf16[1024,896]{1,0:T(8,128)(2,1)}, u32[]{:S(2)}, u32[]{:S(2)}) collective-permute-start(bf16[1024,896]{1,0:T(8,128)(2,1)S(1)} %bitcast.96), channel_id=1, source_target_pairs={{0,16},{8,24},{16,0},{24,8},{1,17},{9,25},{17,1},{25,9},{2,18},{10... | collective-permute-start | bytes 5505032 | tf_op jit(solution)/shard_map/ppermute | solution.py:169
  56.4 26.1 %collective-permute-start.1 = (bf16[512,1024]{1,0:T(8,128)(2,1)S(1)}, bf16[512,1024]{1,0:T(8,128)(2,1)S(1)}, u32[]{:S(2)}, u32[]{:S(2)}) collective-permute-start(bf16[512,1024]{1,0:T(8,128)(2,1)S(1)} %constant_dynamic-slice_fusion.5), channel_id=1, source_target_pairs={{0,4},{4,0},{1,5},{5,1},{2,6},{6,2},{3,7},{7,3},{8,12},{12,8},{9,1... | collective-permute-start | bytes 3145736 | tf_op jit(solution)/shard_map/ppermute | solution.py:189
  61.0 34.0 %collective-permute-start.3 = (bf16[256,1024]{0,1:T(8,128)(2,1)S(1)}, bf16[256,1024]{0,1:T(8,128)(2,1)S(1)}, u32[]{:S(2)}, u32[]{:S(2)}) collective-permute-start(bf16[256,1024]{0,1:T(8,128)(2,1)S(1)} %fusion.6), channel_id=1, source_target_pairs={{0,4},{4,0},{1,5},{5,1},{2,6},{6,2},{3,7},{7,3},{8,12},{12,8},{9,1... | collective-permute-start | bytes 1572872 | tf_op jit(solution)/shard_map/ppermute | solution.py:189
  95.7 8.2 %collective-permute-start.4 = (bf16[1024,896]{1,0:T(8,128)(2,1)}, bf16[1024,896]{1,0:T(8,128)(2,1)}, u32[]{:S(2)}, u32[]{:S(2)}) collective-permute-start(bf16[1024,896]{1,0:T(8,128)(2,1)} %collective-permute-done), channel_id=1, source_target_pairs={{0,8},{8,0},{16,24},{24,16},{1,9},{9,1},{17,25},{25,17},{2,10},{10... | collective-permute-start | bytes 5505032 | tf_op jit(solution)/shard_map/ppermute | solution.py:172
  100.4 41.4 %all-to-all-start.1 = ((bf16[4,192,1024]{2,1,0:T(8,128)(2,1)}), bf16[4,192,1024]{2,1,0:T(8,128)(2,1)S(1)}, u32[]{:S(2)}, u32[]{:S(2)}) async-start(bf16[4,192,1024]{2,1,0:T(8,128)(2,1)} %pad_maximum_fusion), calls=%async_computation.1 | async-start | bytes 3145728 | tf_op jit(solution)/shard_map/all_to_all | solution.py:234
  107.9 25.6 %collective-permute-start.5 = (bf16[512,1024]{1,0:T(8,128)(2,1)S(1)}, bf16[512,1024]{1,0:T(8,128)(2,1)S(1)}, u32[]{:S(2)}, u32[]{:S(2)}) collective-permute-start(bf16[512,1024]{1,0:T(8,128)(2,1)S(1)} %constant_dynamic-slice_fusion.4), channel_id=1, source_target_pairs={{0,4},{4,0},{1,5},{5,1},{2,6},{6,2},{3,7},{7,3},{8,12},{12,8},{9,1... | collective-permute-start | bytes 3145736 | tf_op jit(solution)/shard_map/ppermute | solution.py:189
  141.8 30.2 %all-to-all-start.2 = ((bf16[4,128,1024]{2,1,0:T(8,128)(2,1)}), bf16[4,128,1024]{2,1,0:T(8,128)(2,1)}, u32[]{:S(2)}, u32[]{:S(2)}) async-start(bf16[4,128,1024]{2,1,0:T(8,128)(2,1)} %bitcast.113), calls=%async_computation.2 | async-start | bytes 2097152 | tf_op jit(solution)/shard_map/all_to_all | solution.py:234
  155.7 30.5 %copy-start.5 = (bf16[192,1024]{1,0:T(8,128)(2,1)}, bf16[192,1024]{1,0:T(8,128)(2,1)S(1)}, u32[]{:S(2)}) copy-start(bf16[192,1024]{1,0:T(8,128)(2,1)S(1)} %reduce_sum.24) | copy-start | bytes 1179652
  155.7 5.2 %collective-permute-start.6 = (bf16[64,1024]{1,0:T(8,128)(2,1)S(1)}, bf16[64,1024]{1,0:T(8,128)(2,1)S(1)}, u32[]{:S(2)}, u32[]{:S(2)}) collective-permute-start(bf16[64,1024]{1,0:T(8,128)(2,1)S(1)} %slice.39), channel_id=1, source_target_pairs={{0,4},{4,0},{1,5},{5,1},{2,6},{6,2},{3,7},{7,3},{8,12},{12,8},{9,1... | collective-permute-start | bytes 393224 | tf_op jit(solution)/shard_map/ppermute | solution.py:201
  173.5 12.4 %collective-permute-start.7 = (bf16[128,1024]{1,0:T(8,128)(2,1)S(1)}, bf16[128,1024]{1,0:T(8,128)(2,1)S(1)}, u32[]{:S(2)}, u32[]{:S(2)}) collective-permute-start(bf16[128,1024]{1,0:T(8,128)(2,1)S(1)} %reduce_sum.25), channel_id=1, source_target_pairs={{0,2},{1,3},{2,0},{3,1},{4,6},{5,7},{6,4},{7,5},{8,10},{9,11},{10,... | collective-permute-start | bytes 786440 | tf_op jit(solution)/shard_map/ppermute | solution.py:201
  186.0 19.5 %collective-permute-start.9 = (bf16[2,128,1024]{2,1,0:T(8,128)(2,1)S(1)}, bf16[2,128,1024]{2,1,0:T(8,128)(2,1)S(1)}, u32[]{:S(2)}, u32[]{:S(2)}) collective-permute-start(bf16[2,128,1024]{2,1,0:T(8,128)(2,1)S(1)} %pad_maximum_fusion.4), channel_id=1, source_target_pairs={{0,1},{1,0},{2,3},{3,2},{4,5},{5,4},{6,7},{7,6},{8,9},{9,8},{10,11... | collective-permute-start | bytes 1572872 | tf_op jit(solution)/shard_map/ppermute | solution.py:201
  186.2 19.6 %collective-permute-start.8 = (bf16[2,64,1024]{2,1,0:T(8,128)(2,1)S(1)}, bf16[2,64,1024]{2,1,0:T(8,128)(2,1)S(1)}, u32[]{:S(2)}, u32[]{:S(2)}) collective-permute-start(bf16[2,64,1024]{2,1,0:T(8,128)(2,1)S(1)} %pad_maximum_fusion.7), channel_id=1, source_target_pairs={{0,2},{1,3},{2,0},{3,1},{4,6},{5,7},{6,4},{7,5},{8,10},{9,11},{10,... | collective-permute-start | bytes 786440 | tf_op jit(solution)/shard_map/ppermute | solution.py:201
  206.9 13.3 %collective-permute-start.13 = (bf16[512,512]{1,0:T(8,128)(2,1)}, bf16[512,512]{1,0:T(8,128)(2,1)}, u32[]{:S(2)}, u32[]{:S(2)}) collective-permute-start(bf16[512,512]{1,0:T(8,128)(2,1)} %get-tuple-element.97), channel_id=1, source_target_pairs={{0,4},{4,0},{1,5},{5,1},{2,6},{6,2},{3,7},{7,3},{8,12},{12,8},{9,1... | collective-permute-start | bytes 1572872 | tf_op jit(solution)/shard_map/ppermute | solution.py:201
  208.4 12.9 %collective-permute-start.12 = (bf16[2,2,64,1024]{3,2,0,1:T(8,128)(2,1)}, bf16[2,2,64,1024]{3,2,0,1:T(8,128)(2,1)S(1)}, u32[]{:S(2)}, u32[]{:S(2)}) collective-permute-start(bf16[2,2,64,1024]{3,2,0,1:T(8,128)(2,1)} %pad_maximum_fusion.5), channel_id=1, source_target_pairs={{0,1},{1,0},{2,3},{3,2},{4,5},{5,4},{6,7},{7,6},{8,9},{9,8},{10,11... | collective-permute-start | bytes 1572872 | tf_op jit(solution)/shard_map/ppermute | solution.py:201
  212.7 14.5 %collective-permute-start.11 = (bf16[512,512]{0,1:T(8,128)(2,1)}, bf16[512,512]{0,1:T(8,128)(2,1)}, u32[]{:S(2)}, u32[]{:S(2)}) collective-permute-start(bf16[512,512]{0,1:T(8,128)(2,1)} %copy.26), channel_id=1, source_target_pairs={{0,16},{16,8},{8,24},{24,0},{1,17},{17,9},{9,25},{25,1},{2,18},{18... | collective-permute-start | bytes 1572872 | tf_op jit(solution)/shard_map/ppermute | solution.py:179
  221.6 24.2 %copy-start.3 = (bf16[2,2,2,64,1024]{4,3,2,1,0:T(8,128)(2,1)}, bf16[2,2,2,64,1024]{4,3,2,1,0:T(8,128)(2,1)S(1)}, u32[]{:S(2)}) copy-start(bf16[2,2,2,64,1024]{4,3,2,1,0:T(8,128)(2,1)S(1)} %copy.18) | copy-start | bytes 3145732
  221.6 21.4 %collective-permute-start.15 = (bf16[512,1024]{1,0:T(8,128)(2,1)S(1)}, bf16[512,1024]{1,0:T(8,128)(2,1)}, u32[]{:S(2)}, u32[]{:S(2)}) collective-permute-start(bf16[512,1024]{1,0:T(8,128)(2,1)S(1)} %bitcast.106), channel_id=1, source_target_pairs={{0,8},{8,0},{16,24},{24,16},{1,9},{9,1},{17,25},{25,17},{2,10},{10... | collective-permute-start | bytes 3145736 | tf_op jit(solution)/shard_map/ppermute | solution.py:172
  222.2 15.3 %collective-permute-start.10 = (bf16[128,1024]{1,0:T(8,128)(2,1)S(1)}, bf16[128,1024]{1,0:T(8,128)(2,1)S(1)}, u32[]{:S(2)}, u32[]{:S(2)}) collective-permute-start(bf16[128,1024]{1,0:T(8,128)(2,1)S(1)} %slice.38), channel_id=1, source_target_pairs={{0,2},{1,3},{2,0},{3,1},{4,6},{5,7},{6,4},{7,5},{8,10},{9,11},{10,... | collective-permute-start | bytes 786440 | tf_op jit(solution)/shard_map/ppermute | solution.py:201
  224.6 15.3 %collective-permute-start.17 = (bf16[512,512]{0,1:T(8,128)(2,1)S(1)}, bf16[512,512]{0,1:T(8,128)(2,1)}, u32[]{:S(2)}, u32[]{:S(2)}) collective-permute-start(bf16[512,512]{0,1:T(8,128)(2,1)S(1)} %get-tuple-element.66), channel_id=1, source_target_pairs={{0,4},{4,0},{1,5},{5,1},{2,6},{6,2},{3,7},{7,3},{8,12},{12,8},{9,1... | collective-permute-start | bytes 1572872 | tf_op jit(solution)/shard_map/ppermute | solution.py:201
  227.2 14.1 %collective-permute-start.16 = (bf16[512,512]{1,0:T(8,128)(2,1)}, bf16[512,512]{1,0:T(8,128)(2,1)S(1)}, u32[]{:S(2)}, u32[]{:S(2)}) collective-permute-start(bf16[512,512]{1,0:T(8,128)(2,1)} %collective-permute-done.13), channel_id=1, source_target_pairs={{0,16},{16,8},{8,24},{24,0},{1,17},{17,9},{9,25},{25,1},{2,18},{18... | collective-permute-start | bytes 1572872 | tf_op jit(solution)/shard_map/ppermute | solution.py:179
  238.4 13.8 %collective-permute-start.14 = (bf16[2,128,1024]{2,1,0:T(8,128)(2,1)}, bf16[2,128,1024]{2,1,0:T(8,128)(2,1)}, u32[]{:S(2)}, u32[]{:S(2)}) collective-permute-start(bf16[2,128,1024]{2,1,0:T(8,128)(2,1)} %pad_maximum_fusion.6), channel_id=1, source_target_pairs={{0,1},{1,0},{2,3},{3,2},{4,5},{5,4},{6,7},{7,6},{8,9},{9,8},{10,11... | collective-permute-start | bytes 1572872 | tf_op jit(solution)/shard_map/ppermute | solution.py:201
  238.4 29.6 %collective-permute-start.20 = (bf16[512,512]{0,1:T(8,128)(2,1)}, bf16[512,512]{0,1:T(8,128)(2,1)}, u32[]{:S(2)}, u32[]{:S(2)}) collective-permute-start(bf16[512,512]{0,1:T(8,128)(2,1)} %get-tuple-element.73), channel_id=1, source_target_pairs={{0,16},{16,8},{8,24},{24,0},{1,17},{17,9},{9,25},{25,1},{2,18},{18... | collective-permute-start | bytes 1572872 | tf_op jit(solution)/shard_map/ppermute | solution.py:179
  241.6 34.6 %collective-permute-start.19 = (bf16[512,512]{0,1:T(8,128)(2,1)}, bf16[512,512]{0,1:T(8,128)(2,1)}, u32[]{:S(2)}, u32[]{:S(2)}) collective-permute-start(bf16[512,512]{0,1:T(8,128)(2,1)} %collective-permute-done.17), channel_id=1, source_target_pairs={{0,16},{16,8},{8,24},{24,0},{1,17},{17,9},{9,25},{25,1},{2,18},{18... | collective-permute-start | bytes 1572872 | tf_op jit(solution)/shard_map/ppermute | solution.py:179
  254.4 24.2 %collective-permute-start.18 = (bf16[512,1024]{1,0:T(8,128)(2,1)}, bf16[512,1024]{1,0:T(8,128)(2,1)}, u32[]{:S(2)}, u32[]{:S(2)}) collective-permute-start(bf16[512,1024]{1,0:T(8,128)(2,1)} %bitcast.32), channel_id=1, source_target_pairs={{0,4},{4,0},{1,5},{5,1},{2,6},{6,2},{3,7},{7,3},{8,12},{12,8},{9,1... | collective-permute-start | bytes 3145736 | tf_op jit(solution)/shard_map/ppermute | solution.py:201
  266.4 22.7 %collective-permute-start.23 = (bf16[512,896]{1,0:T(8,128)(2,1)S(1)}, bf16[512,896]{1,0:T(8,128)(2,1)S(1)}, u32[]{:S(2)}, u32[]{:S(2)}) collective-permute-start(bf16[512,896]{1,0:T(8,128)(2,1)S(1)} %shard_map.18.refs_0_.refs_7_), channel_id=1, source_target_pairs={{0,16},{8,24},{16,0},{24,8},{1,17},{9,25},{17,1},{25,9},{2,18},{10... | collective-permute-start | bytes 2752520 | tf_op jit(solution)/shard_map/ppermute | solution.py:169
  267.9 23.3 %collective-permute-start.22 = (bf16[512,896]{1,0:T(8,128)(2,1)S(1)}, bf16[512,896]{1,0:T(8,128)(2,1)}, u32[]{:S(2)}, u32[]{:S(2)}) collective-permute-start(bf16[512,896]{1,0:T(8,128)(2,1)S(1)} %shard_map.18.refs_0_.refs_7_), channel_id=1, source_target_pairs={{0,8},{8,0},{16,24},{24,16},{1,9},{9,1},{17,25},{25,17},{2,10},{10... | collective-permute-start | bytes 2752520 | tf_op jit(solution)/shard_map/ppermute | solution.py:172
  289.1 2.7 collective-permute-start.24
  289.2 3.9 %collective-permute-start.25 = (bf16[512,896]{1,0:T(8,128)(2,1)S(1)}, bf16[512,896]{1,0:T(8,128)(2,1)}, u32[]{:S(2)}, u32[]{:S(2)}) collective-permute-start(bf16[512,896]{1,0:T(8,128)(2,1)S(1)} %shard_map.19.refs_4_.refs_8_), channel_id=1, source_target_pairs={{0,8},{8,0},{16,24},{24,16},{1,9},{9,1},{17,25},{25,17},{2,10},{10... | collective-permute-start | bytes 2752520 | tf_op jit(solution)/shard_map/ppermute | solution.py:172
  289.7 22.4 %collective-permute-start.21 = (bf16[512,896]{1,0:T(8,128)(2,1)S(1)}, bf16[512,896]{1,0:T(8,128)(2,1)}, u32[]{:S(2)}, u32[]{:S(2)}) collective-permute-start(bf16[512,896]{1,0:T(8,128)(2,1)S(1)} %shard_map.19.refs_4_.refs_8_), channel_id=1, source_target_pairs={{0,16},{8,24},{16,0},{24,8},{1,17},{9,25},{17,1},{25,9},{2,18},{10... | collective-permute-start | bytes 2752520 | tf_op jit(solution)/shard_map/ppermute | solution.py:169
  312.1 2.7 collective-permute-start.26
  (8 other events, 51.8 us)

commit v5 on v4

--- a/solution.py
+++ b/solution.py
@@ -320,7 +320,7 @@
             return [swap(block, *over_grp[-1]) for block in blocks]
 
         came_first = swap_all(columns_from(there))
-        rung_own = ring_all(columns_from(here))
+        rung_own = ring_all(own_half)
         pair_got, *own_half = lax.optimization_barrier((pair_got, *own_half))
         pair.take(pair_got)
         while len(pair.steps) > 1:
@@ -332,9 +332,6 @@
         later = columns_from(here)
         later[0] = after(later[0], *came_first)
         came_second = swap_all(later)
-        later = columns_from(there)
-        later[0] = after(later[0], *rung_own)
-        rung_other = ring_all(later)
         rung_second = ring_all(came_second)
 
         gram_rows = begin_gram(own_half[0], n_row, 2)
@@ -349,9 +346,11 @@
                 )
             return held_rows
 
-        def put_rung(blocks, row, column):
+        def put_rung(blocks, row, column, part=None):
             (*blocks, held_rows) = lax.optimization_barrier((*blocks, gram_rows))
             for at, block in zip(steps, blocks):
+                if part is not None:
+                    block = lax.dynamic_slice_in_dim(block, part, half, 1)
                 held_rows = lax.dynamic_update_slice(
                     held_rows, block.T, (row, (2 * at + 1) * rows + column)
                 )
@@ -362,14 +361,13 @@
         pair.take(pair_got)
         pair_half = pair.value.reshape(half, rows)
         pair_other = on_chip(pair_half)
-        gram_rows = put_rung(rung_own, 0, here)
         own_got, gram_rows = lax.optimization_barrier((own_got, gram_rows))
         own.take(own_got)
         while len(own.steps) > 1:
             own.take(own.send())
         own_got = own.send()
         gram_rows = after(gram_rows, own.value, *came_second)
-        gram_rows = put_rung(rung_first, 0, there)
+        gram_rows = put_rung(rung_own, 0, here, here)
         pair_other, gram_rows = lax.optimization_barrier((pair_other, gram_rows))
 
         left, right = pair_half[:, :half], pair_half[:, half:]
@@ -387,6 +385,7 @@
             return lax.dynamic_update_slice(held_rows, second, (row, rows + half))
 
         gram_rows = put_pair(0, as_upper)
+        gram_rows = put_rung(rung_first, 0, there)
         own_got, gram_rows = lax.optimization_barrier((own_got, gram_rows))
         own.take(own_got)
         own_rows = own.value.reshape(half, rows)
@@ -394,7 +393,7 @@
         gram_rows = put(own_rows, 0, 0)
         images = [product(gram_rows, whole, half, 0)]
         gram_rows = after(gram_rows, images[0])
-        gram_rows = put_rung(rung_other, half, here)
+        gram_rows = put_rung(rung_own, half, here, there)
         gram_rows = put_pair(half, jnp.logical_not(as_upper))
         gram_rows = put_came(came_first, here)
         gram_rows = put_came(came_second, there)

time: 324 us -> 330 us (1.019)
  waiting for transfers between devices: 139 us -> 144 us
    ppermute x4 -> x3, waiting for transfers between devices: 2.67 us -> 6.92 us  [ring(): return lax.ppermute(value, 'fsdp', pairs)]
  transfers between devices with their start and end apart: 29 -> 28, of which waited for: 19 -> 17; matrix products, arithmetic and copies ran while one was open for 18% -> 18% of each run, Pallas kernels for 10% -> 10%
where the time goes in v5:
time: 330 us; the launch traced here: 328 us
  waiting for transfers between devices  144 us (44%)
  blocking collectives  50.6 us (15%)
  Pallas kernels  39 us (12%)
  local copies, waits for them, and re-layouts  37.6 us (11%)
  starting transfers between devices  28.2 us (9%)
  other arithmetic  18 us (5%)
  matrix products  10.1 us (3%)
    all_to_all x1, blocking collectives, body(): lax.all_to_all(iterate, over, split_axis=1, concat_axis=0, tiled=True)  50.6 us
    ppermute x10, waiting for transfers between devices, swap(): return lax.ppermute(value, axis, [(at, at ^ bit) for at in range(size)])  50.5 us
    ppermute x3, waiting for transfers between devices, begin_sum(): got = lax.ppermute(sent, 'grp', [(at, at ^ bit) for at in range(n_grp)])  45 us
    pallas_call x2, Pallas kernels, add_terms(): pl.pallas_call(kernel(len(rights)), out_shape=jax.ShapeDtypeStruct((rows,...  20.5 us
    ppermute x3, waiting for transfers between devices, from_chip(): return lax.ppermute(value, 'fsdp', pairs)  18.5 us
    all_to_all x2, waiting for transfers between devices, to_rep(): return lax.all_to_all(cut, 'rep', split_axis=0, concat_axis=0, tiled=True)  18 us
    pallas_call x2, Pallas kernels, product(): pl.pallas_call(first_kernel, out_shape=jax.ShapeDtypeStruct((rows, width)...  16.3 us
    dynamic_update_slice x4, local copies, waits for them, and re-layouts, in_order(): lax.dynamic_update_slice(whole, block, (slots[at] * rows + start, 0))  12.2 us
  transfers between devices with their start and end apart: 28, of which 17 were waited for; matrix products, arithmetic and copies ran while one was open for 18% of the time, Pallas kernels for 10%

profile of v5, /device:TPU:0, one launch (start us, length us, event | category | flops | bytes accessed | tf_op | source)
XLA Modules:
  0.0 328.3 jit_solution(5757882827794904593)
XLA Ops:
  1.8 50.6 %all_to_all.29 = bf16[128,8,896]{2,0,1:T(8,128)(2,1)S(1)} all-to-all(bf16[128,8,896]{2,0,1:T(8,128)(2,1)S(1)} %bitcast.112), channel_id=1, replica_groups=mesh['fsdp'=4,'grp'=2,'rep'=4] {'grp','rep'}, dimensions={1} | all-to-all | bytes 3670016 | tf_op jit(solution)/shard_map/all_to_all | solution.py:242
  54.0 2.4 convolution_convert_fusion
  62.5 20.0 %collective-permute-done.1 = bf16[512,1024]{1,0:T(8,128)(2,1)S(1)} collective-permute-done((bf16[512,1024]{1,0:T(8,128)(2,1)S(1)}, bf16[512,1024]{1,0:T(8,128)(2,1)S(1)}, u32[]{:S(2)}, u32[]{:S(2)}) %collective-permute-start.1) | collective-permute-done | bytes 1048608 | tf_op jit(solution)/shard_map/ppermute | solution.py:189
  82.5 12.4 %collective-permute-done = bf16[1024,896]{1,0:T(8,128)(2,1)} collective-permute-done((bf16[1024,896]{1,0:T(8,128)(2,1)S(1)}, bf16[1024,896]{1,0:T(8,128)(2,1)}, u32[]{:S(2)}, u32[]{:S(2)}) %collective-permute-start) | collective-permute-done | bytes 1835040 | tf_op jit(solution)/shard_map/ppermute | solution.py:169
  100.4 3.6 %all-to-all-start.1 = ((bf16[4,192,1024]{2,1,0:T(8,128)(2,1)}), bf16[4,192,1024]{2,1,0:T(8,128)(2,1)S(1)}, u32[]{:S(2)}, u32[]{:S(2)}) async-start(bf16[4,192,1024]{2,1,0:T(8,128)(2,1)} %pad_maximum_fusion), calls=%async_computation.1 | async-start | bytes 3145728 | tf_op jit(solution)/shard_map/all_to_all | solution.py:234
  104.0 3.9 %convert_bitcast_fusion = bf16[1024,1024]{1,0:T(8,128)(2,1)S(1)} fusion(bf16[1024,896]{1,0:T(8,128)(2,1)S(1)} %bitcast.100, bf16[1024,896]{1,0:T(8,128)(2,1)} %collective-permute-done, bf16[1024,896]{1,0:T(8,128)(2,1)} %collective-permute-done.4, pred[]{:T(512)S(6)} %lt.82), kind=kOutput, calls=%fused_computation.1 | convolution fusion | flops 1881014272 | bytes 7602177 | tf_op jit(solution)/shard_map/dot_general | solution.py:24
  108.6 25.0 %collective-permute-done.5 = bf16[512,1024]{1,0:T(8,128)(2,1)S(1)} collective-permute-done((bf16[512,1024]{1,0:T(8,128)(2,1)S(1)}, bf16[512,1024]{1,0:T(8,128)(2,1)S(1)}, u32[]{:S(2)}, u32[]{:S(2)}) %collective-permute-start.5) | collective-permute-done | bytes 1048608 | tf_op jit(solution)/shard_map/ppermute | solution.py:189
  135.0 6.9 %all-to-all-done.1 = bf16[4,192,1024]{2,1,0:T(8,128)(2,1)S(1)} async-done(((bf16[4,192,1024]{2,1,0:T(8,128)(2,1)}), bf16[4,192,1024]{2,1,0:T(8,128)(2,1)S(1)}, u32[]{:S(2)}, u32[]{:S(2)}) %all-to-all-start.1) | async-done | bytes 1572896 | tf_op jit(solution)/shard_map/all_to_all | solution.py:234
  141.8 4.2 %all-to-all-start.2 = ((bf16[4,128,1024]{2,1,0:T(8,128)(2,1)}), bf16[4,128,1024]{2,1,0:T(8,128)(2,1)}, u32[]{:S(2)}, u32[]{:S(2)}) async-start(bf16[4,128,1024]{2,1,0:T(8,128)(2,1)} %bitcast.114), calls=%async_computation.2 | async-start | bytes 2097152 | tf_op jit(solution)/shard_map/all_to_all | solution.py:234
  146.1 3.5 %dynamic_update_slice.48 = bf16[4096,896]{1,0:T(8,128)(2,1)} pad(bf16[1024,896]{1,0:T(8,128)(2,1)S(1)} %bitcast.101, bf16[]{:T(256)} %constant.128.clone.1), padding=0_3072x0_0 | pad | bytes 9175042 | tf_op jit(solution)/shard_map/dynamic_update_slice | solution.py:261
  149.5 2.9 constant_dynamic-update-slice_fusion.5
  152.4 2.9 constant_dynamic-update-slice_fusion.4
  156.3 2.9 constant_dynamic-update-slice_fusion.3.right
  160.9 11.1 %all-to-all-done.2 = bf16[4,128,1024]{2,1,0:T(8,128)(2,1)} async-done(((bf16[4,128,1024]{2,1,0:T(8,128)(2,1)}), bf16[4,128,1024]{2,1,0:T(8,128)(2,1)}, u32[]{:S(2)}, u32[]{:S(2)}) %all-to-all-start.2) | async-done | bytes 1048608 | tf_op jit(solution)/shard_map/all_to_all | solution.py:234
  173.6 12.3 %collective-permute-done.7 = bf16[128,1024]{1,0:T(8,128)(2,1)S(1)} collective-permute-done((bf16[128,1024]{1,0:T(8,128)(2,1)S(1)}, bf16[128,1024]{1,0:T(8,128)(2,1)S(1)}, u32[]{:S(2)}, u32[]{:S(2)}) %collective-permute-start.7) | collective-permute-done | bytes 262176 | tf_op jit(solution)/shard_map/ppermute | solution.py:201
  186.2 3.2 collective-permute-start.8
  189.4 16.2 %collective-permute-done.9 = bf16[2,128,1024]{2,1,0:T(8,128)(2,1)S(1)} collective-permute-done((bf16[2,128,1024]{2,1,0:T(8,128)(2,1)S(1)}, bf16[2,128,1024]{2,1,0:T(8,128)(2,1)S(1)}, u32[]{:S(2)}, u32[]{:S(2)}) %collective-permute-start.9) | collective-permute-done | bytes 524320 | tf_op jit(solution)/shard_map/ppermute | solution.py:201
  210.6 2.3 shard_map.17
  214.4 5.7 %collective-permute-done.12 = bf16[512,512]{1,0:T(8,128)(2,1)} collective-permute-done((bf16[512,512]{1,0:T(8,128)(2,1)}, bf16[512,512]{1,0:T(8,128)(2,1)}, u32[]{:S(2)}, u32[]{:S(2)}) %collective-permute-start.12) | collective-permute-done | bytes 524320 | tf_op jit(solution)/shard_map/ppermute | solution.py:201
  225.1 12.3 %collective-permute-done.10 = bf16[128,1024]{1,0:T(8,128)(2,1)} collective-permute-done((bf16[128,1024]{1,0:T(8,128)(2,1)S(1)}, bf16[128,1024]{1,0:T(8,128)(2,1)}, u32[]{:S(2)}, u32[]{:S(2)}) %collective-permute-start.10) | collective-permute-done | bytes 262176 | tf_op jit(solution)/shard_map/ppermute | solution.py:201
  246.9 6.9 %collective-permute-done.14 = bf16[512,512]{1,0:T(8,128)(2,1)} collective-permute-done((bf16[512,512]{1,0:T(8,128)(2,1)}, bf16[512,512]{1,0:T(8,128)(2,1)}, u32[]{:S(2)}, u32[]{:S(2)}) %collective-permute-start.14) | collective-permute-done | bytes 524320 | tf_op jit(solution)/shard_map/ppermute | solution.py:179
  259.6 2.4 constant_dynamic-update-slice_fusion.1.left
  262.0 8.2 %shard_map.18.refs_0_.refs_7_ = bf16[512,896]{1,0:T(8,128)(2,1)S(1)} custom-call(bf16[1024,4096]{1,0:T(8,128)(2,1)} %constant_dynamic-update-slice_fusion.1.left, bf16[4096,896]{1,0:T(8,128)(2,1)} %constant_dynamic-update-slice_fusion.3.right), custom_call_target="tpu_custom_call" | custom-call | tf_op jit(solution)/shard_map/pallas_call | solution.py:55
  270.1 2.2 collective-permute-start.22
  280.5 2.0 bitcast_dynamic-update-slice_fusion
  283.7 2.4 constant_dynamic-update-slice_fusion.left
  286.1 8.1 %shard_map.19.refs_4_.refs_8_ = bf16[512,896]{1,0:T(8,128)(2,1)S(1)} custom-call(bf16[1024,4096]{1,0:T(8,128)(2,1)} %constant_dynamic-update-slice_fusion.left, bf16[4096,896]{1,0:T(8,128)(2,1)} %constant_dynamic-update-slice_fusion.3.right), custom_call_target="tpu_custom_call" | custom-call | tf_op jit(solution)/shard_map/pallas_call | solution.py:55
  294.9 2.0 collective-permute-done.23.refs_3_
  298.2 13.0 %shard_map.20.refs_2_ = f32[1024,896]{1,0:T(8,128)} custom-call(s32[7]{0:T(128)S(1)} %stack.125.columns, bf16[1024,4096]{1,0:T(8,128)(2,1)} %constant_dynamic-update-slice_fusion.left, bf16[512,896]{1,0:T(8,128)(2,1)S(1)} %shard_map.18.refs_0_.refs_7_, bf16[512,896]{1,0:T(8,128)(2,1)} %collective-permute-done.21.refs_1_, ...), custom_call_target="tpu_custom_call" | custom-call | tf_op jit(solution)/shard_map/pallas_call | solution.py:127
  311.2 6.0 %collective-permute-done.20.refs_0_ = bf16[512,896]{1,0:T(8,128)(2,1)} collective-permute-done((bf16[512,896]{1,0:T(8,128)(2,1)S(1)}, bf16[512,896]{1,0:T(8,128)(2,1)}, u32[]{:S(2)}, u32[]{:S(2)}) %collective-permute-start.20) | collective-permute-done | bytes 917536 | tf_op jit(solution)/shard_map/ppermute | solution.py:169
  317.9 2.1 collective-permute-done.25.refs_1_
  320.9 7.4 %shard_map.21 = bf16[1024,896]{1,0:T(8,128)(2,1)} custom-call(s32[3]{0:T(128)} %pad_add_fusion.columns, bf16[1024,4096]{1,0:T(8,128)(2,1)} %constant_dynamic-update-slice_fusion.left, bf16[512,896]{1,0:T(8,128)(2,1)} %collective-permute-done.20.refs_0_, bf16[512,896]{1,0:T(8,128)(2,1)} %copy-done.9, f32[1024,896]{1,0:T(8,128)} %shard_map.20.refs_2_), custom_call_target="tpu_custom_call" | custom-call | tf_op jit(solution)/shard_map/pallas_call | solution.py:127
  (113 shorter events, 60.9 us)
Async XLA Ops:
  52.4 93.7 %copy-start = (bf16[128,8,896]{2,0,1:T(8,128)(2,1)}, bf16[128,8,896]{2,0,1:T(8,128)(2,1)S(1)}, u32[]{:S(2)}) copy-start(bf16[128,8,896]{2,0,1:T(8,128)(2,1)S(1)} %all_to_all.29) | copy-start | bytes 5505028
  52.4 4.7 %collective-permute-start.2 = (bf16[1024,896]{1,0:T(8,128)(2,1)S(1)}, bf16[1024,896]{1,0:T(8,128)(2,1)}, u32[]{:S(2)}, u32[]{:S(2)}) collective-permute-start(bf16[1024,896]{1,0:T(8,128)(2,1)S(1)} %bitcast.95), channel_id=1, source_target_pairs={{0,8},{8,0},{16,24},{24,16},{1,9},{9,1},{17,25},{25,17},{2,10},{10... | collective-permute-start | bytes 5505032 | tf_op jit(solution)/shard_map/ppermute | solution.py:172
  52.4 42.5 %collective-permute-start = (bf16[1024,896]{1,0:T(8,128)(2,1)S(1)}, bf16[1024,896]{1,0:T(8,128)(2,1)}, u32[]{:S(2)}, u32[]{:S(2)}) collective-permute-start(bf16[1024,896]{1,0:T(8,128)(2,1)S(1)} %bitcast.96), channel_id=1, source_target_pairs={{0,16},{8,24},{16,0},{24,8},{1,17},{9,25},{17,1},{25,9},{2,18},{10... | collective-permute-start | bytes 5505032 | tf_op jit(solution)/shard_map/ppermute | solution.py:169
  56.4 26.1 %collective-permute-start.1 = (bf16[512,1024]{1,0:T(8,128)(2,1)S(1)}, bf16[512,1024]{1,0:T(8,128)(2,1)S(1)}, u32[]{:S(2)}, u32[]{:S(2)}) collective-permute-start(bf16[512,1024]{1,0:T(8,128)(2,1)S(1)} %constant_dynamic-slice_fusion.3), channel_id=1, source_target_pairs={{0,4},{4,0},{1,5},{5,1},{2,6},{6,2},{3,7},{7,3},{8,12},{12,8},{9,1... | collective-permute-start | bytes 3145736 | tf_op jit(solution)/shard_map/ppermute | solution.py:189
  61.0 34.0 %collective-permute-start.3 = (bf16[256,1024]{0,1:T(8,128)(2,1)S(1)}, bf16[256,1024]{0,1:T(8,128)(2,1)S(1)}, u32[]{:S(2)}, u32[]{:S(2)}) collective-permute-start(bf16[256,1024]{0,1:T(8,128)(2,1)S(1)} %fusion.6), channel_id=1, source_target_pairs={{0,4},{4,0},{1,5},{5,1},{2,6},{6,2},{3,7},{7,3},{8,12},{12,8},{9,1... | collective-permute-start | bytes 1572872 | tf_op jit(solution)/shard_map/ppermute | solution.py:189
  82.5 12.4 %copy-start.8 = (bf16[512,1024]{1,0:T(8,128)(2,1)}, bf16[512,1024]{1,0:T(8,128)(2,1)S(1)}, u32[]{:S(2)}) copy-start(bf16[512,1024]{1,0:T(8,128)(2,1)S(1)} %collective-permute-done.1) | copy-start | bytes 3145732
  95.7 8.2 %collective-permute-start.4 = (bf16[1024,896]{1,0:T(8,128)(2,1)}, bf16[1024,896]{1,0:T(8,128)(2,1)}, u32[]{:S(2)}, u32[]{:S(2)}) collective-permute-start(bf16[1024,896]{1,0:T(8,128)(2,1)} %collective-permute-done), channel_id=1, source_target_pairs={{0,8},{8,0},{16,24},{24,16},{1,9},{9,1},{17,25},{25,17},{2,10},{10... | collective-permute-start | bytes 5505032 | tf_op jit(solution)/shard_map/ppermute | solution.py:172
  100.4 41.4 %all-to-all-start.1 = ((bf16[4,192,1024]{2,1,0:T(8,128)(2,1)}), bf16[4,192,1024]{2,1,0:T(8,128)(2,1)S(1)}, u32[]{:S(2)}, u32[]{:S(2)}) async-start(bf16[4,192,1024]{2,1,0:T(8,128)(2,1)} %pad_maximum_fusion), calls=%async_computation.1 | async-start | bytes 3145728 | tf_op jit(solution)/shard_map/all_to_all | solution.py:234
  107.9 25.6 %collective-permute-start.5 = (bf16[512,1024]{1,0:T(8,128)(2,1)S(1)}, bf16[512,1024]{1,0:T(8,128)(2,1)S(1)}, u32[]{:S(2)}, u32[]{:S(2)}) collective-permute-start(bf16[512,1024]{1,0:T(8,128)(2,1)S(1)} %constant_dynamic-slice_fusion.2), channel_id=1, source_target_pairs={{0,4},{4,0},{1,5},{5,1},{2,6},{6,2},{3,7},{7,3},{8,12},{12,8},{9,1... | collective-permute-start | bytes 3145736 | tf_op jit(solution)/shard_map/ppermute | solution.py:189
  141.8 30.2 %all-to-all-start.2 = ((bf16[4,128,1024]{2,1,0:T(8,128)(2,1)}), bf16[4,128,1024]{2,1,0:T(8,128)(2,1)}, u32[]{:S(2)}, u32[]{:S(2)}) async-start(bf16[4,128,1024]{2,1,0:T(8,128)(2,1)} %bitcast.114), calls=%async_computation.2 | async-start | bytes 2097152 | tf_op jit(solution)/shard_map/all_to_all | solution.py:234
  155.7 30.4 %copy-start.5 = (bf16[192,1024]{1,0:T(8,128)(2,1)}, bf16[192,1024]{1,0:T(8,128)(2,1)S(1)}, u32[]{:S(2)}) copy-start(bf16[192,1024]{1,0:T(8,128)(2,1)S(1)} %reduce_sum.24) | copy-start | bytes 1179652
  155.7 5.2 %collective-permute-start.6 = (bf16[64,1024]{1,0:T(8,128)(2,1)S(1)}, bf16[64,1024]{1,0:T(8,128)(2,1)S(1)}, u32[]{:S(2)}, u32[]{:S(2)}) collective-permute-start(bf16[64,1024]{1,0:T(8,128)(2,1)S(1)} %slice.39), channel_id=1, source_target_pairs={{0,4},{4,0},{1,5},{5,1},{2,6},{6,2},{3,7},{7,3},{8,12},{12,8},{9,1... | collective-permute-start | bytes 393224 | tf_op jit(solution)/shard_map/ppermute | solution.py:201
  173.5 12.4 %collective-permute-start.7 = (bf16[128,1024]{1,0:T(8,128)(2,1)S(1)}, bf16[128,1024]{1,0:T(8,128)(2,1)S(1)}, u32[]{:S(2)}, u32[]{:S(2)}) collective-permute-start(bf16[128,1024]{1,0:T(8,128)(2,1)S(1)} %reduce_sum.25), channel_id=1, source_target_pairs={{0,2},{1,3},{2,0},{3,1},{4,6},{5,7},{6,4},{7,5},{8,10},{9,11},{10,... | collective-permute-start | bytes 786440 | tf_op jit(solution)/shard_map/ppermute | solution.py:201
  186.0 19.5 %collective-permute-start.9 = (bf16[2,128,1024]{2,1,0:T(8,128)(2,1)S(1)}, bf16[2,128,1024]{2,1,0:T(8,128)(2,1)S(1)}, u32[]{:S(2)}, u32[]{:S(2)}) collective-permute-start(bf16[2,128,1024]{2,1,0:T(8,128)(2,1)S(1)} %pad_maximum_fusion.4), channel_id=1, source_target_pairs={{0,1},{1,0},{2,3},{3,2},{4,5},{5,4},{6,7},{7,6},{8,9},{9,8},{10,11... | collective-permute-start | bytes 1572872 | tf_op jit(solution)/shard_map/ppermute | solution.py:201
  186.2 19.6 %collective-permute-start.8 = (bf16[2,64,1024]{2,1,0:T(8,128)(2,1)S(1)}, bf16[2,64,1024]{2,1,0:T(8,128)(2,1)S(1)}, u32[]{:S(2)}, u32[]{:S(2)}) collective-permute-start(bf16[2,64,1024]{2,1,0:T(8,128)(2,1)S(1)} %pad_maximum_fusion.7), channel_id=1, source_target_pairs={{0,2},{1,3},{2,0},{3,1},{4,6},{5,7},{6,4},{7,5},{8,10},{9,11},{10,... | collective-permute-start | bytes 786440 | tf_op jit(solution)/shard_map/ppermute | solution.py:201
  206.7 13.3 %collective-permute-start.12 = (bf16[512,512]{1,0:T(8,128)(2,1)}, bf16[512,512]{1,0:T(8,128)(2,1)}, u32[]{:S(2)}, u32[]{:S(2)}) collective-permute-start(bf16[512,512]{1,0:T(8,128)(2,1)} %constant_dynamic-slice_fusion.1), channel_id=1, source_target_pairs={{0,4},{4,0},{1,5},{5,1},{2,6},{6,2},{3,7},{7,3},{8,12},{12,8},{9,1... | collective-permute-start | bytes 1572872 | tf_op jit(solution)/shard_map/ppermute | solution.py:201
  208.2 12.9 %collective-permute-start.11 = (bf16[2,2,64,1024]{3,2,0,1:T(8,128)(2,1)}, bf16[2,2,64,1024]{3,2,0,1:T(8,128)(2,1)S(1)}, u32[]{:S(2)}, u32[]{:S(2)}) collective-permute-start(bf16[2,2,64,1024]{3,2,0,1:T(8,128)(2,1)} %pad_maximum_fusion.5), channel_id=1, source_target_pairs={{0,1},{1,0},{2,3},{3,2},{4,5},{5,4},{6,7},{7,6},{8,9},{9,8},{10,11... | collective-permute-start | bytes 1572872 | tf_op jit(solution)/shard_map/ppermute | solution.py:201
  212.9 27.9 %collective-permute-start.16 = (bf16[512,1024]{0,1:T(8,128)(2,1)}, bf16[512,1024]{0,1:T(8,128)(2,1)}, u32[]{:S(2)}, u32[]{:S(2)}) collective-permute-start(bf16[512,1024]{0,1:T(8,128)(2,1)} %copy.17), channel_id=1, source_target_pairs={{0,16},{16,8},{8,24},{24,0},{1,17},{17,9},{9,25},{25,1},{2,18},{18... | collective-permute-start | bytes 3145736 | tf_op jit(solution)/shard_map/ppermute | solution.py:179
  221.4 24.4 %copy-start.3 = (bf16[2,2,2,64,1024]{4,3,2,1,0:T(8,128)(2,1)}, bf16[2,2,2,64,1024]{4,3,2,1,0:T(8,128)(2,1)S(1)}, u32[]{:S(2)}) copy-start(bf16[2,2,2,64,1024]{4,3,2,1,0:T(8,128)(2,1)S(1)} %copy.16) | copy-start | bytes 3145732
  221.4 21.5 %collective-permute-start.15 = (bf16[512,1024]{1,0:T(8,128)(2,1)S(1)}, bf16[512,1024]{1,0:T(8,128)(2,1)}, u32[]{:S(2)}, u32[]{:S(2)}) collective-permute-start(bf16[512,1024]{1,0:T(8,128)(2,1)S(1)} %bitcast.107), channel_id=1, source_target_pairs={{0,8},{8,0},{16,24},{24,16},{1,9},{9,1},{17,25},{25,17},{2,10},{10... | collective-permute-start | bytes 3145736 | tf_op jit(solution)/shard_map/ppermute | solution.py:172
  222.1 15.4 %collective-permute-start.10 = (bf16[128,1024]{1,0:T(8,128)(2,1)S(1)}, bf16[128,1024]{1,0:T(8,128)(2,1)}, u32[]{:S(2)}, u32[]{:S(2)}) collective-permute-start(bf16[128,1024]{1,0:T(8,128)(2,1)S(1)} %slice.38), channel_id=1, source_target_pairs={{0,2},{1,3},{2,0},{3,1},{4,6},{5,7},{6,4},{7,5},{8,10},{9,11},{10,... | collective-permute-start | bytes 786440 | tf_op jit(solution)/shard_map/ppermute | solution.py:201
  223.6 17.2 %collective-permute-start.17 = (bf16[512,512]{0,1:T(8,128)(2,1)S(1)}, bf16[512,512]{0,1:T(8,128)(2,1)}, u32[]{:S(2)}, u32[]{:S(2)}) collective-permute-start(bf16[512,512]{0,1:T(8,128)(2,1)S(1)} %constant_dynamic-slice_fusion), channel_id=1, source_target_pairs={{0,4},{4,0},{1,5},{5,1},{2,6},{6,2},{3,7},{7,3},{8,12},{12,8},{9,1... | collective-permute-start | bytes 1572872 | tf_op jit(solution)/shard_map/ppermute | solution.py:201
  239.3 16.6 %collective-permute-start.13 = (bf16[2,128,1024]{2,1,0:T(8,128)(2,1)}, bf16[2,128,1024]{2,1,0:T(8,128)(2,1)}, u32[]{:S(2)}, u32[]{:S(2)}) collective-permute-start(bf16[2,128,1024]{2,1,0:T(8,128)(2,1)} %pad_maximum_fusion.6), channel_id=1, source_target_pairs={{0,1},{1,0},{2,3},{3,2},{4,5},{5,4},{6,7},{7,6},{8,9},{9,8},{10,11... | collective-permute-start | bytes 1572872 | tf_op jit(solution)/shard_map/ppermute | solution.py:201
  239.3 14.5 %collective-permute-start.14 = (bf16[512,512]{1,0:T(8,128)(2,1)}, bf16[512,512]{1,0:T(8,128)(2,1)}, u32[]{:S(2)}, u32[]{:S(2)}) collective-permute-start(bf16[512,512]{1,0:T(8,128)(2,1)} %collective-permute-done.12), channel_id=1, source_target_pairs={{0,16},{16,8},{8,24},{24,0},{1,17},{17,9},{9,25},{25,1},{2,18},{18... | collective-permute-start | bytes 1572872 | tf_op jit(solution)/shard_map/ppermute | solution.py:179
  240.8 39.7 %collective-permute-start.19 = (bf16[512,512]{0,1:T(8,128)(2,1)}, bf16[512,512]{0,1:T(8,128)(2,1)}, u32[]{:S(2)}, u32[]{:S(2)}) collective-permute-start(bf16[512,512]{0,1:T(8,128)(2,1)} %collective-permute-done.17), channel_id=1, source_target_pairs={{0,16},{16,8},{8,24},{24,0},{1,17},{17,9},{9,25},{25,1},{2,18},{18... | collective-permute-start | bytes 1572872 | tf_op jit(solution)/shard_map/ppermute | solution.py:179
  258.2 25.6 %collective-permute-start.18 = (bf16[512,1024]{1,0:T(8,128)(2,1)}, bf16[512,1024]{1,0:T(8,128)(2,1)}, u32[]{:S(2)}, u32[]{:S(2)}) collective-permute-start(bf16[512,1024]{1,0:T(8,128)(2,1)} %bitcast.32), channel_id=1, source_target_pairs={{0,4},{4,0},{1,5},{5,1},{2,6},{6,2},{3,7},{7,3},{8,12},{12,8},{9,1... | collective-permute-start | bytes 3145736 | tf_op jit(solution)/shard_map/ppermute | solution.py:201
  270.1 24.1 %collective-permute-start.22 = (bf16[512,896]{1,0:T(8,128)(2,1)S(1)}, bf16[512,896]{1,0:T(8,128)(2,1)S(1)}, u32[]{:S(2)}, u32[]{:S(2)}) collective-permute-start(bf16[512,896]{1,0:T(8,128)(2,1)S(1)} %shard_map.18.refs_0_.refs_7_), channel_id=1, source_target_pairs={{0,16},{8,24},{16,0},{24,8},{1,17},{9,25},{17,1},{25,9},{2,18},{10... | collective-permute-start | bytes 2752520 | tf_op jit(solution)/shard_map/ppermute | solution.py:169
  272.3 22.6 %collective-permute-start.21 = (bf16[512,896]{1,0:T(8,128)(2,1)S(1)}, bf16[512,896]{1,0:T(8,128)(2,1)}, u32[]{:S(2)}, u32[]{:S(2)}) collective-permute-start(bf16[512,896]{1,0:T(8,128)(2,1)S(1)} %shard_map.18.refs_0_.refs_7_), channel_id=1, source_target_pairs={{0,8},{8,0},{16,24},{24,16},{1,9},{9,1},{17,25},{25,17},{2,10},{10... | collective-permute-start | bytes 2752520 | tf_op jit(solution)/shard_map/ppermute | solution.py:172
  294.2 2.7 collective-permute-start.23
  294.3 3.9 %collective-permute-start.24 = (bf16[512,896]{1,0:T(8,128)(2,1)S(1)}, bf16[512,896]{1,0:T(8,128)(2,1)}, u32[]{:S(2)}, u32[]{:S(2)}) collective-permute-start(bf16[512,896]{1,0:T(8,128)(2,1)S(1)} %shard_map.19.refs_4_.refs_8_), channel_id=1, source_target_pairs={{0,8},{8,0},{16,24},{24,16},{1,9},{9,1},{17,25},{25,17},{2,10},{10... | collective-permute-start | bytes 2752520 | tf_op jit(solution)/shard_map/ppermute | solution.py:172
  294.8 22.4 %collective-permute-start.20 = (bf16[512,896]{1,0:T(8,128)(2,1)S(1)}, bf16[512,896]{1,0:T(8,128)(2,1)}, u32[]{:S(2)}, u32[]{:S(2)}) collective-permute-start(bf16[512,896]{1,0:T(8,128)(2,1)S(1)} %shard_map.19.refs_4_.refs_8_), channel_id=1, source_target_pairs={{0,16},{8,24},{16,0},{24,8},{1,17},{9,25},{17,1},{25,9},{2,18},{10... | collective-permute-start | bytes 2752520 | tf_op jit(solution)/shard_map/ppermute | solution.py:169
  317.2 2.7 collective-permute-start.25
  (7 other events, 40.7 us)

commit v6 on v4

--- a/solution.py
+++ b/solution.py
@@ -357,19 +357,18 @@
                 )
             return held_rows
 
-        gram_rows = after(gram_rows, *came_first)
-        pair_got, gram_rows = lax.optimization_barrier((pair_got, gram_rows))
+        pair_got, own_got, gram_rows, *_ = lax.optimization_barrier(
+            (pair_got, own_got, gram_rows, *came_first, *rung_own)
+        )
         pair.take(pair_got)
         pair_half = pair.value.reshape(half, rows)
         pair_other = on_chip(pair_half)
-        gram_rows = put_rung(rung_own, 0, here)
-        own_got, gram_rows = lax.optimization_barrier((own_got, gram_rows))
         own.take(own_got)
         while len(own.steps) > 1:
             own.take(own.send())
         own_got = own.send()
-        gram_rows = after(gram_rows, own.value, *came_second)
-        gram_rows = put_rung(rung_first, 0, there)
+        gram_rows = after(gram_rows, own.value)
+        gram_rows = put_rung(rung_own, 0, here)
         pair_other, gram_rows = lax.optimization_barrier((pair_other, gram_rows))
 
         left, right = pair_half[:, :half], pair_half[:, half:]
@@ -387,6 +386,8 @@
             return lax.dynamic_update_slice(held_rows, second, (row, rows + half))
 
         gram_rows = put_pair(0, as_upper)
+        gram_rows = after(gram_rows, *came_second)
+        gram_rows = put_rung(rung_first, 0, there)
         own_got, gram_rows = lax.optimization_barrier((own_got, gram_rows))
         own.take(own_got)
         own_rows = own.value.reshape(half, rows)

time: 324 us -> 338 us (1.043)
  waiting for transfers between devices: 139 us -> 148 us
    ppermute x4, waiting for transfers between devices: 2.67 us -> 11 us  [ring(): return lax.ppermute(value, 'fsdp', pairs)]
  transfers between devices with their start and end apart: 29 -> 29, of which waited for: 19 -> 17; matrix products, arithmetic and copies ran while one was open for 18% -> 18% of each run, Pallas kernels for 10% -> 9%
where the time goes in v6:
time: 338 us; the launch traced here: 337 us
  waiting for transfers between devices  148 us (44%)
  blocking collectives  50.6 us (15%)
  Pallas kernels  39.1 us (12%)
  local copies, waits for them, and re-layouts  38.3 us (11%)
  starting transfers between devices  32.7 us (10%)
  other arithmetic  17.9 us (5%)
  matrix products  10.1 us (3%)
    all_to_all x1, blocking collectives, body(): lax.all_to_all(iterate, over, split_axis=1, concat_axis=0, tiled=True)  50.6 us
    ppermute x10, waiting for transfers between devices, swap(): return lax.ppermute(value, axis, [(at, at ^ bit) for at in range(size)])  49.9 us
    ppermute x3, waiting for transfers between devices, begin_sum(): got = lax.ppermute(sent, 'grp', [(at, at ^ bit) for at in range(n_grp)])  45 us
    pallas_call x2, Pallas kernels, add_terms(): pl.pallas_call(kernel(len(rights)), out_shape=jax.ShapeDtypeStruct((rows,...  20.5 us
    ppermute x3, waiting for transfers between devices, from_chip(): return lax.ppermute(value, 'fsdp', pairs)  18.4 us
    all_to_all x2, waiting for transfers between devices, to_rep(): return lax.all_to_all(cut, 'rep', split_axis=0, concat_axis=0, tiled=True)  18 us
    pallas_call x2, Pallas kernels, product(): pl.pallas_call(first_kernel, out_shape=jax.ShapeDtypeStruct((rows, width)...  16.3 us
    dynamic_update_slice x4, local copies, waits for them, and re-layouts, in_order(): lax.dynamic_update_slice(whole, block, (slots[at] * rows + start, 0))  12.1 us
  transfers between devices with their start and end apart: 29, of which 17 were waited for; matrix products, arithmetic and copies ran while one was open for 18% of the time, Pallas kernels for 9%

profile of v6, /device:TPU:0, one launch (start us, length us, event | category | flops | bytes accessed | tf_op | source)
XLA Modules:
  0.0 337.0 jit_solution(16168555694707837171)
XLA Ops:
  1.8 50.6 %all_to_all.29 = bf16[128,8,896]{2,0,1:T(8,128)(2,1)S(1)} all-to-all(bf16[128,8,896]{2,0,1:T(8,128)(2,1)S(1)} %bitcast.111), channel_id=1, replica_groups=mesh['fsdp'=4,'grp'=2,'rep'=4] {'grp','rep'}, dimensions={1} | all-to-all | bytes 3670016 | tf_op jit(solution)/shard_map/all_to_all | solution.py:242
  54.0 2.4 convolution_convert_fusion
  62.5 20.0 %collective-permute-done.1 = bf16[512,1024]{1,0:T(8,128)(2,1)S(1)} collective-permute-done((bf16[512,1024]{1,0:T(8,128)(2,1)S(1)}, bf16[512,1024]{1,0:T(8,128)(2,1)S(1)}, u32[]{:S(2)}, u32[]{:S(2)}) %collective-permute-start.1) | collective-permute-done | bytes 1048608 | tf_op jit(solution)/shard_map/ppermute | solution.py:189
  82.5 12.4 %collective-permute-done = bf16[1024,896]{1,0:T(8,128)(2,1)} collective-permute-done((bf16[1024,896]{1,0:T(8,128)(2,1)S(1)}, bf16[1024,896]{1,0:T(8,128)(2,1)}, u32[]{:S(2)}, u32[]{:S(2)}) %collective-permute-start) | collective-permute-done | bytes 1835040 | tf_op jit(solution)/shard_map/ppermute | solution.py:169
  100.4 3.6 %all-to-all-start.1 = ((bf16[4,192,1024]{2,1,0:T(8,128)(2,1)}), bf16[4,192,1024]{2,1,0:T(8,128)(2,1)S(1)}, u32[]{:S(2)}, u32[]{:S(2)}) async-start(bf16[4,192,1024]{2,1,0:T(8,128)(2,1)} %pad_maximum_fusion), calls=%async_computation.1 | async-start | bytes 3145728 | tf_op jit(solution)/shard_map/all_to_all | solution.py:234
  104.0 3.9 %convert_bitcast_fusion = bf16[1024,1024]{1,0:T(8,128)(2,1)S(1)} fusion(bf16[1024,896]{1,0:T(8,128)(2,1)S(1)} %bitcast.100, bf16[1024,896]{1,0:T(8,128)(2,1)} %collective-permute-done, bf16[1024,896]{1,0:T(8,128)(2,1)} %collective-permute-done.4, pred[]{:T(512)S(6)} %lt.82), kind=kOutput, calls=%fused_computation.1 | convolution fusion | flops 1881014272 | bytes 7602177 | tf_op jit(solution)/shard_map/dot_general | solution.py:24
  108.6 25.0 %collective-permute-done.5 = bf16[512,1024]{1,0:T(8,128)(2,1)S(1)} collective-permute-done((bf16[512,1024]{1,0:T(8,128)(2,1)S(1)}, bf16[512,1024]{1,0:T(8,128)(2,1)S(1)}, u32[]{:S(2)}, u32[]{:S(2)}) %collective-permute-start.5) | collective-permute-done | bytes 1048608 | tf_op jit(solution)/shard_map/ppermute | solution.py:189
  134.9 6.9 %all-to-all-done.1 = bf16[4,192,1024]{2,1,0:T(8,128)(2,1)S(1)} async-done(((bf16[4,192,1024]{2,1,0:T(8,128)(2,1)}), bf16[4,192,1024]{2,1,0:T(8,128)(2,1)S(1)}, u32[]{:S(2)}, u32[]{:S(2)}) %all-to-all-start.1) | async-done | bytes 1572896 | tf_op jit(solution)/shard_map/all_to_all | solution.py:234
  141.8 4.2 %all-to-all-start.2 = ((bf16[4,128,1024]{2,1,0:T(8,128)(2,1)}), bf16[4,128,1024]{2,1,0:T(8,128)(2,1)}, u32[]{:S(2)}, u32[]{:S(2)}) async-start(bf16[4,128,1024]{2,1,0:T(8,128)(2,1)} %bitcast.113), calls=%async_computation.2 | async-start | bytes 2097152 | tf_op jit(solution)/shard_map/all_to_all | solution.py:234
  146.1 3.5 %dynamic_update_slice.48 = bf16[4096,896]{1,0:T(8,128)(2,1)} pad(bf16[1024,896]{1,0:T(8,128)(2,1)S(1)} %bitcast.101, bf16[]{:T(256)} %constant.128.clone.1), padding=0_3072x0_0 | pad | bytes 9175042 | tf_op jit(solution)/shard_map/dynamic_update_slice | solution.py:261
  149.5 2.9 constant_dynamic-update-slice_fusion.5
  152.4 2.9 constant_dynamic-update-slice_fusion.4
  156.3 2.9 constant_dynamic-update-slice_fusion.3.right
  160.9 11.2 %all-to-all-done.2 = bf16[4,128,1024]{2,1,0:T(8,128)(2,1)} async-done(((bf16[4,128,1024]{2,1,0:T(8,128)(2,1)}), bf16[4,128,1024]{2,1,0:T(8,128)(2,1)}, u32[]{:S(2)}, u32[]{:S(2)}) %all-to-all-start.2) | async-done | bytes 1048608 | tf_op jit(solution)/shard_map/all_to_all | solution.py:234
  173.6 12.3 %collective-permute-done.7 = bf16[128,1024]{1,0:T(8,128)(2,1)S(1)} collective-permute-done((bf16[128,1024]{1,0:T(8,128)(2,1)S(1)}, bf16[128,1024]{1,0:T(8,128)(2,1)S(1)}, u32[]{:S(2)}, u32[]{:S(2)}) %collective-permute-start.7) | collective-permute-done | bytes 262176 | tf_op jit(solution)/shard_map/ppermute | solution.py:201
  186.2 3.2 collective-permute-start.8
  189.4 16.2 %collective-permute-done.9 = bf16[2,128,1024]{2,1,0:T(8,128)(2,1)S(1)} collective-permute-done((bf16[2,128,1024]{2,1,0:T(8,128)(2,1)S(1)}, bf16[2,128,1024]{2,1,0:T(8,128)(2,1)S(1)}, u32[]{:S(2)}, u32[]{:S(2)}) %collective-permute-start.9) | collective-permute-done | bytes 524320 | tf_op jit(solution)/shard_map/ppermute | solution.py:201
  211.9 2.2 collective-permute-start.11
  214.1 2.3 shard_map.17
  216.4 11.5 %collective-permute-done.11 = bf16[128,1024]{1,0:T(8,128)(2,1)S(1)} collective-permute-done((bf16[128,1024]{1,0:T(8,128)(2,1)S(1)}, bf16[128,1024]{1,0:T(8,128)(2,1)S(1)}, u32[]{:S(2)}, u32[]{:S(2)}) %collective-permute-start.11) | collective-permute-done | bytes 262176 | tf_op jit(solution)/shard_map/ppermute | solution.py:201
  236.3 2.1 collective-permute-start.20
  240.3 5.0 %collective-permute-done.17 = bf16[512,512]{0,1:T(8,128)(2,1)} collective-permute-done((bf16[512,512]{0,1:T(8,128)(2,1)S(1)}, bf16[512,512]{0,1:T(8,128)(2,1)}, u32[]{:S(2)}, u32[]{:S(2)}) %collective-permute-start.17) | collective-permute-done | bytes 524320 | tf_op jit(solution)/shard_map/ppermute | solution.py:201
  251.2 11.0 %collective-permute-done.15 = bf16[512,512]{1,0:T(8,128)(2,1)} collective-permute-done((bf16[512,512]{1,0:T(8,128)(2,1)}, bf16[512,512]{1,0:T(8,128)(2,1)}, u32[]{:S(2)}, u32[]{:S(2)}) %collective-permute-start.15) | collective-permute-done | bytes 524320 | tf_op jit(solution)/shard_map/ppermute | solution.py:179
  267.1 2.3 constant_dynamic-update-slice_fusion.1.left
  269.5 8.2 %shard_map.18.refs_0_.refs_7_ = bf16[512,896]{1,0:T(8,128)(2,1)S(1)} custom-call(bf16[1024,4096]{1,0:T(8,128)(2,1)} %constant_dynamic-update-slice_fusion.1.left, bf16[4096,896]{1,0:T(8,128)(2,1)} %constant_dynamic-update-slice_fusion.3.right), custom_call_target="tpu_custom_call" | custom-call | tf_op jit(solution)/shard_map/pallas_call | solution.py:55
  277.7 2.5 collective-permute-start.23
  292.5 2.4 constant_dynamic-update-slice_fusion.left
  294.9 8.1 %shard_map.19.refs_4_.refs_8_ = bf16[512,896]{1,0:T(8,128)(2,1)S(1)} custom-call(bf16[1024,4096]{1,0:T(8,128)(2,1)} %constant_dynamic-update-slice_fusion.left, bf16[4096,896]{1,0:T(8,128)(2,1)} %constant_dynamic-update-slice_fusion.3.right), custom_call_target="tpu_custom_call" | custom-call | tf_op jit(solution)/shard_map/pallas_call | solution.py:55
  306.9 13.0 %shard_map.20.refs_2_ = f32[1024,896]{1,0:T(8,128)} custom-call(s32[7]{0:T(128)S(1)} %stack.125.columns, bf16[1024,4096]{1,0:T(8,128)(2,1)} %constant_dynamic-update-slice_fusion.left, bf16[512,896]{1,0:T(8,128)(2,1)S(1)} %shard_map.18.refs_0_.refs_7_, bf16[512,896]{1,0:T(8,128)(2,1)} %collective-permute-done.22.refs_1_, ...), custom_call_target="tpu_custom_call" | custom-call | tf_op jit(solution)/shard_map/pallas_call | solution.py:127
  320.0 6.0 %collective-permute-done.21.refs_0_ = bf16[512,896]{1,0:T(8,128)(2,1)} collective-permute-done((bf16[512,896]{1,0:T(8,128)(2,1)S(1)}, bf16[512,896]{1,0:T(8,128)(2,1)}, u32[]{:S(2)}, u32[]{:S(2)}) %collective-permute-start.21) | collective-permute-done | bytes 917536 | tf_op jit(solution)/shard_map/ppermute | solution.py:169
  326.6 2.1 collective-permute-done.26.refs_1_
  329.6 7.5 %shard_map.21 = bf16[1024,896]{1,0:T(8,128)(2,1)} custom-call(s32[3]{0:T(128)} %pad_add_fusion.columns, bf16[1024,4096]{1,0:T(8,128)(2,1)} %constant_dynamic-update-slice_fusion.left, bf16[512,896]{1,0:T(8,128)(2,1)} %collective-permute-done.21.refs_0_, bf16[512,896]{1,0:T(8,128)(2,1)} %copy-done.7, f32[1024,896]{1,0:T(8,128)} %shard_map.20.refs_2_), custom_call_target="tpu_custom_call" | custom-call | tf_op jit(solution)/shard_map/pallas_call | solution.py:127
  (113 shorter events, 66.3 us)
Async XLA Ops:
  52.4 93.7 %copy-start = (bf16[128,8,896]{2,0,1:T(8,128)(2,1)}, bf16[128,8,896]{2,0,1:T(8,128)(2,1)S(1)}, u32[]{:S(2)}) copy-start(bf16[128,8,896]{2,0,1:T(8,128)(2,1)S(1)} %all_to_all.29) | copy-start | bytes 5505028
  52.4 4.7 %collective-permute-start.2 = (bf16[1024,896]{1,0:T(8,128)(2,1)S(1)}, bf16[1024,896]{1,0:T(8,128)(2,1)}, u32[]{:S(2)}, u32[]{:S(2)}) collective-permute-start(bf16[1024,896]{1,0:T(8,128)(2,1)S(1)} %bitcast.95), channel_id=1, source_target_pairs={{0,8},{8,0},{16,24},{24,16},{1,9},{9,1},{17,25},{25,17},{2,10},{10... | collective-permute-start | bytes 5505032 | tf_op jit(solution)/shard_map/ppermute | solution.py:172
  52.4 42.5 %collective-permute-start = (bf16[1024,896]{1,0:T(8,128)(2,1)S(1)}, bf16[1024,896]{1,0:T(8,128)(2,1)}, u32[]{:S(2)}, u32[]{:S(2)}) collective-permute-start(bf16[1024,896]{1,0:T(8,128)(2,1)S(1)} %bitcast.96), channel_id=1, source_target_pairs={{0,16},{8,24},{16,0},{24,8},{1,17},{9,25},{17,1},{25,9},{2,18},{10... | collective-permute-start | bytes 5505032 | tf_op jit(solution)/shard_map/ppermute | solution.py:169
  56.4 26.1 %collective-permute-start.1 = (bf16[512,1024]{1,0:T(8,128)(2,1)S(1)}, bf16[512,1024]{1,0:T(8,128)(2,1)S(1)}, u32[]{:S(2)}, u32[]{:S(2)}) collective-permute-start(bf16[512,1024]{1,0:T(8,128)(2,1)S(1)} %constant_dynamic-slice_fusion.5), channel_id=1, source_target_pairs={{0,4},{4,0},{1,5},{5,1},{2,6},{6,2},{3,7},{7,3},{8,12},{12,8},{9,1... | collective-permute-start | bytes 3145736 | tf_op jit(solution)/shard_map/ppermute | solution.py:189
  61.0 34.0 %collective-permute-start.3 = (bf16[256,1024]{0,1:T(8,128)(2,1)S(1)}, bf16[256,1024]{0,1:T(8,128)(2,1)S(1)}, u32[]{:S(2)}, u32[]{:S(2)}) collective-permute-start(bf16[256,1024]{0,1:T(8,128)(2,1)S(1)} %fusion.6), channel_id=1, source_target_pairs={{0,4},{4,0},{1,5},{5,1},{2,6},{6,2},{3,7},{7,3},{8,12},{12,8},{9,1... | collective-permute-start | bytes 1572872 | tf_op jit(solution)/shard_map/ppermute | solution.py:189
  95.7 8.2 %collective-permute-start.4 = (bf16[1024,896]{1,0:T(8,128)(2,1)}, bf16[1024,896]{1,0:T(8,128)(2,1)}, u32[]{:S(2)}, u32[]{:S(2)}) collective-permute-start(bf16[1024,896]{1,0:T(8,128)(2,1)} %collective-permute-done), channel_id=1, source_target_pairs={{0,8},{8,0},{16,24},{24,16},{1,9},{9,1},{17,25},{25,17},{2,10},{10... | collective-permute-start | bytes 5505032 | tf_op jit(solution)/shard_map/ppermute | solution.py:172
  100.4 41.4 %all-to-all-start.1 = ((bf16[4,192,1024]{2,1,0:T(8,128)(2,1)}), bf16[4,192,1024]{2,1,0:T(8,128)(2,1)S(1)}, u32[]{:S(2)}, u32[]{:S(2)}) async-start(bf16[4,192,1024]{2,1,0:T(8,128)(2,1)} %pad_maximum_fusion), calls=%async_computation.1 | async-start | bytes 3145728 | tf_op jit(solution)/shard_map/all_to_all | solution.py:234
  107.9 25.6 %collective-permute-start.5 = (bf16[512,1024]{1,0:T(8,128)(2,1)S(1)}, bf16[512,1024]{1,0:T(8,128)(2,1)S(1)}, u32[]{:S(2)}, u32[]{:S(2)}) collective-permute-start(bf16[512,1024]{1,0:T(8,128)(2,1)S(1)} %constant_dynamic-slice_fusion.4), channel_id=1, source_target_pairs={{0,4},{4,0},{1,5},{5,1},{2,6},{6,2},{3,7},{7,3},{8,12},{12,8},{9,1... | collective-permute-start | bytes 3145736 | tf_op jit(solution)/shard_map/ppermute | solution.py:189
  141.8 30.2 %all-to-all-start.2 = ((bf16[4,128,1024]{2,1,0:T(8,128)(2,1)}), bf16[4,128,1024]{2,1,0:T(8,128)(2,1)}, u32[]{:S(2)}, u32[]{:S(2)}) async-start(bf16[4,128,1024]{2,1,0:T(8,128)(2,1)} %bitcast.113), calls=%async_computation.2 | async-start | bytes 2097152 | tf_op jit(solution)/shard_map/all_to_all | solution.py:234
  155.7 5.2 %collective-permute-start.6 = (bf16[64,1024]{1,0:T(8,128)(2,1)S(1)}, bf16[64,1024]{1,0:T(8,128)(2,1)S(1)}, u32[]{:S(2)}, u32[]{:S(2)}) collective-permute-start(bf16[64,1024]{1,0:T(8,128)(2,1)S(1)} %slice.39), channel_id=1, source_target_pairs={{0,4},{4,0},{1,5},{5,1},{2,6},{6,2},{3,7},{7,3},{8,12},{12,8},{9,1... | collective-permute-start | bytes 393224 | tf_op jit(solution)/shard_map/ppermute | solution.py:201
  173.4 12.4 %collective-permute-start.7 = (bf16[128,1024]{1,0:T(8,128)(2,1)S(1)}, bf16[128,1024]{1,0:T(8,128)(2,1)S(1)}, u32[]{:S(2)}, u32[]{:S(2)}) collective-permute-start(bf16[128,1024]{1,0:T(8,128)(2,1)S(1)} %reduce_sum.25), channel_id=1, source_target_pairs={{0,2},{1,3},{2,0},{3,1},{4,6},{5,7},{6,4},{7,5},{8,10},{9,11},{10,... | collective-permute-start | bytes 786440 | tf_op jit(solution)/shard_map/ppermute | solution.py:201
  186.0 19.5 %collective-permute-start.9 = (bf16[2,128,1024]{2,1,0:T(8,128)(2,1)S(1)}, bf16[2,128,1024]{2,1,0:T(8,128)(2,1)S(1)}, u32[]{:S(2)}, u32[]{:S(2)}) collective-permute-start(bf16[2,128,1024]{2,1,0:T(8,128)(2,1)S(1)} %pad_maximum_fusion.4), channel_id=1, source_target_pairs={{0,1},{1,0},{2,3},{3,2},{4,5},{5,4},{6,7},{7,6},{8,9},{9,8},{10,11... | collective-permute-start | bytes 1572872 | tf_op jit(solution)/shard_map/ppermute | solution.py:201
  186.2 19.6 %collective-permute-start.8 = (bf16[2,64,1024]{2,1,0:T(8,128)(2,1)S(1)}, bf16[2,64,1024]{2,1,0:T(8,128)(2,1)S(1)}, u32[]{:S(2)}, u32[]{:S(2)}) collective-permute-start(bf16[2,64,1024]{2,1,0:T(8,128)(2,1)S(1)} %pad_maximum_fusion.7), channel_id=1, source_target_pairs={{0,2},{1,3},{2,0},{3,1},{4,6},{5,7},{6,4},{7,5},{8,10},{9,11},{10,... | collective-permute-start | bytes 786440 | tf_op jit(solution)/shard_map/ppermute | solution.py:201
  206.9 21.1 %collective-permute-start.12 = (bf16[512,512]{1,0:T(8,128)(2,1)}, bf16[512,512]{1,0:T(8,128)(2,1)}, u32[]{:S(2)}, u32[]{:S(2)}) collective-permute-start(bf16[512,512]{1,0:T(8,128)(2,1)} %get-tuple-element.96), channel_id=1, source_target_pairs={{0,4},{4,0},{1,5},{5,1},{2,6},{6,2},{3,7},{7,3},{8,12},{12,8},{9,1... | collective-permute-start | bytes 1572872 | tf_op jit(solution)/shard_map/ppermute | solution.py:201
  208.5 19.5 %collective-permute-start.13 = (bf16[512,512]{0,1:T(8,128)(2,1)}, bf16[512,512]{0,1:T(8,128)(2,1)}, u32[]{:S(2)}, u32[]{:S(2)}) collective-permute-start(bf16[512,512]{0,1:T(8,128)(2,1)} %copy.26), channel_id=1, source_target_pairs={{0,16},{16,8},{8,24},{24,0},{1,17},{17,9},{9,25},{25,1},{2,18},{18... | collective-permute-start | bytes 1572872 | tf_op jit(solution)/shard_map/ppermute | solution.py:179
  210.8 18.3 %collective-permute-start.10 = (bf16[2,2,64,1024]{3,2,0,1:T(8,128)(2,1)}, bf16[2,2,64,1024]{3,2,0,1:T(8,128)(2,1)S(1)}, u32[]{:S(2)}, u32[]{:S(2)}) collective-permute-start(bf16[2,2,64,1024]{3,2,0,1:T(8,128)(2,1)} %pad_maximum_fusion.5), channel_id=1, source_target_pairs={{0,1},{1,0},{2,3},{3,2},{4,5},{5,4},{6,7},{7,6},{8,9},{9,8},{10,11... | collective-permute-start | bytes 1572872 | tf_op jit(solution)/shard_map/ppermute | solution.py:201
  211.9 16.1 %collective-permute-start.11 = (bf16[128,1024]{1,0:T(8,128)(2,1)S(1)}, bf16[128,1024]{1,0:T(8,128)(2,1)S(1)}, u32[]{:S(2)}, u32[]{:S(2)}) collective-permute-start(bf16[128,1024]{1,0:T(8,128)(2,1)S(1)} %slice.38), channel_id=1, source_target_pairs={{0,2},{1,3},{2,0},{3,1},{4,6},{5,7},{6,4},{7,5},{8,10},{9,11},{10,... | collective-permute-start | bytes 786440 | tf_op jit(solution)/shard_map/ppermute | solution.py:201
  216.4 13.1 %copy-start.2 = (bf16[2,2,128,1024]{3,2,1,0:T(8,128)(2,1)S(1)}, bf16[2,2,128,1024]{3,2,1,0:T(8,128)(2,1)}, u32[]{:S(2)}) copy-start(bf16[2,2,128,1024]{3,2,1,0:T(8,128)(2,1)} %copy-done.1) | copy-start | bytes 3145732
  229.4 20.8 %copy-start.3 = (bf16[2,2,2,64,1024]{4,3,2,1,0:T(8,128)(2,1)}, bf16[2,2,2,64,1024]{4,3,2,1,0:T(8,128)(2,1)S(1)}, u32[]{:S(2)}) copy-start(bf16[2,2,2,64,1024]{4,3,2,1,0:T(8,128)(2,1)S(1)} %copy.18) | copy-start | bytes 3145732
  229.4 18.0 %collective-permute-start.16 = (bf16[512,1024]{1,0:T(8,128)(2,1)S(1)}, bf16[512,1024]{1,0:T(8,128)(2,1)}, u32[]{:S(2)}, u32[]{:S(2)}) collective-permute-start(bf16[512,1024]{1,0:T(8,128)(2,1)S(1)} %bitcast.106), channel_id=1, source_target_pairs={{0,8},{8,0},{16,24},{24,16},{1,9},{9,1},{17,25},{25,17},{2,10},{10... | collective-permute-start | bytes 3145736 | tf_op jit(solution)/shard_map/ppermute | solution.py:172
  230.9 14.4 %collective-permute-start.17 = (bf16[512,512]{0,1:T(8,128)(2,1)S(1)}, bf16[512,512]{0,1:T(8,128)(2,1)}, u32[]{:S(2)}, u32[]{:S(2)}) collective-permute-start(bf16[512,512]{0,1:T(8,128)(2,1)S(1)} %get-tuple-element.66), channel_id=1, source_target_pairs={{0,4},{4,0},{1,5},{5,1},{2,6},{6,2},{3,7},{7,3},{8,12},{12,8},{9,1... | collective-permute-start | bytes 1572872 | tf_op jit(solution)/shard_map/ppermute | solution.py:201
  234.2 30.2 %collective-permute-start.14 = (bf16[2,128,1024]{2,1,0:T(8,128)(2,1)}, bf16[2,128,1024]{2,1,0:T(8,128)(2,1)}, u32[]{:S(2)}, u32[]{:S(2)}) collective-permute-start(bf16[2,128,1024]{2,1,0:T(8,128)(2,1)} %pad_maximum_fusion.6), channel_id=1, source_target_pairs={{0,1},{1,0},{2,3},{3,2},{4,5},{5,4},{6,7},{7,6},{8,9},{9,8},{10,11... | collective-permute-start | bytes 1572872 | tf_op jit(solution)/shard_map/ppermute | solution.py:201
  236.3 43.9 %collective-permute-start.20 = (bf16[512,512]{0,1:T(8,128)(2,1)}, bf16[512,512]{0,1:T(8,128)(2,1)}, u32[]{:S(2)}, u32[]{:S(2)}) collective-permute-start(bf16[512,512]{0,1:T(8,128)(2,1)} %get-tuple-element.71), channel_id=1, source_target_pairs={{0,16},{16,8},{8,24},{24,0},{1,17},{17,9},{9,25},{25,1},{2,18},{18... | collective-permute-start | bytes 1572872 | tf_op jit(solution)/shard_map/ppermute | solution.py:179
  238.3 23.9 %collective-permute-start.15 = (bf16[512,512]{1,0:T(8,128)(2,1)}, bf16[512,512]{1,0:T(8,128)(2,1)}, u32[]{:S(2)}, u32[]{:S(2)}) collective-permute-start(bf16[512,512]{1,0:T(8,128)(2,1)} %collective-permute-done.12), channel_id=1, source_target_pairs={{0,16},{16,8},{8,24},{24,0},{1,17},{17,9},{9,25},{25,1},{2,18},{18... | collective-permute-start | bytes 1572872 | tf_op jit(solution)/shard_map/ppermute | solution.py:179
  245.3 43.2 %collective-permute-start.19 = (bf16[512,512]{0,1:T(8,128)(2,1)}, bf16[512,512]{0,1:T(8,128)(2,1)}, u32[]{:S(2)}, u32[]{:S(2)}) collective-permute-start(bf16[512,512]{0,1:T(8,128)(2,1)} %collective-permute-done.17), channel_id=1, source_target_pairs={{0,16},{16,8},{8,24},{24,0},{1,17},{17,9},{9,25},{25,1},{2,18},{18... | collective-permute-start | bytes 1572872 | tf_op jit(solution)/shard_map/ppermute | solution.py:179
  266.6 25.9 %collective-permute-start.18 = (bf16[512,1024]{1,0:T(8,128)(2,1)}, bf16[512,1024]{1,0:T(8,128)(2,1)}, u32[]{:S(2)}, u32[]{:S(2)}) collective-permute-start(bf16[512,1024]{1,0:T(8,128)(2,1)} %bitcast.32), channel_id=1, source_target_pairs={{0,4},{4,0},{1,5},{5,1},{2,6},{6,2},{3,7},{7,3},{8,12},{12,8},{9,1... | collective-permute-start | bytes 3145736 | tf_op jit(solution)/shard_map/ppermute | solution.py:201
  277.7 25.3 %collective-permute-start.23 = (bf16[512,896]{1,0:T(8,128)(2,1)S(1)}, bf16[512,896]{1,0:T(8,128)(2,1)S(1)}, u32[]{:S(2)}, u32[]{:S(2)}) collective-permute-start(bf16[512,896]{1,0:T(8,128)(2,1)S(1)} %shard_map.18.refs_0_.refs_7_), channel_id=1, source_target_pairs={{0,16},{8,24},{16,0},{24,8},{1,17},{9,25},{17,1},{25,9},{2,18},{10... | collective-permute-start | bytes 2752520 | tf_op jit(solution)/shard_map/ppermute | solution.py:169
  280.2 23.4 %collective-permute-start.22 = (bf16[512,896]{1,0:T(8,128)(2,1)S(1)}, bf16[512,896]{1,0:T(8,128)(2,1)}, u32[]{:S(2)}, u32[]{:S(2)}) collective-permute-start(bf16[512,896]{1,0:T(8,128)(2,1)S(1)} %shard_map.18.refs_0_.refs_7_), channel_id=1, source_target_pairs={{0,8},{8,0},{16,24},{24,16},{1,9},{9,1},{17,25},{25,17},{2,10},{10... | collective-permute-start | bytes 2752520 | tf_op jit(solution)/shard_map/ppermute | solution.py:172
  303.0 2.7 collective-permute-start.24
  303.0 3.9 %collective-permute-start.25 = (bf16[512,896]{1,0:T(8,128)(2,1)S(1)}, bf16[512,896]{1,0:T(8,128)(2,1)}, u32[]{:S(2)}, u32[]{:S(2)}) collective-permute-start(bf16[512,896]{1,0:T(8,128)(2,1)S(1)} %shard_map.19.refs_4_.refs_8_), channel_id=1, source_target_pairs={{0,8},{8,0},{16,24},{24,16},{1,9},{9,1},{17,25},{25,17},{2,10},{10... | collective-permute-start | bytes 2752520 | tf_op jit(solution)/shard_map/ppermute | solution.py:172
  303.5 22.4 %collective-permute-start.21 = (bf16[512,896]{1,0:T(8,128)(2,1)S(1)}, bf16[512,896]{1,0:T(8,128)(2,1)}, u32[]{:S(2)}, u32[]{:S(2)}) collective-permute-start(bf16[512,896]{1,0:T(8,128)(2,1)S(1)} %shard_map.19.refs_4_.refs_8_), channel_id=1, source_target_pairs={{0,16},{8,24},{16,0},{24,8},{1,17},{9,25},{17,1},{25,9},{2,18},{10... | collective-permute-start | bytes 2752520 | tf_op jit(solution)/shard_map/ppermute | solution.py:169
  326.0 2.7 collective-permute-start.26
  (7 other events, 41.0 us)

commit v7 on v6

--- a/solution.py
+++ b/solution.py
@@ -358,7 +358,7 @@
             return held_rows
 
         pair_got, own_got, gram_rows, *_ = lax.optimization_barrier(
-            (pair_got, own_got, gram_rows, *came_first, *rung_own)
+            (pair_got, own_got, gram_rows, *came_first)
         )
         pair.take(pair_got)
         pair_half = pair.value.reshape(half, rows)
@@ -367,8 +367,9 @@
         while len(own.steps) > 1:
             own.take(own.send())
         own_got = own.send()
-        gram_rows = after(gram_rows, own.value)
         gram_rows = put_rung(rung_own, 0, here)
+        gram_rows = after(gram_rows, own.value, *came_second)
+        gram_rows = put_rung(rung_first, 0, there)
         pair_other, gram_rows = lax.optimization_barrier((pair_other, gram_rows))
 
         left, right = pair_half[:, :half], pair_half[:, half:]
@@ -386,8 +387,6 @@
             return lax.dynamic_update_slice(held_rows, second, (row, rows + half))
 
         gram_rows = put_pair(0, as_upper)
-        gram_rows = after(gram_rows, *came_second)
-        gram_rows = put_rung(rung_first, 0, there)
         own_got, gram_rows = lax.optimization_barrier((own_got, gram_rows))
         own.take(own_got)
         own_rows = own.value.reshape(half, rows)

time: 338 us -> 324 us (0.959)
  waiting for transfers between devices: 148 us -> 135 us
    ppermute x4, waiting for transfers between devices: 11 us -> 1.21 us  [ring(): return lax.ppermute(value, 'fsdp', pairs)]
  transfers between devices with their start and end apart: 29 -> 29, of which waited for: 17 -> 17; matrix products, arithmetic and copies ran while one was open for 18% -> 18% of each run, Pallas kernels for 9% -> 10%
where the time goes in v7:
time: 324 us; the launch traced here: 322 us
  waiting for transfers between devices  135 us (42%)
  blocking collectives  50.6 us (16%)
  Pallas kernels  39.1 us (12%)
  local copies, waits for them, and re-layouts  37.2 us (11%)
  starting transfers between devices  32.1 us (10%)
  other arithmetic  17.9 us (6%)
  matrix products  10.1 us (3%)
    all_to_all x1, blocking collectives, body(): lax.all_to_all(iterate, over, split_axis=1, concat_axis=0, tiled=True)  50.6 us
    ppermute x10, waiting for transfers between devices, swap(): return lax.ppermute(value, axis, [(at, at ^ bit) for at in range(size)])  48.2 us
    ppermute x3, waiting for transfers between devices, begin_sum(): got = lax.ppermute(sent, 'grp', [(at, at ^ bit) for at in range(n_grp)])  45 us
    pallas_call x2, Pallas kernels, add_terms(): pl.pallas_call(kernel(len(rights)), out_shape=jax.ShapeDtypeStruct((rows,...  20.5 us
    ppermute x3, waiting for transfers between devices, from_chip(): return lax.ppermute(value, 'fsdp', pairs)  18.4 us
    all_to_all x2, waiting for transfers between devices, to_rep(): return lax.all_to_all(cut, 'rep', split_axis=0, concat_axis=0, tiled=True)  18 us
    pallas_call x2, Pallas kernels, product(): pl.pallas_call(first_kernel, out_shape=jax.ShapeDtypeStruct((rows, width)...  16.3 us
    dynamic_update_slice x4, local copies, waits for them, and re-layouts, in_order(): lax.dynamic_update_slice(whole, block, (slots[at] * rows + start, 0))  12.1 us
  transfers between devices with their start and end apart: 29, of which 17 were waited for; matrix products, arithmetic and copies ran while one was open for 18% of the time, Pallas kernels for 10%

profile of v7, /device:TPU:0, one launch (start us, length us, event | category | flops | bytes accessed | tf_op | source)
XLA Modules:
  0.0 322.4 jit_solution(14129559784955216520)
XLA Ops:
  1.8 50.6 %all_to_all.29 = bf16[128,8,896]{2,0,1:T(8,128)(2,1)S(1)} all-to-all(bf16[128,8,896]{2,0,1:T(8,128)(2,1)S(1)} %bitcast.111), channel_id=1, replica_groups=mesh['fsdp'=4,'grp'=2,'rep'=4] {'grp','rep'}, dimensions={1} | all-to-all | bytes 3670016 | tf_op jit(solution)/shard_map/all_to_all | solution.py:242
  54.0 2.4 convolution_convert_fusion
  62.5 20.0 %collective-permute-done.1 = bf16[512,1024]{1,0:T(8,128)(2,1)S(1)} collective-permute-done((bf16[512,1024]{1,0:T(8,128)(2,1)S(1)}, bf16[512,1024]{1,0:T(8,128)(2,1)S(1)}, u32[]{:S(2)}, u32[]{:S(2)}) %collective-permute-start.1) | collective-permute-done | bytes 1048608 | tf_op jit(solution)/shard_map/ppermute | solution.py:189
  82.5 12.4 %collective-permute-done = bf16[1024,896]{1,0:T(8,128)(2,1)} collective-permute-done((bf16[1024,896]{1,0:T(8,128)(2,1)S(1)}, bf16[1024,896]{1,0:T(8,128)(2,1)}, u32[]{:S(2)}, u32[]{:S(2)}) %collective-permute-start) | collective-permute-done | bytes 1835040 | tf_op jit(solution)/shard_map/ppermute | solution.py:169
  100.4 3.6 %all-to-all-start.1 = ((bf16[4,192,1024]{2,1,0:T(8,128)(2,1)}), bf16[4,192,1024]{2,1,0:T(8,128)(2,1)S(1)}, u32[]{:S(2)}, u32[]{:S(2)}) async-start(bf16[4,192,1024]{2,1,0:T(8,128)(2,1)} %pad_maximum_fusion), calls=%async_computation.1 | async-start | bytes 3145728 | tf_op jit(solution)/shard_map/all_to_all | solution.py:234
  104.0 3.9 %convert_bitcast_fusion = bf16[1024,1024]{1,0:T(8,128)(2,1)S(1)} fusion(bf16[1024,896]{1,0:T(8,128)(2,1)S(1)} %bitcast.100, bf16[1024,896]{1,0:T(8,128)(2,1)} %collective-permute-done, bf16[1024,896]{1,0:T(8,128)(2,1)} %collective-permute-done.4, pred[]{:T(512)S(6)} %lt.82), kind=kOutput, calls=%fused_computation.1 | convolution fusion | flops 1881014272 | bytes 7602177 | tf_op jit(solution)/shard_map/dot_general | solution.py:24
  108.6 25.0 %collective-permute-done.5 = bf16[512,1024]{1,0:T(8,128)(2,1)S(1)} collective-permute-done((bf16[512,1024]{1,0:T(8,128)(2,1)S(1)}, bf16[512,1024]{1,0:T(8,128)(2,1)S(1)}, u32[]{:S(2)}, u32[]{:S(2)}) %collective-permute-start.5) | collective-permute-done | bytes 1048608 | tf_op jit(solution)/shard_map/ppermute | solution.py:189
  134.9 6.9 %all-to-all-done.1 = bf16[4,192,1024]{2,1,0:T(8,128)(2,1)S(1)} async-done(((bf16[4,192,1024]{2,1,0:T(8,128)(2,1)}), bf16[4,192,1024]{2,1,0:T(8,128)(2,1)S(1)}, u32[]{:S(2)}, u32[]{:S(2)}) %all-to-all-start.1) | async-done | bytes 1572896 | tf_op jit(solution)/shard_map/all_to_all | solution.py:234
  141.8 4.2 %all-to-all-start.2 = ((bf16[4,128,1024]{2,1,0:T(8,128)(2,1)}), bf16[4,128,1024]{2,1,0:T(8,128)(2,1)}, u32[]{:S(2)}, u32[]{:S(2)}) async-start(bf16[4,128,1024]{2,1,0:T(8,128)(2,1)} %bitcast.113), calls=%async_computation.2 | async-start | bytes 2097152 | tf_op jit(solution)/shard_map/all_to_all | solution.py:234
  146.1 3.5 %dynamic_update_slice.48 = bf16[4096,896]{1,0:T(8,128)(2,1)} pad(bf16[1024,896]{1,0:T(8,128)(2,1)S(1)} %bitcast.101, bf16[]{:T(256)} %constant.128.clone.1), padding=0_3072x0_0 | pad | bytes 9175042 | tf_op jit(solution)/shard_map/dynamic_update_slice | solution.py:261
  149.5 2.9 constant_dynamic-update-slice_fusion.5
  152.4 2.9 constant_dynamic-update-slice_fusion.4
  156.3 2.9 constant_dynamic-update-slice_fusion.3.right
  160.9 11.2 %all-to-all-done.2 = bf16[4,128,1024]{2,1,0:T(8,128)(2,1)} async-done(((bf16[4,128,1024]{2,1,0:T(8,128)(2,1)}), bf16[4,128,1024]{2,1,0:T(8,128)(2,1)}, u32[]{:S(2)}, u32[]{:S(2)}) %all-to-all-start.2) | async-done | bytes 1048608 | tf_op jit(solution)/shard_map/all_to_all | solution.py:234
  173.6 12.3 %collective-permute-done.7 = bf16[128,1024]{1,0:T(8,128)(2,1)S(1)} collective-permute-done((bf16[128,1024]{1,0:T(8,128)(2,1)S(1)}, bf16[128,1024]{1,0:T(8,128)(2,1)S(1)}, u32[]{:S(2)}, u32[]{:S(2)}) %collective-permute-start.7) | collective-permute-done | bytes 262176 | tf_op jit(solution)/shard_map/ppermute | solution.py:201
  186.2 3.2 collective-permute-start.8
  189.4 16.2 %collective-permute-done.9 = bf16[2,128,1024]{2,1,0:T(8,128)(2,1)S(1)} collective-permute-done((bf16[2,128,1024]{2,1,0:T(8,128)(2,1)S(1)}, bf16[2,128,1024]{2,1,0:T(8,128)(2,1)S(1)}, u32[]{:S(2)}, u32[]{:S(2)}) %collective-permute-start.9) | collective-permute-done | bytes 524320 | tf_op jit(solution)/shard_map/ppermute | solution.py:201
  209.4 2.2 collective-permute-start.11
  211.6 2.3 shard_map.17
  216.4 9.3 %collective-permute-done.11 = bf16[128,1024]{1,0:T(8,128)(2,1)S(1)} collective-permute-done((bf16[128,1024]{1,0:T(8,128)(2,1)S(1)}, bf16[128,1024]{1,0:T(8,128)(2,1)S(1)}, u32[]{:S(2)}, u32[]{:S(2)}) %collective-permute-start.11) | collective-permute-done | bytes 262176 | tf_op jit(solution)/shard_map/ppermute | solution.py:201
  233.5 2.0 collective-permute-start.13
  237.7 5.3 %collective-permute-done.17 = bf16[512,512]{0,1:T(8,128)(2,1)} collective-permute-done((bf16[512,512]{0,1:T(8,128)(2,1)S(1)}, bf16[512,512]{0,1:T(8,128)(2,1)}, u32[]{:S(2)}, u32[]{:S(2)}) %collective-permute-start.17) | collective-permute-done | bytes 524320 | tf_op jit(solution)/shard_map/ppermute | solution.py:201
  244.5 2.5 collective-permute-start.19
  254.6 2.3 constant_dynamic-update-slice_fusion.1.left
  256.9 8.2 %shard_map.18.refs_0_.refs_7_ = bf16[512,896]{1,0:T(8,128)(2,1)S(1)} custom-call(bf16[1024,4096]{1,0:T(8,128)(2,1)} %constant_dynamic-update-slice_fusion.1.left, bf16[4096,896]{1,0:T(8,128)(2,1)} %constant_dynamic-update-slice_fusion.3.right), custom_call_target="tpu_custom_call" | custom-call | tf_op jit(solution)/shard_map/pallas_call | solution.py:55
  275.6 2.3 collective-permute-done.18
  277.9 2.4 constant_dynamic-update-slice_fusion.left
  280.2 8.1 %shard_map.19.refs_4_.refs_8_ = bf16[512,896]{1,0:T(8,128)(2,1)S(1)} custom-call(bf16[1024,4096]{1,0:T(8,128)(2,1)} %constant_dynamic-update-slice_fusion.left, bf16[4096,896]{1,0:T(8,128)(2,1)} %constant_dynamic-update-slice_fusion.3.right), custom_call_target="tpu_custom_call" | custom-call | tf_op jit(solution)/shard_map/pallas_call | solution.py:55
  292.3 13.0 %shard_map.20.refs_2_ = f32[1024,896]{1,0:T(8,128)} custom-call(s32[7]{0:T(128)S(1)} %stack.125.columns, bf16[1024,4096]{1,0:T(8,128)(2,1)} %constant_dynamic-update-slice_fusion.left, bf16[512,896]{1,0:T(8,128)(2,1)S(1)} %shard_map.18.refs_0_.refs_7_, bf16[512,896]{1,0:T(8,128)(2,1)} %collective-permute-done.22.refs_1_, ...), custom_call_target="tpu_custom_call" | custom-call | tf_op jit(solution)/shard_map/pallas_call | solution.py:127
  305.4 6.0 %collective-permute-done.21.refs_0_ = bf16[512,896]{1,0:T(8,128)(2,1)} collective-permute-done((bf16[512,896]{1,0:T(8,128)(2,1)S(1)}, bf16[512,896]{1,0:T(8,128)(2,1)}, u32[]{:S(2)}, u32[]{:S(2)}) %collective-permute-start.21) | collective-permute-done | bytes 917536 | tf_op jit(solution)/shard_map/ppermute | solution.py:169
  311.9 2.1 collective-permute-done.26.refs_1_
  315.0 7.4 %shard_map.21 = bf16[1024,896]{1,0:T(8,128)(2,1)} custom-call(s32[3]{0:T(128)} %pad_add_fusion.columns, bf16[1024,4096]{1,0:T(8,128)(2,1)} %constant_dynamic-update-slice_fusion.left, bf16[512,896]{1,0:T(8,128)(2,1)} %collective-permute-done.21.refs_0_, bf16[512,896]{1,0:T(8,128)(2,1)} %copy-done.7, f32[1024,896]{1,0:T(8,128)} %shard_map.20.refs_2_), custom_call_target="tpu_custom_call" | custom-call | tf_op jit(solution)/shard_map/pallas_call | solution.py:127
  (113 shorter events, 62.4 us)
Async XLA Ops:
  52.4 93.7 %copy-start = (bf16[128,8,896]{2,0,1:T(8,128)(2,1)}, bf16[128,8,896]{2,0,1:T(8,128)(2,1)S(1)}, u32[]{:S(2)}) copy-start(bf16[128,8,896]{2,0,1:T(8,128)(2,1)S(1)} %all_to_all.29) | copy-start | bytes 5505028
  52.4 4.7 %collective-permute-start.2 = (bf16[1024,896]{1,0:T(8,128)(2,1)S(1)}, bf16[1024,896]{1,0:T(8,128)(2,1)}, u32[]{:S(2)}, u32[]{:S(2)}) collective-permute-start(bf16[1024,896]{1,0:T(8,128)(2,1)S(1)} %bitcast.95), channel_id=1, source_target_pairs={{0,8},{8,0},{16,24},{24,16},{1,9},{9,1},{17,25},{25,17},{2,10},{10... | collective-permute-start | bytes 5505032 | tf_op jit(solution)/shard_map/ppermute | solution.py:172
  52.4 42.5 %collective-permute-start = (bf16[1024,896]{1,0:T(8,128)(2,1)S(1)}, bf16[1024,896]{1,0:T(8,128)(2,1)}, u32[]{:S(2)}, u32[]{:S(2)}) collective-permute-start(bf16[1024,896]{1,0:T(8,128)(2,1)S(1)} %bitcast.96), channel_id=1, source_target_pairs={{0,16},{8,24},{16,0},{24,8},{1,17},{9,25},{17,1},{25,9},{2,18},{10... | collective-permute-start | bytes 5505032 | tf_op jit(solution)/shard_map/ppermute | solution.py:169
  56.4 26.1 %collective-permute-start.1 = (bf16[512,1024]{1,0:T(8,128)(2,1)S(1)}, bf16[512,1024]{1,0:T(8,128)(2,1)S(1)}, u32[]{:S(2)}, u32[]{:S(2)}) collective-permute-start(bf16[512,1024]{1,0:T(8,128)(2,1)S(1)} %constant_dynamic-slice_fusion.5), channel_id=1, source_target_pairs={{0,4},{4,0},{1,5},{5,1},{2,6},{6,2},{3,7},{7,3},{8,12},{12,8},{9,1... | collective-permute-start | bytes 3145736 | tf_op jit(solution)/shard_map/ppermute | solution.py:189
  61.0 34.0 %collective-permute-start.3 = (bf16[256,1024]{0,1:T(8,128)(2,1)S(1)}, bf16[256,1024]{0,1:T(8,128)(2,1)S(1)}, u32[]{:S(2)}, u32[]{:S(2)}) collective-permute-start(bf16[256,1024]{0,1:T(8,128)(2,1)S(1)} %fusion.6), channel_id=1, source_target_pairs={{0,4},{4,0},{1,5},{5,1},{2,6},{6,2},{3,7},{7,3},{8,12},{12,8},{9,1... | collective-permute-start | bytes 1572872 | tf_op jit(solution)/shard_map/ppermute | solution.py:189
  82.5 12.4 %copy-start.6 = (bf16[512,1024]{1,0:T(8,128)(2,1)}, bf16[512,1024]{1,0:T(8,128)(2,1)S(1)}, u32[]{:S(2)}) copy-start(bf16[512,1024]{1,0:T(8,128)(2,1)S(1)} %collective-permute-done.1) | copy-start | bytes 3145732
  95.7 8.2 %collective-permute-start.4 = (bf16[1024,896]{1,0:T(8,128)(2,1)}, bf16[1024,896]{1,0:T(8,128)(2,1)}, u32[]{:S(2)}, u32[]{:S(2)}) collective-permute-start(bf16[1024,896]{1,0:T(8,128)(2,1)} %collective-permute-done), channel_id=1, source_target_pairs={{0,8},{8,0},{16,24},{24,16},{1,9},{9,1},{17,25},{25,17},{2,10},{10... | collective-permute-start | bytes 5505032 | tf_op jit(solution)/shard_map/ppermute | solution.py:172
  100.4 41.4 %all-to-all-start.1 = ((bf16[4,192,1024]{2,1,0:T(8,128)(2,1)}), bf16[4,192,1024]{2,1,0:T(8,128)(2,1)S(1)}, u32[]{:S(2)}, u32[]{:S(2)}) async-start(bf16[4,192,1024]{2,1,0:T(8,128)(2,1)} %pad_maximum_fusion), calls=%async_computation.1 | async-start | bytes 3145728 | tf_op jit(solution)/shard_map/all_to_all | solution.py:234
  107.9 25.6 %collective-permute-start.5 = (bf16[512,1024]{1,0:T(8,128)(2,1)S(1)}, bf16[512,1024]{1,0:T(8,128)(2,1)S(1)}, u32[]{:S(2)}, u32[]{:S(2)}) collective-permute-start(bf16[512,1024]{1,0:T(8,128)(2,1)S(1)} %constant_dynamic-slice_fusion.4), channel_id=1, source_target_pairs={{0,4},{4,0},{1,5},{5,1},{2,6},{6,2},{3,7},{7,3},{8,12},{12,8},{9,1... | collective-permute-start | bytes 3145736 | tf_op jit(solution)/shard_map/ppermute | solution.py:189
  141.8 30.2 %all-to-all-start.2 = ((bf16[4,128,1024]{2,1,0:T(8,128)(2,1)}), bf16[4,128,1024]{2,1,0:T(8,128)(2,1)}, u32[]{:S(2)}, u32[]{:S(2)}) async-start(bf16[4,128,1024]{2,1,0:T(8,128)(2,1)} %bitcast.113), calls=%async_computation.2 | async-start | bytes 2097152 | tf_op jit(solution)/shard_map/all_to_all | solution.py:234
  155.7 5.2 %collective-permute-start.6 = (bf16[64,1024]{1,0:T(8,128)(2,1)S(1)}, bf16[64,1024]{1,0:T(8,128)(2,1)S(1)}, u32[]{:S(2)}, u32[]{:S(2)}) collective-permute-start(bf16[64,1024]{1,0:T(8,128)(2,1)S(1)} %slice.39), channel_id=1, source_target_pairs={{0,4},{4,0},{1,5},{5,1},{2,6},{6,2},{3,7},{7,3},{8,12},{12,8},{9,1... | collective-permute-start | bytes 393224 | tf_op jit(solution)/shard_map/ppermute | solution.py:201
  173.4 12.4 %collective-permute-start.7 = (bf16[128,1024]{1,0:T(8,128)(2,1)S(1)}, bf16[128,1024]{1,0:T(8,128)(2,1)S(1)}, u32[]{:S(2)}, u32[]{:S(2)}) collective-permute-start(bf16[128,1024]{1,0:T(8,128)(2,1)S(1)} %reduce_sum.25), channel_id=1, source_target_pairs={{0,2},{1,3},{2,0},{3,1},{4,6},{5,7},{6,4},{7,5},{8,10},{9,11},{10,... | collective-permute-start | bytes 786440 | tf_op jit(solution)/shard_map/ppermute | solution.py:201
  186.0 19.5 %collective-permute-start.9 = (bf16[2,128,1024]{2,1,0:T(8,128)(2,1)S(1)}, bf16[2,128,1024]{2,1,0:T(8,128)(2,1)S(1)}, u32[]{:S(2)}, u32[]{:S(2)}) collective-permute-start(bf16[2,128,1024]{2,1,0:T(8,128)(2,1)S(1)} %pad_maximum_fusion.4), channel_id=1, source_target_pairs={{0,1},{1,0},{2,3},{3,2},{4,5},{5,4},{6,7},{7,6},{8,9},{9,8},{10,11... | collective-permute-start | bytes 1572872 | tf_op jit(solution)/shard_map/ppermute | solution.py:201
  186.2 19.6 %collective-permute-start.8 = (bf16[2,64,1024]{2,1,0:T(8,128)(2,1)S(1)}, bf16[2,64,1024]{2,1,0:T(8,128)(2,1)S(1)}, u32[]{:S(2)}, u32[]{:S(2)}) collective-permute-start(bf16[2,64,1024]{2,1,0:T(8,128)(2,1)S(1)} %pad_maximum_fusion.7), channel_id=1, source_target_pairs={{0,2},{1,3},{2,0},{3,1},{4,6},{5,7},{6,4},{7,5},{8,10},{9,11},{10,... | collective-permute-start | bytes 786440 | tf_op jit(solution)/shard_map/ppermute | solution.py:201
  206.8 18.9 %collective-permute-start.12 = (bf16[512,512]{1,0:T(8,128)(2,1)}, bf16[512,512]{1,0:T(8,128)(2,1)}, u32[]{:S(2)}, u32[]{:S(2)}) collective-permute-start(bf16[512,512]{1,0:T(8,128)(2,1)} %get-tuple-element.92), channel_id=1, source_target_pairs={{0,4},{4,0},{1,5},{5,1},{2,6},{6,2},{3,7},{7,3},{8,12},{12,8},{9,1... | collective-permute-start | bytes 1572872 | tf_op jit(solution)/shard_map/ppermute | solution.py:201
  208.3 18.5 %collective-permute-start.10 = (bf16[2,2,64,1024]{3,2,0,1:T(8,128)(2,1)}, bf16[2,2,64,1024]{3,2,0,1:T(8,128)(2,1)S(1)}, u32[]{:S(2)}, u32[]{:S(2)}) collective-permute-start(bf16[2,2,64,1024]{3,2,0,1:T(8,128)(2,1)} %pad_maximum_fusion.5), channel_id=1, source_target_pairs={{0,1},{1,0},{2,3},{3,2},{4,5},{5,4},{6,7},{7,6},{8,9},{9,8},{10,11... | collective-permute-start | bytes 1572872 | tf_op jit(solution)/shard_map/ppermute | solution.py:201
  209.4 16.4 %collective-permute-start.11 = (bf16[128,1024]{1,0:T(8,128)(2,1)S(1)}, bf16[128,1024]{1,0:T(8,128)(2,1)S(1)}, u32[]{:S(2)}, u32[]{:S(2)}) collective-permute-start(bf16[128,1024]{1,0:T(8,128)(2,1)S(1)} %slice.38), channel_id=1, source_target_pairs={{0,2},{1,3},{2,0},{3,1},{4,6},{5,7},{6,4},{7,5},{8,10},{9,11},{10,... | collective-permute-start | bytes 786440 | tf_op jit(solution)/shard_map/ppermute | solution.py:201
  214.9 15.2 %collective-permute-start.16 = (bf16[512,512]{0,1:T(8,128)(2,1)}, bf16[512,512]{0,1:T(8,128)(2,1)}, u32[]{:S(2)}, u32[]{:S(2)}) collective-permute-start(bf16[512,512]{0,1:T(8,128)(2,1)} %copy.26), channel_id=1, source_target_pairs={{0,16},{16,8},{8,24},{24,0},{1,17},{17,9},{9,25},{25,1},{2,18},{18... | collective-permute-start | bytes 1572872 | tf_op jit(solution)/shard_map/ppermute | solution.py:179
  227.1 23.6 %copy-start.3 = (bf16[2,2,2,64,1024]{4,3,2,1,0:T(8,128)(2,1)}, bf16[2,2,2,64,1024]{4,3,2,1,0:T(8,128)(2,1)S(1)}, u32[]{:S(2)}) copy-start(bf16[2,2,2,64,1024]{4,3,2,1,0:T(8,128)(2,1)S(1)} %copy.17) | copy-start | bytes 3145732
  227.2 20.8 %collective-permute-start.14 = (bf16[512,1024]{1,0:T(8,128)(2,1)S(1)}, bf16[512,1024]{1,0:T(8,128)(2,1)}, u32[]{:S(2)}, u32[]{:S(2)}) collective-permute-start(bf16[512,1024]{1,0:T(8,128)(2,1)S(1)} %bitcast.106), channel_id=1, source_target_pairs={{0,8},{8,0},{16,24},{24,16},{1,9},{9,1},{17,25},{25,17},{2,10},{10... | collective-permute-start | bytes 3145736 | tf_op jit(solution)/shard_map/ppermute | solution.py:172
  228.7 14.4 %collective-permute-start.17 = (bf16[512,512]{0,1:T(8,128)(2,1)S(1)}, bf16[512,512]{0,1:T(8,128)(2,1)}, u32[]{:S(2)}, u32[]{:S(2)}) collective-permute-start(bf16[512,512]{0,1:T(8,128)(2,1)S(1)} %get-tuple-element.62), channel_id=1, source_target_pairs={{0,4},{4,0},{1,5},{5,1},{2,6},{6,2},{3,7},{7,3},{8,12},{12,8},{9,1... | collective-permute-start | bytes 1572872 | tf_op jit(solution)/shard_map/ppermute | solution.py:201
  230.1 14.2 %collective-permute-start.15 = (bf16[512,512]{1,0:T(8,128)(2,1)}, bf16[512,512]{1,0:T(8,128)(2,1)S(1)}, u32[]{:S(2)}, u32[]{:S(2)}) collective-permute-start(bf16[512,512]{1,0:T(8,128)(2,1)} %collective-permute-done.12), channel_id=1, source_target_pairs={{0,16},{16,8},{8,24},{24,0},{1,17},{17,9},{9,25},{25,1},{2,18},{18... | collective-permute-start | bytes 1572872 | tf_op jit(solution)/shard_map/ppermute | solution.py:179
  233.5 18.3 %collective-permute-start.13 = (bf16[2,128,1024]{2,1,0:T(8,128)(2,1)}, bf16[2,128,1024]{2,1,0:T(8,128)(2,1)}, u32[]{:S(2)}, u32[]{:S(2)}) collective-permute-start(bf16[2,128,1024]{2,1,0:T(8,128)(2,1)} %pad_maximum_fusion.6), channel_id=1, source_target_pairs={{0,1},{1,0},{2,3},{3,2},{4,5},{5,4},{6,7},{7,6},{8,9},{9,8},{10,11... | collective-permute-start | bytes 1572872 | tf_op jit(solution)/shard_map/ppermute | solution.py:201
  235.5 29.9 %collective-permute-start.20 = (bf16[512,512]{0,1:T(8,128)(2,1)}, bf16[512,512]{0,1:T(8,128)(2,1)}, u32[]{:S(2)}, u32[]{:S(2)}) collective-permute-start(bf16[512,512]{0,1:T(8,128)(2,1)} %get-tuple-element.69), channel_id=1, source_target_pairs={{0,16},{16,8},{8,24},{24,0},{1,17},{17,9},{9,25},{25,1},{2,18},{18... | collective-permute-start | bytes 1572872 | tf_op jit(solution)/shard_map/ppermute | solution.py:179
  244.5 29.2 %collective-permute-start.19 = (bf16[512,512]{0,1:T(8,128)(2,1)}, bf16[512,512]{0,1:T(8,128)(2,1)}, u32[]{:S(2)}, u32[]{:S(2)}) collective-permute-start(bf16[512,512]{0,1:T(8,128)(2,1)} %collective-permute-done.17), channel_id=1, source_target_pairs={{0,16},{16,8},{8,24},{24,0},{1,17},{17,9},{9,25},{25,1},{2,18},{18... | collective-permute-start | bytes 1572872 | tf_op jit(solution)/shard_map/ppermute | solution.py:179
  254.0 23.9 %collective-permute-start.18 = (bf16[512,1024]{1,0:T(8,128)(2,1)}, bf16[512,1024]{1,0:T(8,128)(2,1)}, u32[]{:S(2)}, u32[]{:S(2)}) collective-permute-start(bf16[512,1024]{1,0:T(8,128)(2,1)} %bitcast.32), channel_id=1, source_target_pairs={{0,4},{4,0},{1,5},{5,1},{2,6},{6,2},{3,7},{7,3},{8,12},{12,8},{9,1... | collective-permute-start | bytes 3145736 | tf_op jit(solution)/shard_map/ppermute | solution.py:201
  265.1 23.3 %collective-permute-start.23 = (bf16[512,896]{1,0:T(8,128)(2,1)S(1)}, bf16[512,896]{1,0:T(8,128)(2,1)S(1)}, u32[]{:S(2)}, u32[]{:S(2)}) collective-permute-start(bf16[512,896]{1,0:T(8,128)(2,1)S(1)} %shard_map.18.refs_0_.refs_7_), channel_id=1, source_target_pairs={{0,16},{8,24},{16,0},{24,8},{1,17},{9,25},{17,1},{25,9},{2,18},{10... | collective-permute-start | bytes 2752520 | tf_op jit(solution)/shard_map/ppermute | solution.py:169
  265.4 25.0 %collective-permute-start.22 = (bf16[512,896]{1,0:T(8,128)(2,1)S(1)}, bf16[512,896]{1,0:T(8,128)(2,1)}, u32[]{:S(2)}, u32[]{:S(2)}) collective-permute-start(bf16[512,896]{1,0:T(8,128)(2,1)S(1)} %shard_map.18.refs_0_.refs_7_), channel_id=1, source_target_pairs={{0,8},{8,0},{16,24},{24,16},{1,9},{9,1},{17,25},{25,17},{2,10},{10... | collective-permute-start | bytes 2752520 | tf_op jit(solution)/shard_map/ppermute | solution.py:172
  288.4 2.7 collective-permute-start.24
  288.4 3.9 %collective-permute-start.25 = (bf16[512,896]{1,0:T(8,128)(2,1)S(1)}, bf16[512,896]{1,0:T(8,128)(2,1)}, u32[]{:S(2)}, u32[]{:S(2)}) collective-permute-start(bf16[512,896]{1,0:T(8,128)(2,1)S(1)} %shard_map.19.refs_4_.refs_8_), channel_id=1, source_target_pairs={{0,8},{8,0},{16,24},{24,16},{1,9},{9,1},{17,25},{25,17},{2,10},{10... | collective-permute-start | bytes 2752520 | tf_op jit(solution)/shard_map/ppermute | solution.py:172
  288.9 22.4 %collective-permute-start.21 = (bf16[512,896]{1,0:T(8,128)(2,1)S(1)}, bf16[512,896]{1,0:T(8,128)(2,1)}, u32[]{:S(2)}, u32[]{:S(2)}) collective-permute-start(bf16[512,896]{1,0:T(8,128)(2,1)S(1)} %shard_map.19.refs_4_.refs_8_), channel_id=1, source_target_pairs={{0,16},{8,24},{16,0},{24,8},{1,17},{9,25},{17,1},{25,9},{2,18},{10... | collective-permute-start | bytes 2752520 | tf_op jit(solution)/shard_map/ppermute | solution.py:169
  311.4 2.7 collective-permute-start.26
  (7 other events, 36.1 us)

commit v8 on v6

--- a/solution.py
+++ b/solution.py
@@ -358,7 +358,7 @@
             return held_rows
 
         pair_got, own_got, gram_rows, *_ = lax.optimization_barrier(
-            (pair_got, own_got, gram_rows, *came_first, *rung_own)
+            (pair_got, own_got, gram_rows, *came_first)
         )
         pair.take(pair_got)
         pair_half = pair.value.reshape(half, rows)
@@ -367,8 +367,8 @@
         while len(own.steps) > 1:
             own.take(own.send())
         own_got = own.send()
+        gram_rows = put_rung(rung_own, 0, here)
         gram_rows = after(gram_rows, own.value)
-        gram_rows = put_rung(rung_own, 0, here)
         pair_other, gram_rows = lax.optimization_barrier((pair_other, gram_rows))
 
         left, right = pair_half[:, :half], pair_half[:, half:]

time: 338 us -> 338 us (level)
  no operation moved by 1% of the time
where the time goes in v8:
time: 338 us; the launch traced here: 336 us
  waiting for transfers between devices  148 us (44%)
  blocking collectives  50.6 us (15%)
  Pallas kernels  39.1 us (12%)
  local copies, waits for them, and re-layouts  38.3 us (11%)
  starting transfers between devices  31.3 us (9%)
  other arithmetic  17.9 us (5%)
  matrix products  10.1 us (3%)
    all_to_all x1, blocking collectives, body(): lax.all_to_all(iterate, over, split_axis=1, concat_axis=0, tiled=True)  50.6 us
    ppermute x10, waiting for transfers between devices, swap(): return lax.ppermute(value, axis, [(at, at ^ bit) for at in range(size)])  48.4 us
    ppermute x3, waiting for transfers between devices, begin_sum(): got = lax.ppermute(sent, 'grp', [(at, at ^ bit) for at in range(n_grp)])  45 us
    pallas_call x2, Pallas kernels, add_terms(): pl.pallas_call(kernel(len(rights)), out_shape=jax.ShapeDtypeStruct((rows,...  20.5 us
    ppermute x3, waiting for transfers between devices, from_chip(): return lax.ppermute(value, 'fsdp', pairs)  18.4 us
    all_to_all x2, waiting for transfers between devices, to_rep(): return lax.all_to_all(cut, 'rep', split_axis=0, concat_axis=0, tiled=True)  18 us
    pallas_call x2, Pallas kernels, product(): pl.pallas_call(first_kernel, out_shape=jax.ShapeDtypeStruct((rows, width)...  16.3 us
    ppermute x4, waiting for transfers between devices, ring(): return lax.ppermute(value, 'fsdp', pairs)  13.2 us
  transfers between devices with their start and end apart: 29, of which 17 were waited for; matrix products, arithmetic and copies ran while one was open for 18% of the time, Pallas kernels for 9%

profile of v8, /device:TPU:0, one launch (start us, length us, event | category | flops | bytes accessed | tf_op | source)
XLA Modules:
  0.0 336.2 jit_solution(18393802184785033700)
XLA Ops:
  1.8 50.6 %all_to_all.29 = bf16[128,8,896]{2,0,1:T(8,128)(2,1)S(1)} all-to-all(bf16[128,8,896]{2,0,1:T(8,128)(2,1)S(1)} %bitcast.111), channel_id=1, replica_groups=mesh['fsdp'=4,'grp'=2,'rep'=4] {'grp','rep'}, dimensions={1} | all-to-all | bytes 3670016 | tf_op jit(solution)/shard_map/all_to_all | solution.py:242
  54.0 2.4 convolution_convert_fusion
  62.5 20.0 %collective-permute-done.1 = bf16[512,1024]{1,0:T(8,128)(2,1)S(1)} collective-permute-done((bf16[512,1024]{1,0:T(8,128)(2,1)S(1)}, bf16[512,1024]{1,0:T(8,128)(2,1)S(1)}, u32[]{:S(2)}, u32[]{:S(2)}) %collective-permute-start.1) | collective-permute-done | bytes 1048608 | tf_op jit(solution)/shard_map/ppermute | solution.py:189
  82.5 12.4 %collective-permute-done = bf16[1024,896]{1,0:T(8,128)(2,1)} collective-permute-done((bf16[1024,896]{1,0:T(8,128)(2,1)S(1)}, bf16[1024,896]{1,0:T(8,128)(2,1)}, u32[]{:S(2)}, u32[]{:S(2)}) %collective-permute-start) | collective-permute-done | bytes 1835040 | tf_op jit(solution)/shard_map/ppermute | solution.py:169
  100.4 3.6 %all-to-all-start.1 = ((bf16[4,192,1024]{2,1,0:T(8,128)(2,1)}), bf16[4,192,1024]{2,1,0:T(8,128)(2,1)S(1)}, u32[]{:S(2)}, u32[]{:S(2)}) async-start(bf16[4,192,1024]{2,1,0:T(8,128)(2,1)} %pad_maximum_fusion), calls=%async_computation.1 | async-start | bytes 3145728 | tf_op jit(solution)/shard_map/all_to_all | solution.py:234
  104.0 3.9 %convert_bitcast_fusion = bf16[1024,1024]{1,0:T(8,128)(2,1)S(1)} fusion(bf16[1024,896]{1,0:T(8,128)(2,1)S(1)} %bitcast.100, bf16[1024,896]{1,0:T(8,128)(2,1)} %collective-permute-done, bf16[1024,896]{1,0:T(8,128)(2,1)} %collective-permute-done.4, pred[]{:T(512)S(6)} %lt.82), kind=kOutput, calls=%fused_computation.1 | convolution fusion | flops 1881014272 | bytes 7602177 | tf_op jit(solution)/shard_map/dot_general | solution.py:24
  108.6 25.0 %collective-permute-done.5 = bf16[512,1024]{1,0:T(8,128)(2,1)S(1)} collective-permute-done((bf16[512,1024]{1,0:T(8,128)(2,1)S(1)}, bf16[512,1024]{1,0:T(8,128)(2,1)S(1)}, u32[]{:S(2)}, u32[]{:S(2)}) %collective-permute-start.5) | collective-permute-done | bytes 1048608 | tf_op jit(solution)/shard_map/ppermute | solution.py:189
  134.9 6.9 %all-to-all-done.1 = bf16[4,192,1024]{2,1,0:T(8,128)(2,1)S(1)} async-done(((bf16[4,192,1024]{2,1,0:T(8,128)(2,1)}), bf16[4,192,1024]{2,1,0:T(8,128)(2,1)S(1)}, u32[]{:S(2)}, u32[]{:S(2)}) %all-to-all-start.1) | async-done | bytes 1572896 | tf_op jit(solution)/shard_map/all_to_all | solution.py:234
  141.8 4.2 %all-to-all-start.2 = ((bf16[4,128,1024]{2,1,0:T(8,128)(2,1)}), bf16[4,128,1024]{2,1,0:T(8,128)(2,1)}, u32[]{:S(2)}, u32[]{:S(2)}) async-start(bf16[4,128,1024]{2,1,0:T(8,128)(2,1)} %bitcast.113), calls=%async_computation.2 | async-start | bytes 2097152 | tf_op jit(solution)/shard_map/all_to_all | solution.py:234
  146.1 3.5 %dynamic_update_slice.48 = bf16[4096,896]{1,0:T(8,128)(2,1)} pad(bf16[1024,896]{1,0:T(8,128)(2,1)S(1)} %bitcast.101, bf16[]{:T(256)} %constant.128.clone.1), padding=0_3072x0_0 | pad | bytes 9175042 | tf_op jit(solution)/shard_map/dynamic_update_slice | solution.py:261
  149.5 2.9 constant_dynamic-update-slice_fusion.5
  152.4 2.9 constant_dynamic-update-slice_fusion.4
  156.3 2.9 constant_dynamic-update-slice_fusion.3.right
  160.9 11.2 %all-to-all-done.2 = bf16[4,128,1024]{2,1,0:T(8,128)(2,1)} async-done(((bf16[4,128,1024]{2,1,0:T(8,128)(2,1)}), bf16[4,128,1024]{2,1,0:T(8,128)(2,1)}, u32[]{:S(2)}, u32[]{:S(2)}) %all-to-all-start.2) | async-done | bytes 1048608 | tf_op jit(solution)/shard_map/all_to_all | solution.py:234
  173.6 12.3 %collective-permute-done.7 = bf16[128,1024]{1,0:T(8,128)(2,1)S(1)} collective-permute-done((bf16[128,1024]{1,0:T(8,128)(2,1)S(1)}, bf16[128,1024]{1,0:T(8,128)(2,1)S(1)}, u32[]{:S(2)}, u32[]{:S(2)}) %collective-permute-start.7) | collective-permute-done | bytes 262176 | tf_op jit(solution)/shard_map/ppermute | solution.py:201
  186.2 3.2 collective-permute-start.8
  189.4 16.2 %collective-permute-done.9 = bf16[2,128,1024]{2,1,0:T(8,128)(2,1)S(1)} collective-permute-done((bf16[2,128,1024]{2,1,0:T(8,128)(2,1)S(1)}, bf16[2,128,1024]{2,1,0:T(8,128)(2,1)S(1)}, u32[]{:S(2)}, u32[]{:S(2)}) %collective-permute-start.9) | collective-permute-done | bytes 524320 | tf_op jit(solution)/shard_map/ppermute | solution.py:201
  209.4 2.2 collective-permute-start.11
  211.6 2.3 shard_map.17
  216.4 9.3 %collective-permute-done.11 = bf16[128,1024]{1,0:T(8,128)(2,1)S(1)} collective-permute-done((bf16[128,1024]{1,0:T(8,128)(2,1)S(1)}, bf16[128,1024]{1,0:T(8,128)(2,1)S(1)}, u32[]{:S(2)}, u32[]{:S(2)}) %collective-permute-start.11) | collective-permute-done | bytes 262176 | tf_op jit(solution)/shard_map/ppermute | solution.py:201
  237.5 5.6 %collective-permute-done.17 = bf16[512,512]{0,1:T(8,128)(2,1)} collective-permute-done((bf16[512,512]{0,1:T(8,128)(2,1)S(1)}, bf16[512,512]{0,1:T(8,128)(2,1)}, u32[]{:S(2)}, u32[]{:S(2)}) %collective-permute-start.17) | collective-permute-done | bytes 524320 | tf_op jit(solution)/shard_map/ppermute | solution.py:201
  248.4 13.2 %collective-permute-done.14 = bf16[512,512]{1,0:T(8,128)(2,1)} collective-permute-done((bf16[512,512]{1,0:T(8,128)(2,1)}, bf16[512,512]{1,0:T(8,128)(2,1)}, u32[]{:S(2)}, u32[]{:S(2)}) %collective-permute-start.14) | collective-permute-done | bytes 524320 | tf_op jit(solution)/shard_map/ppermute | solution.py:179
  266.6 2.3 constant_dynamic-update-slice_fusion.1.left
  268.9 8.2 %shard_map.18.refs_0_.refs_7_ = bf16[512,896]{1,0:T(8,128)(2,1)S(1)} custom-call(bf16[1024,4096]{1,0:T(8,128)(2,1)} %constant_dynamic-update-slice_fusion.1.left, bf16[4096,896]{1,0:T(8,128)(2,1)} %constant_dynamic-update-slice_fusion.3.right), custom_call_target="tpu_custom_call" | custom-call | tf_op jit(solution)/shard_map/pallas_call | solution.py:55
  277.1 2.2 collective-permute-start.23
  289.5 2.1 collective-permute-done.18
  291.7 2.4 constant_dynamic-update-slice_fusion.left
  294.0 8.1 %shard_map.19.refs_4_.refs_8_ = bf16[512,896]{1,0:T(8,128)(2,1)S(1)} custom-call(bf16[1024,4096]{1,0:T(8,128)(2,1)} %constant_dynamic-update-slice_fusion.left, bf16[4096,896]{1,0:T(8,128)(2,1)} %constant_dynamic-update-slice_fusion.3.right), custom_call_target="tpu_custom_call" | custom-call | tf_op jit(solution)/shard_map/pallas_call | solution.py:55
  306.1 13.0 %shard_map.20.refs_2_ = f32[1024,896]{1,0:T(8,128)} custom-call(s32[7]{0:T(128)S(1)} %stack.125.columns, bf16[1024,4096]{1,0:T(8,128)(2,1)} %constant_dynamic-update-slice_fusion.left, bf16[512,896]{1,0:T(8,128)(2,1)S(1)} %shard_map.18.refs_0_.refs_7_, bf16[512,896]{1,0:T(8,128)(2,1)} %collective-permute-done.22.refs_1_, ...), custom_call_target="tpu_custom_call" | custom-call | tf_op jit(solution)/shard_map/pallas_call | solution.py:127
  319.2 6.0 %collective-permute-done.21.refs_0_ = bf16[512,896]{1,0:T(8,128)(2,1)} collective-permute-done((bf16[512,896]{1,0:T(8,128)(2,1)S(1)}, bf16[512,896]{1,0:T(8,128)(2,1)}, u32[]{:S(2)}, u32[]{:S(2)}) %collective-permute-start.21) | collective-permute-done | bytes 917536 | tf_op jit(solution)/shard_map/ppermute | solution.py:169
  325.7 2.1 collective-permute-done.26.refs_1_
  328.8 7.4 %shard_map.21 = bf16[1024,896]{1,0:T(8,128)(2,1)} custom-call(s32[3]{0:T(128)} %pad_add_fusion.columns, bf16[1024,4096]{1,0:T(8,128)(2,1)} %constant_dynamic-update-slice_fusion.left, bf16[512,896]{1,0:T(8,128)(2,1)} %collective-permute-done.21.refs_0_, bf16[512,896]{1,0:T(8,128)(2,1)} %copy-done.7, f32[1024,896]{1,0:T(8,128)} %shard_map.20.refs_2_), custom_call_target="tpu_custom_call" | custom-call | tf_op jit(solution)/shard_map/pallas_call | solution.py:127
  (113 shorter events, 65.2 us)
Async XLA Ops:
  52.4 93.7 %copy-start = (bf16[128,8,896]{2,0,1:T(8,128)(2,1)}, bf16[128,8,896]{2,0,1:T(8,128)(2,1)S(1)}, u32[]{:S(2)}) copy-start(bf16[128,8,896]{2,0,1:T(8,128)(2,1)S(1)} %all_to_all.29) | copy-start | bytes 5505028
  52.4 4.7 %collective-permute-start.2 = (bf16[1024,896]{1,0:T(8,128)(2,1)S(1)}, bf16[1024,896]{1,0:T(8,128)(2,1)}, u32[]{:S(2)}, u32[]{:S(2)}) collective-permute-start(bf16[1024,896]{1,0:T(8,128)(2,1)S(1)} %bitcast.95), channel_id=1, source_target_pairs={{0,8},{8,0},{16,24},{24,16},{1,9},{9,1},{17,25},{25,17},{2,10},{10... | collective-permute-start | bytes 5505032 | tf_op jit(solution)/shard_map/ppermute | solution.py:172
  52.4 42.5 %collective-permute-start = (bf16[1024,896]{1,0:T(8,128)(2,1)S(1)}, bf16[1024,896]{1,0:T(8,128)(2,1)}, u32[]{:S(2)}, u32[]{:S(2)}) collective-permute-start(bf16[1024,896]{1,0:T(8,128)(2,1)S(1)} %bitcast.96), channel_id=1, source_target_pairs={{0,16},{8,24},{16,0},{24,8},{1,17},{9,25},{17,1},{25,9},{2,18},{10... | collective-permute-start | bytes 5505032 | tf_op jit(solution)/shard_map/ppermute | solution.py:169
  56.4 26.1 %collective-permute-start.1 = (bf16[512,1024]{1,0:T(8,128)(2,1)S(1)}, bf16[512,1024]{1,0:T(8,128)(2,1)S(1)}, u32[]{:S(2)}, u32[]{:S(2)}) collective-permute-start(bf16[512,1024]{1,0:T(8,128)(2,1)S(1)} %constant_dynamic-slice_fusion.5), channel_id=1, source_target_pairs={{0,4},{4,0},{1,5},{5,1},{2,6},{6,2},{3,7},{7,3},{8,12},{12,8},{9,1... | collective-permute-start | bytes 3145736 | tf_op jit(solution)/shard_map/ppermute | solution.py:189
  61.0 34.0 %collective-permute-start.3 = (bf16[256,1024]{0,1:T(8,128)(2,1)S(1)}, bf16[256,1024]{0,1:T(8,128)(2,1)S(1)}, u32[]{:S(2)}, u32[]{:S(2)}) collective-permute-start(bf16[256,1024]{0,1:T(8,128)(2,1)S(1)} %fusion.6), channel_id=1, source_target_pairs={{0,4},{4,0},{1,5},{5,1},{2,6},{6,2},{3,7},{7,3},{8,12},{12,8},{9,1... | collective-permute-start | bytes 1572872 | tf_op jit(solution)/shard_map/ppermute | solution.py:189
  82.5 12.4 %copy-start.6 = (bf16[512,1024]{1,0:T(8,128)(2,1)}, bf16[512,1024]{1,0:T(8,128)(2,1)S(1)}, u32[]{:S(2)}) copy-start(bf16[512,1024]{1,0:T(8,128)(2,1)S(1)} %collective-permute-done.1) | copy-start | bytes 3145732
  95.7 8.2 %collective-permute-start.4 = (bf16[1024,896]{1,0:T(8,128)(2,1)}, bf16[1024,896]{1,0:T(8,128)(2,1)}, u32[]{:S(2)}, u32[]{:S(2)}) collective-permute-start(bf16[1024,896]{1,0:T(8,128)(2,1)} %collective-permute-done), channel_id=1, source_target_pairs={{0,8},{8,0},{16,24},{24,16},{1,9},{9,1},{17,25},{25,17},{2,10},{10... | collective-permute-start | bytes 5505032 | tf_op jit(solution)/shard_map/ppermute | solution.py:172
  100.4 41.4 %all-to-all-start.1 = ((bf16[4,192,1024]{2,1,0:T(8,128)(2,1)}), bf16[4,192,1024]{2,1,0:T(8,128)(2,1)S(1)}, u32[]{:S(2)}, u32[]{:S(2)}) async-start(bf16[4,192,1024]{2,1,0:T(8,128)(2,1)} %pad_maximum_fusion), calls=%async_computation.1 | async-start | bytes 3145728 | tf_op jit(solution)/shard_map/all_to_all | solution.py:234
  107.9 25.6 %collective-permute-start.5 = (bf16[512,1024]{1,0:T(8,128)(2,1)S(1)}, bf16[512,1024]{1,0:T(8,128)(2,1)S(1)}, u32[]{:S(2)}, u32[]{:S(2)}) collective-permute-start(bf16[512,1024]{1,0:T(8,128)(2,1)S(1)} %constant_dynamic-slice_fusion.4), channel_id=1, source_target_pairs={{0,4},{4,0},{1,5},{5,1},{2,6},{6,2},{3,7},{7,3},{8,12},{12,8},{9,1... | collective-permute-start | bytes 3145736 | tf_op jit(solution)/shard_map/ppermute | solution.py:189
  141.8 30.2 %all-to-all-start.2 = ((bf16[4,128,1024]{2,1,0:T(8,128)(2,1)}), bf16[4,128,1024]{2,1,0:T(8,128)(2,1)}, u32[]{:S(2)}, u32[]{:S(2)}) async-start(bf16[4,128,1024]{2,1,0:T(8,128)(2,1)} %bitcast.113), calls=%async_computation.2 | async-start | bytes 2097152 | tf_op jit(solution)/shard_map/all_to_all | solution.py:234
  155.7 5.2 %collective-permute-start.6 = (bf16[64,1024]{1,0:T(8,128)(2,1)S(1)}, bf16[64,1024]{1,0:T(8,128)(2,1)S(1)}, u32[]{:S(2)}, u32[]{:S(2)}) collective-permute-start(bf16[64,1024]{1,0:T(8,128)(2,1)S(1)} %slice.39), channel_id=1, source_target_pairs={{0,4},{4,0},{1,5},{5,1},{2,6},{6,2},{3,7},{7,3},{8,12},{12,8},{9,1... | collective-permute-start | bytes 393224 | tf_op jit(solution)/shard_map/ppermute | solution.py:201
  173.4 12.4 %collective-permute-start.7 = (bf16[128,1024]{1,0:T(8,128)(2,1)S(1)}, bf16[128,1024]{1,0:T(8,128)(2,1)S(1)}, u32[]{:S(2)}, u32[]{:S(2)}) collective-permute-start(bf16[128,1024]{1,0:T(8,128)(2,1)S(1)} %reduce_sum.25), channel_id=1, source_target_pairs={{0,2},{1,3},{2,0},{3,1},{4,6},{5,7},{6,4},{7,5},{8,10},{9,11},{10,... | collective-permute-start | bytes 786440 | tf_op jit(solution)/shard_map/ppermute | solution.py:201
  186.0 19.5 %collective-permute-start.9 = (bf16[2,128,1024]{2,1,0:T(8,128)(2,1)S(1)}, bf16[2,128,1024]{2,1,0:T(8,128)(2,1)S(1)}, u32[]{:S(2)}, u32[]{:S(2)}) collective-permute-start(bf16[2,128,1024]{2,1,0:T(8,128)(2,1)S(1)} %pad_maximum_fusion.4), channel_id=1, source_target_pairs={{0,1},{1,0},{2,3},{3,2},{4,5},{5,4},{6,7},{7,6},{8,9},{9,8},{10,11... | collective-permute-start | bytes 1572872 | tf_op jit(solution)/shard_map/ppermute | solution.py:201
  186.2 19.6 %collective-permute-start.8 = (bf16[2,64,1024]{2,1,0:T(8,128)(2,1)S(1)}, bf16[2,64,1024]{2,1,0:T(8,128)(2,1)S(1)}, u32[]{:S(2)}, u32[]{:S(2)}) collective-permute-start(bf16[2,64,1024]{2,1,0:T(8,128)(2,1)S(1)} %pad_maximum_fusion.7), channel_id=1, source_target_pairs={{0,2},{1,3},{2,0},{3,1},{4,6},{5,7},{6,4},{7,5},{8,10},{9,11},{10,... | collective-permute-start | bytes 786440 | tf_op jit(solution)/shard_map/ppermute | solution.py:201
  206.8 18.9 %collective-permute-start.12 = (bf16[512,512]{1,0:T(8,128)(2,1)}, bf16[512,512]{1,0:T(8,128)(2,1)}, u32[]{:S(2)}, u32[]{:S(2)}) collective-permute-start(bf16[512,512]{1,0:T(8,128)(2,1)} %get-tuple-element.94), channel_id=1, source_target_pairs={{0,4},{4,0},{1,5},{5,1},{2,6},{6,2},{3,7},{7,3},{8,12},{12,8},{9,1... | collective-permute-start | bytes 1572872 | tf_op jit(solution)/shard_map/ppermute | solution.py:201
  208.3 18.5 %collective-permute-start.10 = (bf16[2,2,64,1024]{3,2,0,1:T(8,128)(2,1)}, bf16[2,2,64,1024]{3,2,0,1:T(8,128)(2,1)S(1)}, u32[]{:S(2)}, u32[]{:S(2)}) collective-permute-start(bf16[2,2,64,1024]{3,2,0,1:T(8,128)(2,1)} %pad_maximum_fusion.5), channel_id=1, source_target_pairs={{0,1},{1,0},{2,3},{3,2},{4,5},{5,4},{6,7},{7,6},{8,9},{9,8},{10,11... | collective-permute-start | bytes 1572872 | tf_op jit(solution)/shard_map/ppermute | solution.py:201
  209.4 16.4 %collective-permute-start.11 = (bf16[128,1024]{1,0:T(8,128)(2,1)S(1)}, bf16[128,1024]{1,0:T(8,128)(2,1)S(1)}, u32[]{:S(2)}, u32[]{:S(2)}) collective-permute-start(bf16[128,1024]{1,0:T(8,128)(2,1)S(1)} %slice.38), channel_id=1, source_target_pairs={{0,2},{1,3},{2,0},{3,1},{4,6},{5,7},{6,4},{7,5},{8,10},{9,11},{10,... | collective-permute-start | bytes 786440 | tf_op jit(solution)/shard_map/ppermute | solution.py:201
  214.9 15.2 %collective-permute-start.16 = (bf16[512,512]{0,1:T(8,128)(2,1)}, bf16[512,512]{0,1:T(8,128)(2,1)}, u32[]{:S(2)}, u32[]{:S(2)}) collective-permute-start(bf16[512,512]{0,1:T(8,128)(2,1)} %copy.26), channel_id=1, source_target_pairs={{0,16},{16,8},{8,24},{24,0},{1,17},{17,9},{9,25},{25,1},{2,18},{18... | collective-permute-start | bytes 1572872 | tf_op jit(solution)/shard_map/ppermute | solution.py:179
  227.1 20.2 %copy-start.3 = (bf16[2,2,2,64,1024]{4,3,2,1,0:T(8,128)(2,1)}, bf16[2,2,2,64,1024]{4,3,2,1,0:T(8,128)(2,1)S(1)}, u32[]{:S(2)}) copy-start(bf16[2,2,2,64,1024]{4,3,2,1,0:T(8,128)(2,1)S(1)} %copy.17) | copy-start | bytes 3145732
  227.2 17.4 %collective-permute-start.15 = (bf16[512,1024]{1,0:T(8,128)(2,1)S(1)}, bf16[512,1024]{1,0:T(8,128)(2,1)}, u32[]{:S(2)}, u32[]{:S(2)}) collective-permute-start(bf16[512,1024]{1,0:T(8,128)(2,1)S(1)} %bitcast.106), channel_id=1, source_target_pairs={{0,8},{8,0},{16,24},{24,16},{1,9},{9,1},{17,25},{25,17},{2,10},{10... | collective-permute-start | bytes 3145736 | tf_op jit(solution)/shard_map/ppermute | solution.py:172
  228.7 14.4 %collective-permute-start.17 = (bf16[512,512]{0,1:T(8,128)(2,1)S(1)}, bf16[512,512]{0,1:T(8,128)(2,1)}, u32[]{:S(2)}, u32[]{:S(2)}) collective-permute-start(bf16[512,512]{0,1:T(8,128)(2,1)S(1)} %get-tuple-element.66), channel_id=1, source_target_pairs={{0,4},{4,0},{1,5},{5,1},{2,6},{6,2},{3,7},{7,3},{8,12},{12,8},{9,1... | collective-permute-start | bytes 1572872 | tf_op jit(solution)/shard_map/ppermute | solution.py:201
  232.0 31.8 %collective-permute-start.13 = (bf16[2,128,1024]{2,1,0:T(8,128)(2,1)}, bf16[2,128,1024]{2,1,0:T(8,128)(2,1)}, u32[]{:S(2)}, u32[]{:S(2)}) collective-permute-start(bf16[2,128,1024]{2,1,0:T(8,128)(2,1)} %pad_maximum_fusion.6), channel_id=1, source_target_pairs={{0,1},{1,0},{2,3},{3,2},{4,5},{5,4},{6,7},{7,6},{8,9},{9,8},{10,11... | collective-permute-start | bytes 1572872 | tf_op jit(solution)/shard_map/ppermute | solution.py:201
  235.9 43.4 %collective-permute-start.20 = (bf16[512,512]{0,1:T(8,128)(2,1)}, bf16[512,512]{0,1:T(8,128)(2,1)}, u32[]{:S(2)}, u32[]{:S(2)}) collective-permute-start(bf16[512,512]{0,1:T(8,128)(2,1)} %get-tuple-element.71), channel_id=1, source_target_pairs={{0,16},{16,8},{8,24},{24,0},{1,17},{17,9},{9,25},{25,1},{2,18},{18... | collective-permute-start | bytes 1572872 | tf_op jit(solution)/shard_map/ppermute | solution.py:179
  237.4 24.2 %collective-permute-start.14 = (bf16[512,512]{1,0:T(8,128)(2,1)}, bf16[512,512]{1,0:T(8,128)(2,1)}, u32[]{:S(2)}, u32[]{:S(2)}) collective-permute-start(bf16[512,512]{1,0:T(8,128)(2,1)} %collective-permute-done.12), channel_id=1, source_target_pairs={{0,16},{16,8},{8,24},{24,0},{1,17},{17,9},{9,25},{25,1},{2,18},{18... | collective-permute-start | bytes 1572872 | tf_op jit(solution)/shard_map/ppermute | solution.py:179
  243.1 44.5 %collective-permute-start.19 = (bf16[512,512]{0,1:T(8,128)(2,1)}, bf16[512,512]{0,1:T(8,128)(2,1)}, u32[]{:S(2)}, u32[]{:S(2)}) collective-permute-start(bf16[512,512]{0,1:T(8,128)(2,1)} %collective-permute-done.17), channel_id=1, source_target_pairs={{0,16},{16,8},{8,24},{24,0},{1,17},{17,9},{9,25},{25,1},{2,18},{18... | collective-permute-start | bytes 1572872 | tf_op jit(solution)/shard_map/ppermute | solution.py:179
  266.0 25.7 %collective-permute-start.18 = (bf16[512,1024]{1,0:T(8,128)(2,1)}, bf16[512,1024]{1,0:T(8,128)(2,1)}, u32[]{:S(2)}, u32[]{:S(2)}) collective-permute-start(bf16[512,1024]{1,0:T(8,128)(2,1)} %bitcast.32), channel_id=1, source_target_pairs={{0,4},{4,0},{1,5},{5,1},{2,6},{6,2},{3,7},{7,3},{8,12},{12,8},{9,1... | collective-permute-start | bytes 3145736 | tf_op jit(solution)/shard_map/ppermute | solution.py:201
  277.1 25.1 %collective-permute-start.23 = (bf16[512,896]{1,0:T(8,128)(2,1)S(1)}, bf16[512,896]{1,0:T(8,128)(2,1)S(1)}, u32[]{:S(2)}, u32[]{:S(2)}) collective-permute-start(bf16[512,896]{1,0:T(8,128)(2,1)S(1)} %shard_map.18.refs_0_.refs_7_), channel_id=1, source_target_pairs={{0,16},{8,24},{16,0},{24,8},{1,17},{9,25},{17,1},{25,9},{2,18},{10... | collective-permute-start | bytes 2752520 | tf_op jit(solution)/shard_map/ppermute | solution.py:169
  279.3 23.5 %collective-permute-start.22 = (bf16[512,896]{1,0:T(8,128)(2,1)S(1)}, bf16[512,896]{1,0:T(8,128)(2,1)}, u32[]{:S(2)}, u32[]{:S(2)}) collective-permute-start(bf16[512,896]{1,0:T(8,128)(2,1)S(1)} %shard_map.18.refs_0_.refs_7_), channel_id=1, source_target_pairs={{0,8},{8,0},{16,24},{24,16},{1,9},{9,1},{17,25},{25,17},{2,10},{10... | collective-permute-start | bytes 2752520 | tf_op jit(solution)/shard_map/ppermute | solution.py:172
  302.1 2.7 collective-permute-start.24
  302.2 3.9 %collective-permute-start.25 = (bf16[512,896]{1,0:T(8,128)(2,1)S(1)}, bf16[512,896]{1,0:T(8,128)(2,1)}, u32[]{:S(2)}, u32[]{:S(2)}) collective-permute-start(bf16[512,896]{1,0:T(8,128)(2,1)S(1)} %shard_map.19.refs_4_.refs_8_), channel_id=1, source_target_pairs={{0,8},{8,0},{16,24},{24,16},{1,9},{9,1},{17,25},{25,17},{2,10},{10... | collective-permute-start | bytes 2752520 | tf_op jit(solution)/shard_map/ppermute | solution.py:172
  302.7 22.4 %collective-permute-start.21 = (bf16[512,896]{1,0:T(8,128)(2,1)S(1)}, bf16[512,896]{1,0:T(8,128)(2,1)}, u32[]{:S(2)}, u32[]{:S(2)}) collective-permute-start(bf16[512,896]{1,0:T(8,128)(2,1)S(1)} %shard_map.19.refs_4_.refs_8_), channel_id=1, source_target_pairs={{0,16},{8,24},{16,0},{24,8},{1,17},{9,25},{17,1},{25,9},{2,18},{10... | collective-permute-start | bytes 2752520 | tf_op jit(solution)/shard_map/ppermute | solution.py:169
  325.2 2.7 collective-permute-start.26
  (7 other events, 38.0 us)
